TPU v7x, 32 devices: a whole 2x2x4 slice. The times are simulated.
32 devices in a mesh: occ: 4 (over y, x), vir: 8 (over z, core).
Axes of the slice: x: 2, y: 2, z: 4, core: 2. Of those that a mesh axis runs over, the one named last changes fastest.
Arguments:
- amplitudes: float32 [4, 1024, 1024], P(None, 'occ', 'vir'), may hold values from -6 to 6
- integrals: float32 [4, 7168, 1024], P(None, 'vir', 'occ'), may hold values from -0.1875 to 0.1875
Outputs:
- ladder: float32 [4, 1024, 7168], P(None, 'occ', 'vir')
All inputs are finite; a program needn't handle non-finite values.
Results may differ from a plain program's by a relative error of at most 0.000073.
Values sent between devices are 32-bit elements; how exact they have to be, the bound alone decides.
No kernel may reach another device: no remote copies, remote signals or barrier semaphores. Data moves between devices by JAX's collectives and lax.ppermute only.
A program may use at most 64 MiB of HBM per device.

v0:
```python
import jax
import jax.numpy as jnp
from jax import lax
from jax.sharding import PartitionSpec as P


def contract_block(left, piece):
    return lax.dot_general(
        left,
        piece,
        (((2,), (2,)), ((0,), (0,))),
        precision=lax.Precision.HIGHEST,
        preferred_element_type=jnp.float32,
    )


def body(amplitudes, integrals):
    gathered = lax.all_gather(amplitudes, "vir", axis=2, tiled=True)
    panel_sum = contract_block(gathered, lax.all_gather(integrals, "occ", axis=2, tiled=True))
    return 0.5 * panel_sum


def solution(mesh):
    in_specs = (P(None, "occ", "vir"), P(None, "vir", "occ"))
    out_specs = P(None, "occ", "vir")
    return jax.shard_map(body, mesh=mesh, in_specs=in_specs, out_specs=out_specs, check_vma=False)
```

profile of v0, /device:TPU:0, one launch (start us, length us, event | category | flops | bytes accessed | tf_op | source)
XLA Modules:
  0.0 225.4 jit_solution(5486413498970945923)
XLA Ops:
  6.5 0.0 all-gather.3.cloned.1.call-start
  6.5 0.7 all-gather.3.cloned.1.call-update
  7.3 0.0 all-gather.5.cloned.1.call-start
  7.3 0.7 all-gather.5.cloned.1.call-update
  8.0 51.5 %all-gather.3.cloned.1.call-done = f32[4,256,1024]{2,1,0:T(8,128)} async-done(((f32[4,256,128]{2,1,0:T(8,128)}), f32[4,256,1024]{2,1,0:T(8,128)}) %all-gather.3.cloned.1.call-update) | async-done | bytes 4194320 | tf_op jit(solution)/shard_map/all_gather | solution.py:18
  59.5 139.9 %all-gather.5.cloned.1.call-done = f32[4,896,1024]{2,1,0:T(8,128)} async-done(((f32[4,896,256]{2,1,0:T(8,128)}), f32[4,896,1024]{2,1,0:T(8,128)}) %all-gather.5.cloned.1.call-update) | async-done | bytes 14680080 | tf_op jit(solution)/shard_map/all_gather | solution.py:19
  199.4 19.1 %convolution_multiply_fusion = f32[4,256,896]{2,1,0:T(8,128)} fusion(f32[4,256,1024]{2,1,0:T(8,128)} %all-gather.3.cloned.1.call-done, f32[4,896,1024]{2,1,0:T(8,128)} %all-gather.5.cloned.1.call-done), kind=kOutput, calls=%fused_computation | convolution fusion | flops 11275206656 | bytes 22544384 | tf_op jit(solution)/shard_map/dot_general | solution.py:8
Async XLA Ops:
  6.5 52.9 %all-gather.3.cloned.1.call-start = ((), (), s32[]{:S(2)}) async-start(), calls=%async_computation | async-start | bytes 4718592 | tf_op jit(solution)/shard_map/all_gather | solution.py:18
  7.3 192.1 %all-gather.5.cloned.1.call-start = ((), (), s32[]{:S(2)}) async-start(), calls=%async_computation.1 | async-start | bytes 18350080 | tf_op jit(solution)/shard_map/all_gather | solution.py:19
Sparse Core Ops, SparseCore 0:
  8.9 50.4 all-gather.2
  61.3 138.0 all-gather.4
where the time goes:
time: 225 us
  waiting for transfers between devices  193 us (86%)
  matrix products  19.1 us (8%)
  between operations  13.4 us (6%)
    all_gather x1, waiting for transfers between devices, body(): lax.all_gather(integrals, 'occ', axis=2, tiled=True)  140 us
    all_gather x1, waiting for transfers between devices, body(): gathered = lax.all_gather(amplitudes, 'vir', axis=2, tiled=True)  51.5 us
    dot_general x1, matrix products, contract_block(): lax.dot_general(left, piece, (((2,), (2,)), ((0,), (0,))), precision=lax....  19.1 us
  transfers between devices with their start and end apart: 2, of which 2 were waited for; matrix products, arithmetic and copies ran while one was open for 0% of the time, Pallas kernels for 0%

commit v1 on v0

v1 whole, which is shorter than its diff:
```python
import functools

import jax
import jax.numpy as jnp
from jax import lax
from jax.experimental import pallas as pl
from jax.experimental.pallas import tpu as pltpu
from jax.sharding import PartitionSpec as P

MESH = {"occ": 4, "vir": 8}


def contract_block(left, piece):
    return lax.dot_general(
        left,
        piece,
        (((2,), (2,)), ((0,), (0,))),
        precision=lax.Precision.HIGHEST,
        preferred_element_type=jnp.float32,
    )


def gather_body(amplitudes, integrals):
    gathered = lax.all_gather(amplitudes, "vir", axis=2, tiled=True)
    panel_sum = contract_block(gathered, lax.all_gather(integrals, "occ", axis=2, tiled=True))
    return 0.5 * panel_sum


BOTH = ("occ", "vir")
OVER = ([(o, o ^ 1) for o in range(4)], [(o, o ^ 2) for o in range(4)])
OVER_CORE = [(v, v ^ 1) for v in range(8)]


def pairs(move):
    return [(o * 8 + v, move(o, v >> 1, v & 1)) for o in range(4) for v in range(8)]


SAME_CORE = pairs(lambda o, z, c: (o ^ (1 if c else 2)) * 8 + 2 * z + c)
CROSS_CORE = pairs(lambda o, z, c: (o ^ (2 if c else 1)) * 8 + 2 * z + 1 - c)
FIRST_Z = pairs(lambda o, z, c: o * 8 + 2 * (z ^ (1 if c else 2)) + c)
SECOND_Z = pairs(lambda o, z, c: o * 8 + 2 * (z ^ (2 if c else 1)) + c)


def split(a):
    high = a.astype(jnp.bfloat16)
    low = (a - high.astype(jnp.float32)).astype(jnp.bfloat16)
    return high, low


def dot3(left, right):
    (lh, ll), (rh, rl) = left, right

    def dot(a, b):
        return lax.dot_general(a, b, (((1,), (1,)), ((), ())), preferred_element_type=jnp.float32)

    return dot(lh, rh) + (dot(lh, rl) + dot(ll, rh))


def partial_kernel(kind, i, place, same0, same1, other0, other1, own_ref, got_ref, out_ref):
    y, x, z, core = place[0], place[1], place[2], place[3]
    first_half, own_half = (lax.rem(z, 2), x) if kind == 0 else (z // 2, y)
    in_order = first_half == own_half

    def rows(a, b):
        return jnp.concatenate([jnp.where(core == kind, a[c, i], b[c, i]) for c in range(2)], axis=1)

    first, second = rows(same0, other0), rows(same1, other1)
    t = split(jnp.concatenate([jnp.where(in_order, first, second), jnp.where(in_order, second, first)], axis=1))
    width = own_ref.shape[0]
    step = 256
    for start in range(0, width, step):
        size = min(step, width - start)
        v = split(jnp.concatenate([own_ref[start : start + size, :], got_ref[start : start + size, :]], axis=1))
        out_ref[:, start : start + size] = dot3(t, v)


def partial_sum(kind, i, place, blocks, own, got):
    n_ij, n_ab, n_cd = blocks[0].shape[2], own.shape[0], 2 * own.shape[1]
    vmem = pl.BlockSpec(memory_space=pltpu.VMEM)
    return pl.pallas_call(
        functools.partial(partial_kernel, kind, i),
        out_shape=jax.ShapeDtypeStruct((n_ij, n_ab), jnp.float32),
        in_specs=[pl.BlockSpec(memory_space=pltpu.SMEM)] + [vmem] * 6,
        out_specs=vmem,
        compiler_params=pltpu.CompilerParams(vmem_limit_bytes=32 * 1024 * 1024),
        cost_estimate=pl.CostEstimate(
            flops=6 * n_ij * n_ab * n_cd, bytes_accessed=4 * (2 * n_ij * n_cd + n_ab * n_cd + n_ij * n_ab), transcendentals=0
        ),
    )(place, *blocks, own, got)


def spread(first, second, core, holder):
    first, second = jnp.where(core == 0, first, second), jnp.where(core == 0, second, first)
    held = jnp.stack([first, second])
    near = jnp.where(holder, held, lax.ppermute(held, BOTH, FIRST_Z))
    far = lax.ppermute(near, BOTH, SECOND_Z)
    return near, far, lax.ppermute(near, "vir", OVER_CORE), lax.ppermute(far, "vir", OVER_CORE)


def hybrid_body(amplitudes, integrals):
    o, v = lax.axis_index("occ"), lax.axis_index("vir")
    y, x, z, core = o // 2, o % 2, v // 2, v % 2
    place = jnp.stack([y, x, z, core]).astype(jnp.int32)
    holder = jnp.where(core == 0, z // 2 == y, z % 2 == x)
    mine = jnp.where(core == 0, amplitudes[:2], amplitudes[2:])
    give = jnp.where(core == 0, amplitudes[2:], amplitudes[:2])
    same, cross = lax.ppermute(mine, BOTH, SAME_CORE), lax.ppermute(give, BOTH, CROSS_CORE)
    got = {(k, i): lax.ppermute(integrals[2 * k + i], "occ", OVER[k]) for i in range(2) for k in range(2)}
    send_t = spread(same, cross, core, holder)
    keep_t = spread(mine, lax.ppermute(give, "vir", OVER_CORE), core, holder)
    came = {}
    for i in range(2):
        for k in range(2):
            part = partial_sum(k, i, place, send_t, integrals[2 * k + i], got[k, i])
            came[k, i] = lax.ppermute(part, "occ", OVER[1 - k])
    out = []
    for k in range(2):
        for i in range(2):
            out.append(0.5 * (partial_sum(k, i, place, keep_t, integrals[2 * k + i], got[k, i]) + came[k, i]))
    return jnp.stack(out)


def solution(mesh):
    in_specs = (P(None, "occ", "vir"), P(None, "vir", "occ"))
    out_specs = P(None, "occ", "vir")
    body = hybrid_body if dict(mesh.shape) == MESH else gather_body
    return jax.shard_map(body, mesh=mesh, in_specs=in_specs, out_specs=out_specs, check_vma=False)
```

time: 225 us -> 117 us (0.52)
  waiting for transfers between devices: 193 us -> 69.6 us
  starting transfers between devices: 0.04 us -> 24 us
  matrix products: 19.1 us -> 0 us
  Pallas kernels: 0 us -> 14.4 us
  between operations: 13.4 us -> 0.18 us
  other arithmetic: 0 us -> 6.98 us
    all_gather x2 -> x0, waiting for transfers between devices: 191 us -> none  [the longest x1 140 us: body(): lax.all_gather(integrals, 'occ', axis=2, tiled=True)]
    ppermute x0 -> x19, waiting for transfers between devices: none -> 69.6 us  [the longest x4 32.2 us: hybrid_body(): came[k, i] = lax.ppermute(part, 'occ', OVER[1 - k])]
    ppermute x0 -> x19, starting transfers between devices: none -> 24 us  [the longest x4 6.91 us: hybrid_body(): lax.ppermute(integrals[2 * k + i], 'occ', OVER[k])]
    dot_general x1 -> x0, matrix products: 19.1 us -> none  [contract_block(): lax.dot_general(left, piece, (((2,), (2,)), ((0,), (0,))), precision=lax....]
    pallas_call x0 -> x8, Pallas kernels: none -> 14.4 us  [partial_sum(): pl.pallas_call(functools.partial(partial_kernel, kind, i), out_shape=jax....]
    another operation x0 -> x11, other arithmetic: none -> 5.64 us  [the longest x5 3.11 us: spread(): held = jnp.stack([first, second])]
  transfers between devices with their start and end apart: 2 -> 19, of which waited for: 2 -> 8; matrix products, arithmetic and copies ran while one was open for 0% -> 3% of each run, Pallas kernels for 0% -> 12%
where the time goes in v1:
time: 117 us; the launch traced here: 116 us
  waiting for transfers between devices  69.6 us (59%)
  starting transfers between devices  24 us (21%)
  Pallas kernels  14.4 us (12%)
  other arithmetic  6.98 us (6%)
  local copies, waits for them, and re-layouts  1.21 us (1%)
    ppermute x4, waiting for transfers between devices, hybrid_body(): came[k, i] = lax.ppermute(part, 'occ', OVER[1 - k])  32.2 us
    ppermute x2, waiting for transfers between devices, spread(): near = jnp.where(holder, held, lax.ppermute(held, BOTH, FIRST_Z))  23.5 us
    pallas_call x8, Pallas kernels, partial_sum(): pl.pallas_call(functools.partial(partial_kernel, kind, i), out_shape=jax....  14.4 us
    ppermute x2, waiting for transfers between devices, spread(): far = lax.ppermute(near, BOTH, SECOND_Z)  8.39 us
    ppermute x4, starting transfers between devices, hybrid_body(): lax.ppermute(integrals[2 * k + i], 'occ', OVER[k])  6.91 us
    ppermute x4, starting transfers between devices, hybrid_body(): came[k, i] = lax.ppermute(part, 'occ', OVER[1 - k])  4.32 us
    ppermute x2, starting transfers between devices, spread(): far = lax.ppermute(near, BOTH, SECOND_Z)  3.41 us
    another operation x5, other arithmetic, spread(): held = jnp.stack([first, second])  3.11 us
  transfers between devices with their start and end apart: 19, of which 8 were waited for; matrix products, arithmetic and copies ran while one was open for 3% of the time, Pallas kernels for 12%

profile of v1, /device:TPU:0, one launch (start us, length us, event | category | flops | bytes accessed | tf_op | source)
XLA Modules:
  0.0 116.5 jit_solution(7529910136650136960)
XLA Ops:
  0.0 1.2 %slice_select_fusion = f32[2,256,128]{2,1,0:T(8,128)S(1)} fusion(f32[4,256,128]{2,1,0:T(8,128)} %param.2, pred[]{:T(512)S(6)} %eq.10), kind=kLoop, calls=%fused_computation.17 | loop fusion | flops 65536 | bytes 786433 | tf_op jit(solution)/shard_map/jit(_where)/select_n | solution.py:106
  1.7 2.6 %collective-permute-start.7 = (f32[2,256,128]{2,1,0:T(8,128)S(1)}, f32[2,256,128]{2,1,0:T(8,128)S(1)}, u32[]{:S(2)}, u32[]{:S(2)}) collective-permute-start(f32[2,256,128]{2,1,0:T(8,128)S(1)} %slice_select_fusion), channel_id=1, source_target_pairs={{0,9},{1,16},{2,11},{3,18},{4,13},{5,20},{6,15},{7,22},{8,1},{9,24... | collective-permute-start | bytes 786440 | tf_op jit(solution)/shard_map/ppermute | solution.py:107
  4.3 1.2 %select_bitcast_fusion.3 = (f32[1,2,256,128]{3,2,1,0:T(8,128)S(1)}, f32[2,256,128]{2,1,0:T(8,128)S(1)}) fusion(f32[2,256,128]{2,1,0:T(8,128)S(1)} %collective-permute-done, pred[]{:T(512)S(6)} %eq.10, f32[4,256,128]{2,1,0:T(8,128)} %param.2), kind=kLoop, calls=%fused_computation.14 | loop fusion | flops 131072 | bytes 1310721 | tf_op jit(solution)/shard_map/stack | solution.py:94
  5.5 1.6 %collective-permute-start.6 = (f32[2,256,128]{2,1,0:T(8,128)S(1)}, f32[2,256,128]{2,1,0:T(8,128)S(1)}, u32[]{:S(2)}, u32[]{:S(2)}) collective-permute-start(f32[2,256,128]{2,1,0:T(8,128)S(1)} %get-tuple-element.6), channel_id=1, source_target_pairs={{0,16},{1,9},{2,18},{3,11},{4,20},{5,13},{6,22},{7,15},{8,24},{9,1... | collective-permute-start | bytes 786440 | tf_op jit(solution)/shard_map/ppermute | solution.py:107
  7.1 2.0 %collective-permute-done.7 = f32[2,256,128]{2,1,0:T(8,128)S(1)} collective-permute-done((f32[2,256,128]{2,1,0:T(8,128)S(1)}, f32[2,256,128]{2,1,0:T(8,128)S(1)}, u32[]{:S(2)}, u32[]{:S(2)}) %collective-permute-start.7) | collective-permute-done | bytes 262176 | tf_op jit(solution)/shard_map/ppermute | solution.py:107
  9.1 2.9 %collective-permute-done.6 = f32[2,256,128]{2,1,0:T(8,128)S(1)} collective-permute-done((f32[2,256,128]{2,1,0:T(8,128)S(1)}, f32[2,256,128]{2,1,0:T(8,128)S(1)}, u32[]{:S(2)}, u32[]{:S(2)}) %collective-permute-start.6) | collective-permute-done | bytes 262176 | tf_op jit(solution)/shard_map/ppermute | solution.py:107
  12.9 2.6 %collective-permute-start.8 = (f32[2,2,256,128]{3,2,1,0:T(8,128)}, f32[2,2,256,128]{3,2,1,0:T(8,128)}, u32[]{:S(2)}, u32[]{:S(2)}) collective-permute-start(f32[2,2,256,128]{3,2,1,0:T(8,128)} %pad_maximum_fusion.2), channel_id=1, source_target_pairs={{0,4},{1,3},{2,6},{3,1},{4,0},{5,7},{6,2},{7,5},{8,12},{9,11},{10,... | collective-permute-start | bytes 1572872 | tf_op jit(solution)/shard_map/ppermute | solution.py:95
  15.5 1.2 %slice_bitcast_fusion.3 = (f32[896,256]{1,0:T(8,128)}, f32[896,256]{1,0:T(8,128)S(1)}, f32[896,256]{1,0:T(8,128)S(1)}, f32[896,256]{1,0:T(8,128)S(1)}) fusion(f32[4,896,256]{2,1,0:T(8,128)S(1)} %copy-done), kind=kLoop, calls=%fused_computation.8 | loop fusion | bytes 7340032 | tf_op jit(solution)/shard_map/squeeze | solution.py:119
  16.7 1.4 %collective-permute-start.5 = (f32[896,256]{1,0:T(8,128)}, f32[896,256]{1,0:T(8,128)}, u32[]{:S(2)}, u32[]{:S(2)}) collective-permute-start(f32[896,256]{1,0:T(8,128)} %get-tuple-element.7.own_ref), channel_id=1, source_target_pairs={{0,8},{8,0},{16,24},{24,16},{1,9},{9,1},{17,25},{25,17},{2,10},{10... | collective-permute-start | bytes 2752520 | tf_op jit(solution)/shard_map/ppermute | solution.py:108
  18.1 1.0 select_bitcast_fusion.2
  19.5 8.6 %collective-permute-done.8 = f32[2,2,256,128]{3,2,1,0:T(8,128)} collective-permute-done((f32[2,2,256,128]{3,2,1,0:T(8,128)}, f32[2,2,256,128]{3,2,1,0:T(8,128)}, u32[]{:S(2)}, u32[]{:S(2)}) %collective-permute-start.8) | collective-permute-done | bytes 524320 | tf_op jit(solution)/shard_map/ppermute | solution.py:95
  28.2 2.3 %collective-permute-start.9 = (f32[2,2,256,128]{3,2,1,0:T(8,128)S(1)}, f32[2,2,256,128]{3,2,1,0:T(8,128)S(1)}, u32[]{:S(2)}, u32[]{:S(2)}) collective-permute-start(f32[2,2,256,128]{3,2,1,0:T(8,128)S(1)} %broadcast_select_fusion.same0), channel_id=1, source_target_pairs={{0,2},{1,5},{2,0},{3,7},{4,6},{5,1},{6,4},{7,3},{8,10},{9,13},{10,... | collective-permute-start | bytes 1572872 | tf_op jit(solution)/shard_map/ppermute | solution.py:96
  30.5 1.4 %collective-permute-start.13 = (f32[896,256]{1,0:T(8,128)S(1)}, f32[896,256]{1,0:T(8,128)S(1)}, u32[]{:S(2)}, u32[]{:S(2)}) collective-permute-start(f32[896,256]{1,0:T(8,128)S(1)} %get-tuple-element.8.own_ref), channel_id=1, source_target_pairs={{0,8},{8,0},{16,24},{24,16},{1,9},{9,1},{17,25},{25,17},{2,10},{10... | collective-permute-start | bytes 2752520 | tf_op jit(solution)/shard_map/ppermute | solution.py:108
  32.0 2.6 %collective-permute-start.17 = (f32[896,256]{1,0:T(8,128)S(1)}, f32[896,256]{1,0:T(8,128)S(1)}, u32[]{:S(2)}, u32[]{:S(2)}) collective-permute-start(f32[896,256]{1,0:T(8,128)S(1)} %get-tuple-element.9.own_ref), channel_id=1, source_target_pairs={{0,16},{8,24},{16,0},{24,8},{1,17},{9,25},{17,1},{25,9},{2,18},{10... | collective-permute-start | bytes 2752520 | tf_op jit(solution)/shard_map/ppermute | solution.py:108
  34.5 14.9 %collective-permute-done.1 = f32[2,2,256,128]{3,2,1,0:T(8,128)S(1)} collective-permute-done((f32[2,2,256,128]{3,2,1,0:T(8,128)S(1)}, f32[2,2,256,128]{3,2,1,0:T(8,128)S(1)}, u32[]{:S(2)}, u32[]{:S(2)}) %collective-permute-start.1) | collective-permute-done | bytes 524320 | tf_op jit(solution)/shard_map/ppermute | solution.py:95
  49.4 1.7 %collective-permute-start.11 = (f32[2,2,256,128]{3,2,1,0:T(8,128)S(1)}, f32[2,2,256,128]{3,2,1,0:T(8,128)S(1)}, u32[]{:S(2)}, u32[]{:S(2)}) collective-permute-start(f32[2,2,256,128]{3,2,1,0:T(8,128)S(1)} %collective-permute-done.9.same1), channel_id=1, source_target_pairs={{0,1},{1,0},{2,3},{3,2},{4,5},{5,4},{6,7},{7,6},{8,9},{9,8},{10,11... | collective-permute-start | bytes 1572872 | tf_op jit(solution)/shard_map/ppermute | solution.py:97
  51.2 1.1 collective-permute-start.2
  52.3 1.5 %collective-permute-start.15 = (f32[896,256]{1,0:T(8,128)S(1)}, f32[896,256]{1,0:T(8,128)S(1)}, u32[]{:S(2)}, u32[]{:S(2)}) collective-permute-start(f32[896,256]{1,0:T(8,128)S(1)} %get-tuple-element.10.own_ref), channel_id=1, source_target_pairs={{0,16},{8,24},{16,0},{24,8},{1,17},{9,25},{17,1},{25,9},{2,18},{10... | collective-permute-start | bytes 2752520 | tf_op jit(solution)/shard_map/ppermute | solution.py:108
  53.9 2.5 %shard_map.29 = f32[256,896]{1,0:T(8,128)S(1)} custom-call(s32[4]{0:T(128)S(1)} %pad_add_fusion.place, f32[2,2,256,128]{3,2,1,0:T(8,128)S(1)} %broadcast_select_fusion.same0, f32[2,2,256,128]{3,2,1,0:T(8,128)S(1)} %collective-permute-done.9.same1, f32[2,2,256,128]{3,2,1,0:T(8,128)S(1)} %collective-permute-done.10.other0, ...), custom_call_target="tpu_custom_call" | custom-call | flops 704643072 | bytes 3801088 | tf_op jit(solution)/shard_map/pallas_call | solution.py:80
  57.6 8.4 %collective-permute-done.2.same1 = f32[2,2,256,128]{3,2,1,0:T(8,128)S(1)} collective-permute-done((f32[2,2,256,128]{3,2,1,0:T(8,128)S(1)}, f32[2,2,256,128]{3,2,1,0:T(8,128)S(1)}, u32[]{:S(2)}, u32[]{:S(2)}) %collective-permute-start.2) | collective-permute-done | bytes 524320 | tf_op jit(solution)/shard_map/ppermute | solution.py:96
  66.0 1.6 %shard_map.31 = f32[256,896]{1,0:T(8,128)S(1)} custom-call(s32[4]{0:T(128)S(1)} %pad_add_fusion.place, f32[2,2,256,128]{3,2,1,0:T(8,128)S(1)} %broadcast_select_fusion.same0, f32[2,2,256,128]{3,2,1,0:T(8,128)S(1)} %collective-permute-done.9.same1, f32[2,2,256,128]{3,2,1,0:T(8,128)S(1)} %collective-permute-done.10.other0, ...), custom_call_target="tpu_custom_call" | custom-call | flops 704643072 | bytes 3801088 | tf_op jit(solution)/shard_map/pallas_call | solution.py:80
  67.6 1.6 %collective-permute-start.14 = (f32[256,896]{1,0:T(8,128)S(1)}, f32[256,896]{1,0:T(8,128)S(1)}, u32[]{:S(2)}, u32[]{:S(2)}) collective-permute-start(f32[256,896]{1,0:T(8,128)S(1)} %shard_map.31), channel_id=1, source_target_pairs={{0,16},{8,24},{16,0},{24,8},{1,17},{9,25},{17,1},{25,9},{2,18},{10... | collective-permute-start | bytes 2752520 | tf_op jit(solution)/shard_map/ppermute | solution.py:115
  69.2 1.6 %shard_map.35 = f32[256,896]{1,0:T(8,128)S(1)} custom-call(s32[4]{0:T(128)S(1)} %pad_add_fusion.place, f32[2,2,256,128]{3,2,1,0:T(8,128)S(1)} %broadcast_select_fusion.same0, f32[2,2,256,128]{3,2,1,0:T(8,128)S(1)} %collective-permute-done.9.same1, f32[2,2,256,128]{3,2,1,0:T(8,128)S(1)} %collective-permute-done.10.other0, ...), custom_call_target="tpu_custom_call" | custom-call | flops 704643072 | bytes 3801088 | tf_op jit(solution)/shard_map/pallas_call | solution.py:80
  70.8 1.5 %collective-permute-start.18 = (f32[256,896]{1,0:T(8,128)S(1)}, f32[256,896]{1,0:T(8,128)S(1)}, u32[]{:S(2)}, u32[]{:S(2)}) collective-permute-start(f32[256,896]{1,0:T(8,128)S(1)} %shard_map.35), channel_id=1, source_target_pairs={{0,8},{8,0},{16,24},{24,16},{1,9},{9,1},{17,25},{25,17},{2,10},{10... | collective-permute-start | bytes 2752520 | tf_op jit(solution)/shard_map/ppermute | solution.py:115
  72.3 2.5 %shard_map.28 = f32[256,896]{1,0:T(8,128)S(1)} custom-call(s32[4]{0:T(128)S(1)} %pad_add_fusion.place, f32[2,2,256,128]{3,2,1,0:T(8,128)S(1)} %broadcast_select_fusion.1.same0, f32[2,2,256,128]{3,2,1,0:T(8,128)S(1)} %collective-permute-done.2.same1, f32[2,2,256,128]{3,2,1,0:T(8,128)S(1)} %collective-permute-done.3.other0, ...), custom_call_target="tpu_custom_call" | custom-call | flops 704643072 | bytes 3801088 | tf_op jit(solution)/shard_map/pallas_call | solution.py:80
  74.8 1.6 %shard_map.30 = f32[256,896]{1,0:T(8,128)S(1)} custom-call(s32[4]{0:T(128)S(1)} %pad_add_fusion.place, f32[2,2,256,128]{3,2,1,0:T(8,128)S(1)} %broadcast_select_fusion.1.same0, f32[2,2,256,128]{3,2,1,0:T(8,128)S(1)} %collective-permute-done.2.same1, f32[2,2,256,128]{3,2,1,0:T(8,128)S(1)} %collective-permute-done.3.other0, ...), custom_call_target="tpu_custom_call" | custom-call | flops 704643072 | bytes 3801088 | tf_op jit(solution)/shard_map/pallas_call | solution.py:80
  76.3 1.6 %shard_map.34 = f32[256,896]{1,0:T(8,128)S(1)} custom-call(s32[4]{0:T(128)S(1)} %pad_add_fusion.place, f32[2,2,256,128]{3,2,1,0:T(8,128)S(1)} %broadcast_select_fusion.1.same0, f32[2,2,256,128]{3,2,1,0:T(8,128)S(1)} %collective-permute-done.2.same1, f32[2,2,256,128]{3,2,1,0:T(8,128)S(1)} %collective-permute-done.3.other0, ...), custom_call_target="tpu_custom_call" | custom-call | flops 704643072 | bytes 3801088 | tf_op jit(solution)/shard_map/pallas_call | solution.py:80
  77.9 1.6 %shard_map.33 = f32[256,896]{1,0:T(8,128)S(1)} custom-call(s32[4]{0:T(128)S(1)} %pad_add_fusion.place, f32[2,2,256,128]{3,2,1,0:T(8,128)S(1)} %broadcast_select_fusion.same0, f32[2,2,256,128]{3,2,1,0:T(8,128)S(1)} %collective-permute-done.9.same1, f32[2,2,256,128]{3,2,1,0:T(8,128)S(1)} %collective-permute-done.10.other0, ...), custom_call_target="tpu_custom_call" | custom-call | flops 704643072 | bytes 3801088 | tf_op jit(solution)/shard_map/pallas_call | solution.py:80
  80.2 1.6 %shard_map.32 = f32[256,896]{1,0:T(8,128)S(1)} custom-call(s32[4]{0:T(128)S(1)} %pad_add_fusion.place, f32[2,2,256,128]{3,2,1,0:T(8,128)S(1)} %broadcast_select_fusion.1.same0, f32[2,2,256,128]{3,2,1,0:T(8,128)S(1)} %collective-permute-done.2.same1, f32[2,2,256,128]{3,2,1,0:T(8,128)S(1)} %collective-permute-done.3.other0, ...), custom_call_target="tpu_custom_call" | custom-call | flops 704643072 | bytes 3801088 | tf_op jit(solution)/shard_map/pallas_call | solution.py:80
  81.8 13.3 %collective-permute-done.12 = f32[256,896]{1,0:T(8,128)S(1)} collective-permute-done((f32[256,896]{1,0:T(8,128)S(1)}, f32[256,896]{1,0:T(8,128)S(1)}, u32[]{:S(2)}, u32[]{:S(2)}) %collective-permute-start.12) | collective-permute-done | bytes 917536 | tf_op jit(solution)/shard_map/ppermute | solution.py:115
  95.2 18.8 %collective-permute-done.14 = f32[256,896]{1,0:T(8,128)S(1)} collective-permute-done((f32[256,896]{1,0:T(8,128)S(1)}, f32[256,896]{1,0:T(8,128)S(1)}, u32[]{:S(2)}, u32[]{:S(2)}) %collective-permute-start.14) | collective-permute-done | bytes 917536 | tf_op jit(solution)/shard_map/ppermute | solution.py:115
  114.4 2.1 %pad_maximum_fusion = f32[4,256,896]{2,1,0:T(8,128)} fusion(f32[1,256,896]{2,1,0:T(8,128)S(1)} %multiply_bitcast_fusion, f32[1,256,896]{2,1,0:T(8,128)S(1)} %multiply_bitcast_fusion.1, f32[1,256,896]{2,1,0:T(8,128)S(1)} %multiply_bitcast_fusion.2, f32[1,256,896]{2,1,0:T(8,128)S(1)} %multiply_bitcast_fusion.3), kind=kLoop, calls=%fused_computation | loop fusion | flops 2752512 | bytes 7340032 | tf_op jit(solution)/shard_map/stack | solution.py:120
  (35 shorter events, 4.4 us)
Async XLA Ops:
  0.0 15.5 %copy-start = (f32[4,896,256]{2,1,0:T(8,128)S(1)}, f32[4,896,256]{2,1,0:T(8,128)}, u32[]{:S(2)}) copy-start(f32[4,896,256]{2,1,0:T(8,128)} %param.3) | copy-start | bytes 11010052
  1.2 3.1 %collective-permute-start = (f32[2,256,128]{2,1,0:T(8,128)S(1)}, f32[2,256,128]{2,1,0:T(8,128)S(1)}, u32[]{:S(2)}, u32[]{:S(2)}) collective-permute-start(f32[2,256,128]{2,1,0:T(8,128)S(1)} %slice_select_fusion), channel_id=1, source_target_pairs={{0,1},{1,0},{2,3},{3,2},{4,5},{5,4},{6,7},{7,6},{8,9},{9,8},{10,11... | collective-permute-start | bytes 786440 | tf_op jit(solution)/shard_map/ppermute | solution.py:110
  1.7 7.4 %collective-permute-start.7 = (f32[2,256,128]{2,1,0:T(8,128)S(1)}, f32[2,256,128]{2,1,0:T(8,128)S(1)}, u32[]{:S(2)}, u32[]{:S(2)}) collective-permute-start(f32[2,256,128]{2,1,0:T(8,128)S(1)} %slice_select_fusion), channel_id=1, source_target_pairs={{0,9},{1,16},{2,11},{3,18},{4,13},{5,20},{6,15},{7,22},{8,1},{9,24... | collective-permute-start | bytes 786440 | tf_op jit(solution)/shard_map/ppermute | solution.py:107
  4.3 8.5 %copy-start.1 = (f32[2,256,128]{2,1,0:T(8,128)}, f32[2,256,128]{2,1,0:T(8,128)S(1)}, u32[]{:S(2)}) copy-start(f32[2,256,128]{2,1,0:T(8,128)S(1)} %collective-permute-done) | copy-start | bytes 786436
  5.5 7.4 %copy-start.2 = (f32[2,256,128]{2,1,0:T(8,128)}, f32[2,256,128]{2,1,0:T(8,128)S(1)}, u32[]{:S(2)}) copy-start(f32[2,256,128]{2,1,0:T(8,128)S(1)} %get-tuple-element.6) | copy-start | bytes 786436
  5.5 6.4 %collective-permute-start.6 = (f32[2,256,128]{2,1,0:T(8,128)S(1)}, f32[2,256,128]{2,1,0:T(8,128)S(1)}, u32[]{:S(2)}, u32[]{:S(2)}) collective-permute-start(f32[2,256,128]{2,1,0:T(8,128)S(1)} %get-tuple-element.6), channel_id=1, source_target_pairs={{0,16},{1,9},{2,18},{3,11},{4,20},{5,13},{6,22},{7,15},{8,24},{9,1... | collective-permute-start | bytes 786440 | tf_op jit(solution)/shard_map/ppermute | solution.py:107
  12.9 15.3 %collective-permute-start.8 = (f32[2,2,256,128]{3,2,1,0:T(8,128)}, f32[2,2,256,128]{3,2,1,0:T(8,128)}, u32[]{:S(2)}, u32[]{:S(2)}) collective-permute-start(f32[2,2,256,128]{3,2,1,0:T(8,128)} %pad_maximum_fusion.2), channel_id=1, source_target_pairs={{0,4},{1,3},{2,6},{3,1},{4,0},{5,7},{6,2},{7,5},{8,12},{9,11},{10,... | collective-permute-start | bytes 1572872 | tf_op jit(solution)/shard_map/ppermute | solution.py:95
  16.7 34.5 %collective-permute-start.5 = (f32[896,256]{1,0:T(8,128)}, f32[896,256]{1,0:T(8,128)}, u32[]{:S(2)}, u32[]{:S(2)}) collective-permute-start(f32[896,256]{1,0:T(8,128)} %get-tuple-element.7.own_ref), channel_id=1, source_target_pairs={{0,8},{8,0},{16,24},{24,16},{1,9},{9,1},{17,25},{25,17},{2,10},{10... | collective-permute-start | bytes 2752520 | tf_op jit(solution)/shard_map/ppermute | solution.py:108
  19.1 30.3 %collective-permute-start.1 = (f32[2,2,256,128]{3,2,1,0:T(8,128)S(1)}, f32[2,2,256,128]{3,2,1,0:T(8,128)S(1)}, u32[]{:S(2)}, u32[]{:S(2)}) collective-permute-start(f32[2,2,256,128]{3,2,1,0:T(8,128)S(1)} %pad_maximum_fusion.1), channel_id=1, source_target_pairs={{0,4},{1,3},{2,6},{3,1},{4,0},{5,7},{6,2},{7,5},{8,12},{9,11},{10,... | collective-permute-start | bytes 1572872 | tf_op jit(solution)/shard_map/ppermute | solution.py:95
  28.2 21.2 %collective-permute-start.9 = (f32[2,2,256,128]{3,2,1,0:T(8,128)S(1)}, f32[2,2,256,128]{3,2,1,0:T(8,128)S(1)}, u32[]{:S(2)}, u32[]{:S(2)}) collective-permute-start(f32[2,2,256,128]{3,2,1,0:T(8,128)S(1)} %broadcast_select_fusion.same0), channel_id=1, source_target_pairs={{0,2},{1,5},{2,0},{3,7},{4,6},{5,1},{6,4},{7,3},{8,10},{9,13},{10,... | collective-permute-start | bytes 1572872 | tf_op jit(solution)/shard_map/ppermute | solution.py:96
  30.5 27.1 %collective-permute-start.13 = (f32[896,256]{1,0:T(8,128)S(1)}, f32[896,256]{1,0:T(8,128)S(1)}, u32[]{:S(2)}, u32[]{:S(2)}) collective-permute-start(f32[896,256]{1,0:T(8,128)S(1)} %get-tuple-element.8.own_ref), channel_id=1, source_target_pairs={{0,8},{8,0},{16,24},{24,16},{1,9},{9,1},{17,25},{25,17},{2,10},{10... | collective-permute-start | bytes 2752520 | tf_op jit(solution)/shard_map/ppermute | solution.py:108
  32.0 35.6 %collective-permute-start.17 = (f32[896,256]{1,0:T(8,128)S(1)}, f32[896,256]{1,0:T(8,128)S(1)}, u32[]{:S(2)}, u32[]{:S(2)}) collective-permute-start(f32[896,256]{1,0:T(8,128)S(1)} %get-tuple-element.9.own_ref), channel_id=1, source_target_pairs={{0,16},{8,24},{16,0},{24,8},{1,17},{9,25},{17,1},{25,9},{2,18},{10... | collective-permute-start | bytes 2752520 | tf_op jit(solution)/shard_map/ppermute | solution.py:108
  49.4 2.9 %collective-permute-start.10 = (f32[2,2,256,128]{3,2,1,0:T(8,128)S(1)}, f32[2,2,256,128]{3,2,1,0:T(8,128)S(1)}, u32[]{:S(2)}, u32[]{:S(2)}) collective-permute-start(f32[2,2,256,128]{3,2,1,0:T(8,128)S(1)} %broadcast_select_fusion.same0), channel_id=1, source_target_pairs={{0,1},{1,0},{2,3},{3,2},{4,5},{5,4},{6,7},{7,6},{8,9},{9,8},{10,11... | collective-permute-start | bytes 1572872 | tf_op jit(solution)/shard_map/ppermute | solution.py:97
  49.4 4.5 %collective-permute-start.11 = (f32[2,2,256,128]{3,2,1,0:T(8,128)S(1)}, f32[2,2,256,128]{3,2,1,0:T(8,128)S(1)}, u32[]{:S(2)}, u32[]{:S(2)}) collective-permute-start(f32[2,2,256,128]{3,2,1,0:T(8,128)S(1)} %collective-permute-done.9.same1), channel_id=1, source_target_pairs={{0,1},{1,0},{2,3},{3,2},{4,5},{5,4},{6,7},{7,6},{8,9},{9,8},{10,11... | collective-permute-start | bytes 1572872 | tf_op jit(solution)/shard_map/ppermute | solution.py:97
  51.2 14.8 %collective-permute-start.2 = (f32[2,2,256,128]{3,2,1,0:T(8,128)S(1)}, f32[2,2,256,128]{3,2,1,0:T(8,128)S(1)}, u32[]{:S(2)}, u32[]{:S(2)}) collective-permute-start(f32[2,2,256,128]{3,2,1,0:T(8,128)S(1)} %broadcast_select_fusion.1.same0), channel_id=1, source_target_pairs={{0,2},{1,5},{2,0},{3,7},{4,6},{5,1},{6,4},{7,3},{8,10},{9,13},{10,... | collective-permute-start | bytes 1572872 | tf_op jit(solution)/shard_map/ppermute | solution.py:96
  52.3 25.6 %collective-permute-start.15 = (f32[896,256]{1,0:T(8,128)S(1)}, f32[896,256]{1,0:T(8,128)S(1)}, u32[]{:S(2)}, u32[]{:S(2)}) collective-permute-start(f32[896,256]{1,0:T(8,128)S(1)} %get-tuple-element.10.own_ref), channel_id=1, source_target_pairs={{0,16},{8,24},{16,0},{24,8},{1,17},{9,25},{17,1},{25,9},{2,18},{10... | collective-permute-start | bytes 2752520 | tf_op jit(solution)/shard_map/ppermute | solution.py:108
  56.4 38.8 %collective-permute-start.12 = (f32[256,896]{1,0:T(8,128)S(1)}, f32[256,896]{1,0:T(8,128)S(1)}, u32[]{:S(2)}, u32[]{:S(2)}) collective-permute-start(f32[256,896]{1,0:T(8,128)S(1)} %shard_map.29), channel_id=1, source_target_pairs={{0,16},{8,24},{16,0},{24,8},{1,17},{9,25},{17,1},{25,9},{2,18},{10... | collective-permute-start | bytes 2752520 | tf_op jit(solution)/shard_map/ppermute | solution.py:115
  57.6 13.2 %collective-permute-start.3 = (f32[2,2,256,128]{3,2,1,0:T(8,128)S(1)}, f32[2,2,256,128]{3,2,1,0:T(8,128)S(1)}, u32[]{:S(2)}, u32[]{:S(2)}) collective-permute-start(f32[2,2,256,128]{3,2,1,0:T(8,128)S(1)} %broadcast_select_fusion.1.same0), channel_id=1, source_target_pairs={{0,1},{1,0},{2,3},{3,2},{4,5},{5,4},{6,7},{7,6},{8,9},{9,8},{10,11... | collective-permute-start | bytes 1572872 | tf_op jit(solution)/shard_map/ppermute | solution.py:97
  66.0 6.3 %collective-permute-start.4 = (f32[2,2,256,128]{3,2,1,0:T(8,128)S(1)}, f32[2,2,256,128]{3,2,1,0:T(8,128)S(1)}, u32[]{:S(2)}, u32[]{:S(2)}) collective-permute-start(f32[2,2,256,128]{3,2,1,0:T(8,128)S(1)} %collective-permute-done.2.same1), channel_id=1, source_target_pairs={{0,1},{1,0},{2,3},{3,2},{4,5},{5,4},{6,7},{7,6},{8,9},{9,8},{10,11... | collective-permute-start | bytes 1572872 | tf_op jit(solution)/shard_map/ppermute | solution.py:97
  67.6 46.5 %collective-permute-start.14 = (f32[256,896]{1,0:T(8,128)S(1)}, f32[256,896]{1,0:T(8,128)S(1)}, u32[]{:S(2)}, u32[]{:S(2)}) collective-permute-start(f32[256,896]{1,0:T(8,128)S(1)} %shard_map.31), channel_id=1, source_target_pairs={{0,16},{8,24},{16,0},{24,8},{1,17},{9,25},{17,1},{25,9},{2,18},{10... | collective-permute-start | bytes 2752520 | tf_op jit(solution)/shard_map/ppermute | solution.py:115
  70.8 43.4 %collective-permute-start.18 = (f32[256,896]{1,0:T(8,128)S(1)}, f32[256,896]{1,0:T(8,128)S(1)}, u32[]{:S(2)}, u32[]{:S(2)}) collective-permute-start(f32[256,896]{1,0:T(8,128)S(1)} %shard_map.35), channel_id=1, source_target_pairs={{0,8},{8,0},{16,24},{24,16},{1,9},{9,1},{17,25},{25,17},{2,10},{10... | collective-permute-start | bytes 2752520 | tf_op jit(solution)/shard_map/ppermute | solution.py:115
  79.5 34.7 %collective-permute-start.16 = (f32[256,896]{1,0:T(8,128)S(1)}, f32[256,896]{1,0:T(8,128)S(1)}, u32[]{:S(2)}, u32[]{:S(2)}) collective-permute-start(f32[256,896]{1,0:T(8,128)S(1)} %shard_map.33), channel_id=1, source_target_pairs={{0,8},{8,0},{16,24},{24,16},{1,9},{9,1},{17,25},{25,17},{2,10},{10... | collective-permute-start | bytes 2752520 | tf_op jit(solution)/shard_map/ppermute | solution.py:115

commit v2 on v0

v2 whole, which is shorter than its diff:
```python
import functools

import jax
import jax.numpy as jnp
from jax import lax
from jax.experimental import pallas as pl
from jax.experimental.pallas import tpu as pltpu
from jax.sharding import PartitionSpec as P

MESH = {"occ": 4, "vir": 8}
STEP = 256


def contract_block(left, piece):
    return lax.dot_general(
        left,
        piece,
        (((2,), (2,)), ((0,), (0,))),
        precision=lax.Precision.HIGHEST,
        preferred_element_type=jnp.float32,
    )


def gather_body(amplitudes, integrals):
    gathered = lax.all_gather(amplitudes, "vir", axis=2, tiled=True)
    panel_sum = contract_block(gathered, lax.all_gather(integrals, "occ", axis=2, tiled=True))
    return 0.5 * panel_sum


BOTH = ("occ", "vir")
X, Y = 1, 2


def pairs(move):
    return [(o * 8 + v, move(o, v >> 1, v & 1)) for o in range(4) for v in range(8)]


SAME_CORE = pairs(lambda o, z, c: (o ^ (X if c else Y)) * 8 + 2 * z + c)
CROSS_CORE = pairs(lambda o, z, c: (o ^ (Y if c else X)) * 8 + 2 * z + 1 - c)
FIRST_Z = pairs(lambda o, z, c: o * 8 + 2 * (z ^ (1 if c else 2)) + c)
SECOND_Z = pairs(lambda o, z, c: o * 8 + 2 * (z ^ (2 if c else 1)) + c)
OVER_CORE = pairs(lambda o, z, c: o * 8 + 2 * z + 1 - c)
FIRST_KIND = pairs(lambda o, z, c: (o ^ (Y if c else X)) * 8 + 2 * z + c)
SECOND_KIND = SAME_CORE

VMEM, HBM = pl.BlockSpec(memory_space=pltpu.VMEM), pl.BlockSpec(memory_space=pl.ANY)


def call(kernel, out_shape, in_specs, out_specs, flops, *args, **more):
    arrays = [*args, *jax.tree.leaves(out_shape)]
    return pl.pallas_call(
        kernel,
        out_shape=out_shape,
        in_specs=in_specs,
        out_specs=out_specs,
        compiler_params=pltpu.CompilerParams(vmem_limit_bytes=16 * 1024 * 1024),
        cost_estimate=pl.CostEstimate(flops=flops, bytes_accessed=4 * sum(a.size for a in arrays), transcendentals=0),
        **more,
    )(*args)


def like(a, *shape):
    return jax.ShapeDtypeStruct(shape, a.dtype)


def position():
    o, v = lax.axis_index("occ"), lax.axis_index("vir")
    return o // 2, lax.rem(o, 2), v // 2, lax.rem(v, 2)


def holds():
    y, x, z, core = position()
    return jnp.where(core == 0, z // 2 == y, lax.rem(z, 2) == x)


def kinds_kernel(whole, first, second, sems):
    core = position()[3]
    copies = [
        pltpu.make_async_copy(whole.at[pl.ds(2 * core, 2)], first, sems.at[0]),
        pltpu.make_async_copy(whole.at[pl.ds(2 - 2 * core, 2)], second, sems.at[1]),
    ]
    for copy in copies:
        copy.start()
    for copy in copies:
        copy.wait()


def kinds(a):
    half = like(a, 2, *a.shape[1:])
    return call(kinds_kernel, (half, half), [HBM], (VMEM, VMEM), 0, a, scratch_shapes=[pltpu.SemaphoreType.DMA((2,))])


def merge_kernel(first, second, out):
    core = position()[3]
    out[core] = first[...]
    out[1 - core] = second[...]


def merge(first, second):
    return call(merge_kernel, like(first, 2, *first.shape), [VMEM] * 2, VMEM, 0, first, second)


def choose_kernel(held, got, out):
    out[...] = jnp.where(holds(), held[...], got[...])


def choose(held, got):
    return call(choose_kernel, like(held, *held.shape), [VMEM] * 2, VMEM, 0, held, got)


def split(a):
    high = a.astype(jnp.bfloat16)
    low = (a - high.astype(jnp.float32)).astype(jnp.bfloat16)
    return high, low


def dot3(left, right):
    (lh, ll), (rh, rl) = left, right

    def dot(a, b):
        return lax.dot_general(a, b, (((1,), (1,)), ((), ())), preferred_element_type=jnp.float32)

    return dot(lh, rh) + (dot(lh, rl) + dot(ll, rh))


def partial_kernel(order, near, far, own, got, out):
    y, x, z, core = position()
    kind = core if order == 0 else 1 - core
    in_order = jnp.where(kind == 0, lax.rem(z, 2) == x, z // 2 == y)
    n_ab = own.shape[1]
    for i in range(2):
        first, second = (jnp.concatenate([a[0, i], a[1, i]], axis=1) for a in (near, far))
        t = split(jnp.concatenate([jnp.where(in_order, first, second), jnp.where(in_order, second, first)], axis=1))
        for low in range(0, n_ab, STEP):
            high = min(low + STEP, n_ab)
            v = split(jnp.concatenate([own[i, low:high, :], got[i, low:high, :]], axis=1))
            out[i, :, low:high] = dot3(t, v)


def partial_sum(order, near, far, own, got):
    n_ij, (n_g, n_ab, n_o) = near.shape[2], own.shape
    flops = 12 * n_g * n_ij * n_ab * n_o
    return call(functools.partial(partial_kernel, order), like(own, n_g, n_ij, n_ab), [VMEM] * 4, VMEM, flops, near, far, own, got)


def finish_kernel(order, kept, came, *refs):
    out, result, sems = refs[-3:]
    core = position()[3]
    kind = core if order == 0 else 1 - core
    copies = []
    for i in range(2):
        result[i] = 0.5 * (kept[i] + came[i])
        copies.append(pltpu.make_async_copy(result.at[i], out.at[2 * kind + i], sems.at[i]))
        copies[-1].start()
    for copy in copies:
        copy.wait()


def finish(order, kept, came, *out):
    n_g, *rest = kept.shape
    return call(
        functools.partial(finish_kernel, order),
        like(kept, 2 * n_g, *rest),
        [VMEM, VMEM] + [HBM] * len(out),
        HBM,
        2 * kept.size,
        kept,
        came,
        *out,
        scratch_shapes=[pltpu.VMEM(kept.shape, jnp.float32), pltpu.SemaphoreType.DMA((2,))],
        input_output_aliases={2: 0} if out else {},
    )


def tie(a, *others):
    return lax.optimization_barrier((a, *others))[0]


def permute(a, perm):
    return lax.ppermute(a, BOTH, perm)


def spread(held):
    near = choose(held, permute(held, FIRST_Z))
    near_other = permute(near, OVER_CORE)
    far = permute(tie(near, near_other), SECOND_Z)
    return [[near, far], [near_other, permute(far, OVER_CORE)]]


def hybrid_body(amplitudes, integrals):
    mine, give = kinds(amplitudes)
    same, cross = permute(mine, SAME_CORE), permute(give, CROSS_CORE)
    halves = kinds(integrals)
    send = spread(merge(tie(same, *halves), cross))
    own = [tie(halves[0], same, cross), tie(halves[1], send[0][0])]
    got = [permute(a, perm) for a, perm in zip(own, (FIRST_KIND, SECOND_KIND))]
    came = []
    for order, perm in enumerate((SECOND_KIND, FIRST_KIND)):
        came.append(permute(partial_sum(order, *send[order], own[order], got[order]), perm))

    keep = spread(tie(merge(mine, permute(tie(give, send[0][0]), OVER_CORE)), send[0][1]))
    out = []
    for order in range(2):
        kept = partial_sum(order, *keep[order], own[order], got[order])
        out = [finish(order, kept, came[order], *out)]
    return out[0]


def solution(mesh):
    in_specs = (P(None, "occ", "vir"), P(None, "vir", "occ"))
    out_specs = P(None, "occ", "vir")
    body = hybrid_body if dict(mesh.shape) == MESH else gather_body
    return jax.shard_map(body, mesh=mesh, in_specs=in_specs, out_specs=out_specs, check_vma=False)
```

time: 225 us -> 98.2 us (0.44)
  waiting for transfers between devices: 193 us -> 67 us
  matrix products: 19.1 us -> 0 us
  starting transfers between devices: 0.04 us -> 17.3 us
  between operations: 13.4 us -> 0.1 us
  Pallas kernels: 0 us -> 10.5 us
  local copies, waits for them, and re-layouts: 0 us -> 3.08 us
    all_gather x2 -> x0, waiting for transfers between devices: 191 us -> none  [the longest x1 140 us: body(): lax.all_gather(integrals, 'occ', axis=2, tiled=True)]
    ppermute x0 -> x15, waiting for transfers between devices: none -> 67 us  [permute(): return lax.ppermute(a, BOTH, perm)]
    dot_general x1 -> x0, matrix products: 19.1 us -> none  [contract_block(): lax.dot_general(left, piece, (((2,), (2,)), ((0,), (0,))), precision=lax....]
    ppermute x0 -> x15, starting transfers between devices: none -> 17.3 us  [permute(): return lax.ppermute(a, BOTH, perm)]
    pallas_call x0 -> x12, Pallas kernels: none -> 10.5 us  [call(): pl.pallas_call(kernel, out_shape=out_shape, in_specs=in_specs, out_specs=...]
    unnamed x0 -> x4, local copies, waits for them, and re-layouts: none -> 3.08 us
  transfers between devices with their start and end apart: 2 -> 15, of which waited for: 2 -> 13; matrix products, arithmetic and copies ran while one was open for 0% -> 0% of each run, Pallas kernels for 0% -> 9%
where the time goes in v2:
time: 98.2 us; the launch traced here: 98.1 us
  waiting for transfers between devices  67 us (68%)
  starting transfers between devices  17.3 us (18%)
  Pallas kernels  10.5 us (11%)
  local copies, waits for them, and re-layouts  3.08 us (3%)
    ppermute x15, waiting for transfers between devices, permute(): return lax.ppermute(a, BOTH, perm)  67 us
    ppermute x15, starting transfers between devices, permute(): return lax.ppermute(a, BOTH, perm)  17.3 us
    pallas_call x12, Pallas kernels, call(): pl.pallas_call(kernel, out_shape=out_shape, in_specs=in_specs, out_specs=...  10.5 us
    unnamed x4, local copies, waits for them, and re-layouts  3.08 us
  transfers between devices with their start and end apart: 15, of which 13 were waited for; matrix products, arithmetic and copies ran while one was open for 0% of the time, Pallas kernels for 9%

profile of v2, /device:TPU:0, one launch (start us, length us, event | category | flops | bytes accessed | tf_op | source)
XLA Modules:
  0.0 98.1 jit_solution(4778260989579326420)
XLA Ops:
  0.0 1.0 %copy-done.1 = f32[4,256,128]{2,1,0:T(8,128)S(1)} copy-done((f32[4,256,128]{2,1,0:T(8,128)S(1)}, f32[4,256,128]{2,1,0:T(8,128)}, u32[]{:S(2)}) %copy-start.1) | copy-done | bytes 524312
  1.1 3.0 %collective-permute-start = (f32[2,256,128]{2,1,0:T(8,128)S(1)}, f32[2,256,128]{2,1,0:T(8,128)S(1)}, u32[]{:S(2)}, u32[]{:S(2)}) collective-permute-start(f32[2,256,128]{2,1,0:T(8,128)S(1)} %get-tuple-element.16.first), channel_id=1, source_target_pairs={{0,16},{1,9},{2,18},{3,11},{4,20},{5,13},{6,22},{7,15},{8,24},{9,1... | collective-permute-start | bytes 786440 | tf_op jit(solution)/shard_map/ppermute | solution.py:180
  4.1 2.0 %copy-done = f32[4,896,256]{2,1,0:T(8,128)S(1)} copy-done((f32[4,896,256]{2,1,0:T(8,128)S(1)}, f32[4,896,256]{2,1,0:T(8,128)}, u32[]{:S(2)}) %copy-start) | copy-done | bytes 3670040
  6.2 0.3 shard_map.29
  6.5 3.9 %collective-permute-done.first = f32[2,256,128]{2,1,0:T(8,128)S(1)} collective-permute-done((f32[2,256,128]{2,1,0:T(8,128)S(1)}, f32[2,256,128]{2,1,0:T(8,128)S(1)}, u32[]{:S(2)}, u32[]{:S(2)}) %collective-permute-start) | collective-permute-done | bytes 262176 | tf_op jit(solution)/shard_map/ppermute | solution.py:180
  10.3 1.0 collective-permute-done.1.second
  11.3 3.2 %collective-permute-start.2 = (f32[2,2,256,128]{3,2,1,0:T(8,128)S(1)}, f32[2,2,256,128]{3,2,1,0:T(8,128)S(1)}, u32[]{:S(2)}, u32[]{:S(2)}) collective-permute-start(f32[2,2,256,128]{3,2,1,0:T(8,128)S(1)} %shard_map.30.held), channel_id=1, source_target_pairs={{0,4},{1,3},{2,6},{3,1},{4,0},{5,7},{6,2},{7,5},{8,12},{9,11},{10,... | collective-permute-start | bytes 1572872 | tf_op jit(solution)/shard_map/ppermute | solution.py:180
  14.5 1.5 %collective-permute-start.13 = (f32[2,896,256]{2,1,0:T(8,128)S(1)}, f32[2,896,256]{2,1,0:T(8,128)S(1)}, u32[]{:S(2)}, u32[]{:S(2)}) collective-permute-start(f32[2,896,256]{2,1,0:T(8,128)S(1)} %get-tuple-element.26.own), channel_id=1, source_target_pairs={{0,8},{1,17},{2,10},{3,19},{4,12},{5,21},{6,14},{7,23},{8,0},{9,25... | collective-permute-start | bytes 5505032 | tf_op jit(solution)/shard_map/ppermute | solution.py:180
  16.0 11.3 %collective-permute-done.2.got = f32[2,2,256,128]{3,2,1,0:T(8,128)S(1)} collective-permute-done((f32[2,2,256,128]{3,2,1,0:T(8,128)S(1)}, f32[2,2,256,128]{3,2,1,0:T(8,128)S(1)}, u32[]{:S(2)}, u32[]{:S(2)}) %collective-permute-start.2) | collective-permute-done | bytes 524320 | tf_op jit(solution)/shard_map/ppermute | solution.py:180
  27.3 0.1 shard_map.31.near
  27.4 1.5 %collective-permute-start.10 = (f32[2,896,256]{2,1,0:T(8,128)S(1)}, f32[2,896,256]{2,1,0:T(8,128)S(1)}, u32[]{:S(2)}, u32[]{:S(2)}) collective-permute-start(f32[2,896,256]{2,1,0:T(8,128)S(1)} %get-tuple-element.25.own), channel_id=1, source_target_pairs={{0,16},{1,9},{2,18},{3,11},{4,20},{5,13},{6,22},{7,15},{8,24},{9,1... | collective-permute-start | bytes 5505032 | tf_op jit(solution)/shard_map/ppermute | solution.py:180
  28.9 1.9 %collective-permute-done.4.near = f32[2,2,256,128]{3,2,1,0:T(8,128)S(1)} collective-permute-done((f32[2,2,256,128]{3,2,1,0:T(8,128)S(1)}, f32[2,2,256,128]{3,2,1,0:T(8,128)S(1)}, u32[]{:S(2)}, u32[]{:S(2)}) %collective-permute-start.4) | collective-permute-done | bytes 524320 | tf_op jit(solution)/shard_map/ppermute | solution.py:180
  30.8 1.0 %collective-permute-start.5 = (f32[2,2,256,128]{3,2,1,0:T(8,128)S(1)}, f32[2,2,256,128]{3,2,1,0:T(8,128)S(1)}, u32[]{:S(2)}, u32[]{:S(2)}) collective-permute-start(f32[2,2,256,128]{3,2,1,0:T(8,128)S(1)} %shard_map.31.near), channel_id=1, source_target_pairs={{0,2},{1,5},{2,0},{3,7},{4,6},{5,1},{6,4},{7,3},{8,10},{9,13},{10,... | collective-permute-start | bytes 1572872 | tf_op jit(solution)/shard_map/ppermute | solution.py:180
  31.9 13.7 %collective-permute-done.5.far = f32[2,2,256,128]{3,2,1,0:T(8,128)S(1)} collective-permute-done((f32[2,2,256,128]{3,2,1,0:T(8,128)S(1)}, f32[2,2,256,128]{3,2,1,0:T(8,128)S(1)}, u32[]{:S(2)}, u32[]{:S(2)}) %collective-permute-start.5) | collective-permute-done | bytes 524320 | tf_op jit(solution)/shard_map/ppermute | solution.py:180
  45.7 2.0 %collective-permute-start.6 = (f32[2,2,256,128]{3,2,1,0:T(8,128)S(1)}, f32[2,2,256,128]{3,2,1,0:T(8,128)S(1)}, u32[]{:S(2)}, u32[]{:S(2)}) collective-permute-start(f32[2,2,256,128]{3,2,1,0:T(8,128)S(1)} %shard_map.32.held), channel_id=1, source_target_pairs={{0,4},{1,3},{2,6},{3,1},{4,0},{5,7},{6,2},{7,5},{8,12},{9,11},{10,... | collective-permute-start | bytes 1572872 | tf_op jit(solution)/shard_map/ppermute | solution.py:180
  47.7 1.6 %collective-permute-done.13.got = f32[2,896,256]{2,1,0:T(8,128)S(1)} collective-permute-done((f32[2,896,256]{2,1,0:T(8,128)S(1)}, f32[2,896,256]{2,1,0:T(8,128)S(1)}, u32[]{:S(2)}, u32[]{:S(2)}) %collective-permute-start.13) | collective-permute-done | bytes 1835040 | tf_op jit(solution)/shard_map/ppermute | solution.py:180
  49.3 1.8 %shard_map.37 = f32[2,256,896]{2,1,0:T(8,128)S(1)} custom-call(f32[2,2,256,128]{3,2,1,0:T(8,128)S(1)} %shard_map.31.near, f32[2,2,256,128]{3,2,1,0:T(8,128)S(1)} %collective-permute-done.5.far, f32[2,896,256]{2,1,0:T(8,128)S(1)} %get-tuple-element.26.own, f32[2,896,256]{2,1,0:T(8,128)S(1)} %collective-permute-done.13.got), custom_call_target="tpu_custom_call" | custom-call | flops 1409286144 | bytes 6553600 | tf_op jit(solution)/shard_map/pallas_call | solution.py:51
  51.1 1.1 %collective-permute-start.14 = (f32[2,256,896]{2,1,0:T(8,128)S(1)}, f32[2,256,896]{2,1,0:T(8,128)S(1)}, u32[]{:S(2)}, u32[]{:S(2)}) collective-permute-start(f32[2,256,896]{2,1,0:T(8,128)S(1)} %shard_map.37), channel_id=1, source_target_pairs={{0,16},{1,9},{2,18},{3,11},{4,20},{5,13},{6,22},{7,15},{8,24},{9,1... | collective-permute-start | bytes 5505032 | tf_op jit(solution)/shard_map/ppermute | solution.py:180
  52.3 1.9 %collective-permute-done.10.got = f32[2,896,256]{2,1,0:T(8,128)S(1)} collective-permute-done((f32[2,896,256]{2,1,0:T(8,128)S(1)}, f32[2,896,256]{2,1,0:T(8,128)S(1)}, u32[]{:S(2)}, u32[]{:S(2)}) %collective-permute-start.10) | collective-permute-done | bytes 1835040 | tf_op jit(solution)/shard_map/ppermute | solution.py:180
  54.1 1.8 %shard_map.35 = f32[2,256,896]{2,1,0:T(8,128)S(1)} custom-call(f32[2,2,256,128]{3,2,1,0:T(8,128)S(1)} %collective-permute-done.4.near, f32[2,2,256,128]{3,2,1,0:T(8,128)S(1)} %collective-permute-done.11.far, f32[2,896,256]{2,1,0:T(8,128)S(1)} %get-tuple-element.25.own, f32[2,896,256]{2,1,0:T(8,128)S(1)} %collective-permute-done.10.got), custom_call_target="tpu_custom_call" | custom-call | flops 1409286144 | bytes 6553600 | tf_op jit(solution)/shard_map/pallas_call | solution.py:51
  56.0 1.6 %collective-permute-start.12 = (f32[2,256,896]{2,1,0:T(8,128)S(1)}, f32[2,256,896]{2,1,0:T(8,128)S(1)}, u32[]{:S(2)}, u32[]{:S(2)}) collective-permute-start(f32[2,256,896]{2,1,0:T(8,128)S(1)} %shard_map.35), channel_id=1, source_target_pairs={{0,8},{1,17},{2,10},{3,19},{4,12},{5,21},{6,14},{7,23},{8,0},{9,25... | collective-permute-start | bytes 5505032 | tf_op jit(solution)/shard_map/ppermute | solution.py:180
  57.5 3.0 %collective-permute-done.6.got = f32[2,2,256,128]{3,2,1,0:T(8,128)S(1)} collective-permute-done((f32[2,2,256,128]{3,2,1,0:T(8,128)S(1)}, f32[2,2,256,128]{3,2,1,0:T(8,128)S(1)}, u32[]{:S(2)}, u32[]{:S(2)}) %collective-permute-start.6) | collective-permute-done | bytes 524320 | tf_op jit(solution)/shard_map/ppermute | solution.py:180
  60.6 0.1 collective-permute-start.7
  60.7 1.8 %collective-permute-done.7.near = f32[2,2,256,128]{3,2,1,0:T(8,128)S(1)} collective-permute-done((f32[2,2,256,128]{3,2,1,0:T(8,128)S(1)}, f32[2,2,256,128]{3,2,1,0:T(8,128)S(1)}, u32[]{:S(2)}, u32[]{:S(2)}) %collective-permute-start.7) | collective-permute-done | bytes 524320 | tf_op jit(solution)/shard_map/ppermute | solution.py:180
  62.6 2.2 %collective-permute-start.8 = (f32[2,2,256,128]{3,2,1,0:T(8,128)S(1)}, f32[2,2,256,128]{3,2,1,0:T(8,128)S(1)}, u32[]{:S(2)}, u32[]{:S(2)}) collective-permute-start(f32[2,2,256,128]{3,2,1,0:T(8,128)S(1)} %shard_map.33.near), channel_id=1, source_target_pairs={{0,2},{1,5},{2,0},{3,7},{4,6},{5,1},{6,4},{7,3},{8,10},{9,13},{10,... | collective-permute-start | bytes 1572872 | tf_op jit(solution)/shard_map/ppermute | solution.py:180
  64.8 12.6 %collective-permute-done.8.far = f32[2,2,256,128]{3,2,1,0:T(8,128)S(1)} collective-permute-done((f32[2,2,256,128]{3,2,1,0:T(8,128)S(1)}, f32[2,2,256,128]{3,2,1,0:T(8,128)S(1)}, u32[]{:S(2)}, u32[]{:S(2)}) %collective-permute-start.8) | collective-permute-done | bytes 524320 | tf_op jit(solution)/shard_map/ppermute | solution.py:180
  77.5 1.8 %shard_map.36.kept = f32[2,256,896]{2,1,0:T(8,128)S(1)} custom-call(f32[2,2,256,128]{3,2,1,0:T(8,128)S(1)} %shard_map.33.near, f32[2,2,256,128]{3,2,1,0:T(8,128)S(1)} %collective-permute-done.8.far, f32[2,896,256]{2,1,0:T(8,128)S(1)} %get-tuple-element.26.own, f32[2,896,256]{2,1,0:T(8,128)S(1)} %collective-permute-done.13.got), custom_call_target="tpu_custom_call" | custom-call | flops 1409286144 | bytes 6553600 | tf_op jit(solution)/shard_map/pallas_call | solution.py:51
  79.4 1.8 %shard_map.34.kept = f32[2,256,896]{2,1,0:T(8,128)S(1)} custom-call(f32[2,2,256,128]{3,2,1,0:T(8,128)S(1)} %collective-permute-done.7.near, f32[2,2,256,128]{3,2,1,0:T(8,128)S(1)} %collective-permute-done.9.far, f32[2,896,256]{2,1,0:T(8,128)S(1)} %get-tuple-element.25.own, f32[2,896,256]{2,1,0:T(8,128)S(1)} %collective-permute-done.10.got), custom_call_target="tpu_custom_call" | custom-call | flops 1409286144 | bytes 6553600 | tf_op jit(solution)/shard_map/pallas_call | solution.py:51
  81.2 5.6 %collective-permute-done.14.came = f32[2,256,896]{2,1,0:T(8,128)S(1)} collective-permute-done((f32[2,256,896]{2,1,0:T(8,128)S(1)}, f32[2,256,896]{2,1,0:T(8,128)S(1)}, u32[]{:S(2)}, u32[]{:S(2)}) %collective-permute-start.14) | collective-permute-done | bytes 1835040 | tf_op jit(solution)/shard_map/ppermute | solution.py:180
  86.8 1.3 %shard_map.38.refs_0_ = f32[4,256,896]{2,1,0:T(8,128)} custom-call(f32[2,256,896]{2,1,0:T(8,128)S(1)} %shard_map.36.kept, f32[2,256,896]{2,1,0:T(8,128)S(1)} %collective-permute-done.14.came), custom_call_target="tpu_custom_call" | custom-call | flops 917504 | bytes 7340032 | tf_op jit(solution)/shard_map/pallas_call | solution.py:51
  88.2 8.6 %collective-permute-done.12.came = f32[2,256,896]{2,1,0:T(8,128)S(1)} collective-permute-done((f32[2,256,896]{2,1,0:T(8,128)S(1)}, f32[2,256,896]{2,1,0:T(8,128)S(1)}, u32[]{:S(2)}, u32[]{:S(2)}) %collective-permute-start.12) | collective-permute-done | bytes 1835040 | tf_op jit(solution)/shard_map/ppermute | solution.py:180
  96.7 1.3 %shard_map.39 = f32[4,256,896]{2,1,0:T(8,128)} custom-call(f32[2,256,896]{2,1,0:T(8,128)S(1)} %shard_map.34.kept, f32[2,256,896]{2,1,0:T(8,128)S(1)} %collective-permute-done.12.came, f32[4,256,896]{2,1,0:T(8,128)} %shard_map.38.refs_0_), custom_call_target="tpu_custom_call", output_to_operand_aliasing={{}: (2, {})} | custom-call | flops 917504 | bytes 11010048 | tf_op jit(solution)/shard_map/pallas_call | solution.py:51
  (14 shorter events, 0.3 us)
Async XLA Ops:
  0.0 1.0 %copy-start.1 = (f32[4,256,128]{2,1,0:T(8,128)S(1)}, f32[4,256,128]{2,1,0:T(8,128)}, u32[]{:S(2)}) copy-start(f32[4,256,128]{2,1,0:T(8,128)} %whole.2) | copy-start | bytes 1572868
  1.1 9.2 %collective-permute-start = (f32[2,256,128]{2,1,0:T(8,128)S(1)}, f32[2,256,128]{2,1,0:T(8,128)S(1)}, u32[]{:S(2)}, u32[]{:S(2)}) collective-permute-start(f32[2,256,128]{2,1,0:T(8,128)S(1)} %get-tuple-element.16.first), channel_id=1, source_target_pairs={{0,16},{1,9},{2,18},{3,11},{4,20},{5,13},{6,22},{7,15},{8,24},{9,1... | collective-permute-start | bytes 786440 | tf_op jit(solution)/shard_map/ppermute | solution.py:180
  4.1 7.2 %collective-permute-start.1 = (f32[2,256,128]{2,1,0:T(8,128)S(1)}, f32[2,256,128]{2,1,0:T(8,128)S(1)}, u32[]{:S(2)}, u32[]{:S(2)}) collective-permute-start(f32[2,256,128]{2,1,0:T(8,128)S(1)} %get-tuple-element.21), channel_id=1, source_target_pairs={{0,9},{1,16},{2,11},{3,18},{4,13},{5,20},{6,15},{7,22},{8,1},{9,24... | collective-permute-start | bytes 786440 | tf_op jit(solution)/shard_map/ppermute | solution.py:180
  4.1 2.0 %copy-start = (f32[4,896,256]{2,1,0:T(8,128)S(1)}, f32[4,896,256]{2,1,0:T(8,128)}, u32[]{:S(2)}) copy-start(f32[4,896,256]{2,1,0:T(8,128)} %whole.3) | copy-start | bytes 11010052
  11.3 16.0 %collective-permute-start.2 = (f32[2,2,256,128]{3,2,1,0:T(8,128)S(1)}, f32[2,2,256,128]{3,2,1,0:T(8,128)S(1)}, u32[]{:S(2)}, u32[]{:S(2)}) collective-permute-start(f32[2,2,256,128]{3,2,1,0:T(8,128)S(1)} %shard_map.30.held), channel_id=1, source_target_pairs={{0,4},{1,3},{2,6},{3,1},{4,0},{5,7},{6,2},{7,5},{8,12},{9,11},{10,... | collective-permute-start | bytes 1572872 | tf_op jit(solution)/shard_map/ppermute | solution.py:180
  14.5 34.8 %collective-permute-start.13 = (f32[2,896,256]{2,1,0:T(8,128)S(1)}, f32[2,896,256]{2,1,0:T(8,128)S(1)}, u32[]{:S(2)}, u32[]{:S(2)}) collective-permute-start(f32[2,896,256]{2,1,0:T(8,128)S(1)} %get-tuple-element.26.own), channel_id=1, source_target_pairs={{0,8},{1,17},{2,10},{3,19},{4,12},{5,21},{6,14},{7,23},{8,0},{9,25... | collective-permute-start | bytes 5505032 | tf_op jit(solution)/shard_map/ppermute | solution.py:180
  27.4 26.7 %collective-permute-start.10 = (f32[2,896,256]{2,1,0:T(8,128)S(1)}, f32[2,896,256]{2,1,0:T(8,128)S(1)}, u32[]{:S(2)}, u32[]{:S(2)}) collective-permute-start(f32[2,896,256]{2,1,0:T(8,128)S(1)} %get-tuple-element.25.own), channel_id=1, source_target_pairs={{0,16},{1,9},{2,18},{3,11},{4,20},{5,13},{6,22},{7,15},{8,24},{9,1... | collective-permute-start | bytes 5505032 | tf_op jit(solution)/shard_map/ppermute | solution.py:180
  28.9 1.9 %collective-permute-start.4 = (f32[2,2,256,128]{3,2,1,0:T(8,128)S(1)}, f32[2,2,256,128]{3,2,1,0:T(8,128)S(1)}, u32[]{:S(2)}, u32[]{:S(2)}) collective-permute-start(f32[2,2,256,128]{3,2,1,0:T(8,128)S(1)} %shard_map.31.near), channel_id=1, source_target_pairs={{0,1},{1,0},{2,3},{3,2},{4,5},{5,4},{6,7},{7,6},{8,9},{9,8},{10,11... | collective-permute-start | bytes 1572872 | tf_op jit(solution)/shard_map/ppermute | solution.py:180
  30.8 14.8 %collective-permute-start.5 = (f32[2,2,256,128]{3,2,1,0:T(8,128)S(1)}, f32[2,2,256,128]{3,2,1,0:T(8,128)S(1)}, u32[]{:S(2)}, u32[]{:S(2)}) collective-permute-start(f32[2,2,256,128]{3,2,1,0:T(8,128)S(1)} %shard_map.31.near), channel_id=1, source_target_pairs={{0,2},{1,5},{2,0},{3,7},{4,6},{5,1},{6,4},{7,3},{8,10},{9,13},{10,... | collective-permute-start | bytes 1572872 | tf_op jit(solution)/shard_map/ppermute | solution.py:180
  31.9 13.8 %collective-permute-start.3 = (f32[2,256,128]{2,1,0:T(8,128)S(1)}, f32[2,256,128]{2,1,0:T(8,128)S(1)}, u32[]{:S(2)}, u32[]{:S(2)}) collective-permute-start(f32[2,256,128]{2,1,0:T(8,128)S(1)} %get-tuple-element.21), channel_id=1, source_target_pairs={{0,1},{1,0},{2,3},{3,2},{4,5},{5,4},{6,7},{7,6},{8,9},{9,8},{10,11... | collective-permute-start | bytes 786440 | tf_op jit(solution)/shard_map/ppermute | solution.py:180
  45.6 6.7 %collective-permute-start.11 = (f32[2,2,256,128]{3,2,1,0:T(8,128)S(1)}, f32[2,2,256,128]{3,2,1,0:T(8,128)S(1)}, u32[]{:S(2)}, u32[]{:S(2)}) collective-permute-start(f32[2,2,256,128]{3,2,1,0:T(8,128)S(1)} %collective-permute-done.5.far), channel_id=1, source_target_pairs={{0,1},{1,0},{2,3},{3,2},{4,5},{5,4},{6,7},{7,6},{8,9},{9,8},{10,11... | collective-permute-start | bytes 1572872 | tf_op jit(solution)/shard_map/ppermute | solution.py:180
  45.7 14.8 %collective-permute-start.6 = (f32[2,2,256,128]{3,2,1,0:T(8,128)S(1)}, f32[2,2,256,128]{3,2,1,0:T(8,128)S(1)}, u32[]{:S(2)}, u32[]{:S(2)}) collective-permute-start(f32[2,2,256,128]{3,2,1,0:T(8,128)S(1)} %shard_map.32.held), channel_id=1, source_target_pairs={{0,4},{1,3},{2,6},{3,1},{4,0},{5,7},{6,2},{7,5},{8,12},{9,11},{10,... | collective-permute-start | bytes 1572872 | tf_op jit(solution)/shard_map/ppermute | solution.py:180
  51.1 35.7 %collective-permute-start.14 = (f32[2,256,896]{2,1,0:T(8,128)S(1)}, f32[2,256,896]{2,1,0:T(8,128)S(1)}, u32[]{:S(2)}, u32[]{:S(2)}) collective-permute-start(f32[2,256,896]{2,1,0:T(8,128)S(1)} %shard_map.37), channel_id=1, source_target_pairs={{0,16},{1,9},{2,18},{3,11},{4,20},{5,13},{6,22},{7,15},{8,24},{9,1... | collective-permute-start | bytes 5505032 | tf_op jit(solution)/shard_map/ppermute | solution.py:180
  56.0 40.7 %collective-permute-start.12 = (f32[2,256,896]{2,1,0:T(8,128)S(1)}, f32[2,256,896]{2,1,0:T(8,128)S(1)}, u32[]{:S(2)}, u32[]{:S(2)}) collective-permute-start(f32[2,256,896]{2,1,0:T(8,128)S(1)} %shard_map.35), channel_id=1, source_target_pairs={{0,8},{1,17},{2,10},{3,19},{4,12},{5,21},{6,14},{7,23},{8,0},{9,25... | collective-permute-start | bytes 5505032 | tf_op jit(solution)/shard_map/ppermute | solution.py:180
  60.6 2.0 %collective-permute-start.7 = (f32[2,2,256,128]{3,2,1,0:T(8,128)S(1)}, f32[2,2,256,128]{3,2,1,0:T(8,128)S(1)}, u32[]{:S(2)}, u32[]{:S(2)}) collective-permute-start(f32[2,2,256,128]{3,2,1,0:T(8,128)S(1)} %shard_map.33.near), channel_id=1, source_target_pairs={{0,1},{1,0},{2,3},{3,2},{4,5},{5,4},{6,7},{7,6},{8,9},{9,8},{10,11... | collective-permute-start | bytes 1572872 | tf_op jit(solution)/shard_map/ppermute | solution.py:180
  62.6 14.9 %collective-permute-start.8 = (f32[2,2,256,128]{3,2,1,0:T(8,128)S(1)}, f32[2,2,256,128]{3,2,1,0:T(8,128)S(1)}, u32[]{:S(2)}, u32[]{:S(2)}) collective-permute-start(f32[2,2,256,128]{3,2,1,0:T(8,128)S(1)} %shard_map.33.near), channel_id=1, source_target_pairs={{0,2},{1,5},{2,0},{3,7},{4,6},{5,1},{6,4},{7,3},{8,10},{9,13},{10,... | collective-permute-start | bytes 1572872 | tf_op jit(solution)/shard_map/ppermute | solution.py:180
  77.5 1.9 %collective-permute-start.9 = (f32[2,2,256,128]{3,2,1,0:T(8,128)S(1)}, f32[2,2,256,128]{3,2,1,0:T(8,128)S(1)}, u32[]{:S(2)}, u32[]{:S(2)}) collective-permute-start(f32[2,2,256,128]{3,2,1,0:T(8,128)S(1)} %collective-permute-done.8.far), channel_id=1, source_target_pairs={{0,1},{1,0},{2,3},{3,2},{4,5},{5,4},{6,7},{7,6},{8,9},{9,8},{10,11... | collective-permute-start | bytes 1572872 | tf_op jit(solution)/shard_map/ppermute | solution.py:180

commit v3 on v2

--- a/solution.py
+++ b/solution.py
@@ -9,6 +9,7 @@
 
 MESH = {"occ": 4, "vir": 8}
 STEP = 256
+CUTS = (), (512,)
 
 
 def contract_block(left, piece):
@@ -73,21 +74,27 @@
     return jnp.where(core == 0, z // 2 == y, lax.rem(z, 2) == x)
 
 
-def kinds_kernel(whole, first, second, sems):
+def kinds_kernel(spans, whole, *refs):
+    *out, sems = refs
     core = position()[3]
-    copies = [
-        pltpu.make_async_copy(whole.at[pl.ds(2 * core, 2)], first, sems.at[0]),
-        pltpu.make_async_copy(whole.at[pl.ds(2 - 2 * core, 2)], second, sems.at[1]),
-    ]
+    copies = []
+    for ref, (order, low, high) in zip(out, spans):
+        kind = core if order == 0 else 1 - core
+        source = whole.at[pl.ds(2 * kind, 2), pl.ds(low, high - low)]
+        copies.append(pltpu.make_async_copy(source, ref, sems.at[len(copies)]))
     for copy in copies:
         copy.start()
     for copy in copies:
         copy.wait()
 
 
-def kinds(a):
-    half = like(a, 2, *a.shape[1:])
-    return call(kinds_kernel, (half, half), [HBM], (VMEM, VMEM), 0, a, scratch_shapes=[pltpu.SemaphoreType.DMA((2,))])
+def kinds(a, *cuts):
+    n = a.shape[1]
+    spans = [(order, low, high) for order, cut in enumerate(cuts) for low, high in zip((0, *cut), (*cut, n))]
+    out = [like(a, 2, high - low, a.shape[2]) for _, low, high in spans]
+    sems = pltpu.SemaphoreType.DMA((len(spans),))
+    pieces = call(functools.partial(kinds_kernel, spans), out, [HBM], [VMEM] * len(out), 0, a, scratch_shapes=[sems])
+    return [[p for p, span in zip(pieces, spans) if span[0] == order] for order in range(2)]
 
 
 def merge_kernel(first, second, out):
@@ -100,12 +107,23 @@
     return call(merge_kernel, like(first, 2, *first.shape), [VMEM] * 2, VMEM, 0, first, second)
 
 
-def choose_kernel(held, got, out):
+def choose_kernel(held, got, out, *small):
     out[...] = jnp.where(holds(), held[...], got[...])
-
-
-def choose(held, got):
-    return call(choose_kernel, like(held, *held.shape), [VMEM] * 2, VMEM, 0, held, got)
+    for ref in small:
+        ref[...] = out[0, 0, : ref.shape[0], :]
+
+
+def choose(held, got, *small):
+    shapes = [like(held, *held.shape)] + [like(held, 8, held.shape[3])] * len(small)
+    return call(choose_kernel, shapes, [VMEM] * 2, [VMEM] * len(shapes), 0, held, got)
+
+
+def gate_kernel(a, small, out):
+    del a, small, out
+
+
+def gate(a, small):
+    return call(gate_kernel, like(a, *a.shape), [HBM] * 2, HBM, 0, a, small, input_output_aliases={0: 0})
 
 
 def split(a):
@@ -123,24 +141,30 @@
     return dot(lh, rh) + (dot(lh, rl) + dot(ll, rh))
 
 
-def partial_kernel(order, near, far, own, got, out):
+def partial_kernel(order, near, far, *refs):
+    *chunks, out = refs
     y, x, z, core = position()
     kind = core if order == 0 else 1 - core
     in_order = jnp.where(kind == 0, lax.rem(z, 2) == x, z // 2 == y)
-    n_ab = own.shape[1]
     for i in range(2):
         first, second = (jnp.concatenate([a[0, i], a[1, i]], axis=1) for a in (near, far))
         t = split(jnp.concatenate([jnp.where(in_order, first, second), jnp.where(in_order, second, first)], axis=1))
-        for low in range(0, n_ab, STEP):
-            high = min(low + STEP, n_ab)
-            v = split(jnp.concatenate([own[i, low:high, :], got[i, low:high, :]], axis=1))
-            out[i, :, low:high] = dot3(t, v)
+        at = 0
+        for own, got in zip(chunks[::2], chunks[1::2]):
+            n_ab = own.shape[1]
+            for low in range(0, n_ab, STEP):
+                high = min(low + STEP, n_ab)
+                v = split(jnp.concatenate([own[i, low:high, :], got[i, low:high, :]], axis=1))
+                out[i, :, at : at + high - low] = dot3(t, v)
+                at += high - low
 
 
 def partial_sum(order, near, far, own, got):
-    n_ij, (n_g, n_ab, n_o) = near.shape[2], own.shape
+    n_ij, (n_g, _, n_o), n_ab = near.shape[2], own[0].shape, sum(a.shape[1] for a in own)
+    chunks = [a for pair in zip(own, got) for a in pair]
     flops = 12 * n_g * n_ij * n_ab * n_o
-    return call(functools.partial(partial_kernel, order), like(own, n_g, n_ij, n_ab), [VMEM] * 4, VMEM, flops, near, far, own, got)
+    specs = [VMEM] * (2 + len(chunks))
+    return call(functools.partial(partial_kernel, order), like(near, n_g, n_ij, n_ab), specs, VMEM, flops, near, far, *chunks)
 
 
 def finish_kernel(order, kept, came, *refs):
@@ -180,25 +204,32 @@
     return lax.ppermute(a, BOTH, perm)
 
 
-def spread(held):
-    near = choose(held, permute(held, FIRST_Z))
-    near_other = permute(near, OVER_CORE)
-    far = permute(tie(near, near_other), SECOND_Z)
+def spread(held, short):
+    if short:
+        near, small = choose(held, permute(held, FIRST_Z), 1)
+        near = gate(near, permute(small, OVER_CORE))
+        near_other = permute(near, OVER_CORE)
+        far = permute(near, SECOND_Z)
+    else:
+        (near,) = choose(held, permute(held, FIRST_Z))
+        near_other = permute(near, OVER_CORE)
+        far = permute(tie(near, near_other), SECOND_Z)
     return [[near, far], [near_other, permute(far, OVER_CORE)]]
 
 
 def hybrid_body(amplitudes, integrals):
-    mine, give = kinds(amplitudes)
+    (mine,), (give,) = kinds(amplitudes, (), ())
     same, cross = permute(mine, SAME_CORE), permute(give, CROSS_CORE)
-    halves = kinds(integrals)
-    send = spread(merge(tie(same, *halves), cross))
-    own = [tie(halves[0], same, cross), tie(halves[1], send[0][0])]
-    got = [permute(a, perm) for a, perm in zip(own, (FIRST_KIND, SECOND_KIND))]
+    own = kinds(integrals, *CUTS)
+    send = spread(merge(tie(same, *own[0], *own[1]), cross), True)
+    own[0] = [tie(a, same, cross) for a in own[0]]
+    own[1] = [tie(a, send[0][0]) for a in own[1]]
+    got = [[permute(a, perm) for a in pieces] for pieces, perm in zip(own, (FIRST_KIND, SECOND_KIND))]
     came = []
     for order, perm in enumerate((SECOND_KIND, FIRST_KIND)):
         came.append(permute(partial_sum(order, *send[order], own[order], got[order]), perm))
 
-    keep = spread(tie(merge(mine, permute(tie(give, send[0][0]), OVER_CORE)), send[0][1]))
+    keep = spread(tie(merge(mine, permute(tie(give, send[0][0]), OVER_CORE)), send[0][1]), False)
     out = []
     for order in range(2):
         kept = partial_sum(order, *keep[order], own[order], got[order])

time: 98.2 us -> 95 us (0.967)
  waiting for transfers between devices: 67 us -> 65 us
  starting transfers between devices: 17.3 us -> 16.1 us
    ppermute x15 -> x17, waiting for transfers between devices: 67 us -> 65 us  [permute(): return lax.ppermute(a, BOTH, perm)]
    ppermute x15 -> x17, starting transfers between devices: 17.3 us -> 16.1 us  [permute(): return lax.ppermute(a, BOTH, perm)]
    pallas_call x12 -> x13, Pallas kernels: 10.5 us -> 10.6 us  [call(): pl.pallas_call(kernel, out_shape=out_shape, in_specs=in_specs, out_specs=...]
  transfers between devices with their start and end apart: 15 -> 17, of which waited for: 13 -> 13; matrix products, arithmetic and copies ran while one was open for 0% -> 0% of each run, Pallas kernels for 9% -> 10%
where the time goes in v3:
time: 95 us; the launch traced here: 94.8 us
  waiting for transfers between devices  65 us (68%)
  starting transfers between devices  16.1 us (17%)
  Pallas kernels  10.6 us (11%)
  local copies, waits for them, and re-layouts  3.08 us (3%)
    ppermute x17, waiting for transfers between devices, permute(): return lax.ppermute(a, BOTH, perm)  65 us
    ppermute x17, starting transfers between devices, permute(): return lax.ppermute(a, BOTH, perm)  16.1 us
    pallas_call x13, Pallas kernels, call(): pl.pallas_call(kernel, out_shape=out_shape, in_specs=in_specs, out_specs=...  10.6 us
    unnamed x4, local copies, waits for them, and re-layouts  3.08 us
  transfers between devices with their start and end apart: 17, of which 13 were waited for; matrix products, arithmetic and copies ran while one was open for 0% of the time, Pallas kernels for 10%

profile of v3, /device:TPU:0, one launch (start us, length us, event | category | flops | bytes accessed | tf_op | source)
XLA Modules:
  0.0 94.8 jit_solution(9163170707343131217)
XLA Ops:
  0.0 1.0 %copy-done.1 = f32[4,256,128]{2,1,0:T(8,128)S(1)} copy-done((f32[4,256,128]{2,1,0:T(8,128)S(1)}, f32[4,256,128]{2,1,0:T(8,128)}, u32[]{:S(2)}) %copy-start.1) | copy-done | bytes 524312
  1.1 3.0 %collective-permute-start = (f32[2,256,128]{2,1,0:T(8,128)S(1)}, f32[2,256,128]{2,1,0:T(8,128)S(1)}, u32[]{:S(2)}, u32[]{:S(2)}) collective-permute-start(f32[2,256,128]{2,1,0:T(8,128)S(1)} %get-tuple-element.19.first), channel_id=1, source_target_pairs={{0,16},{1,9},{2,18},{3,11},{4,20},{5,13},{6,22},{7,15},{8,24},{9,1... | collective-permute-start | bytes 786440 | tf_op jit(solution)/shard_map/ppermute | solution.py:204
  4.1 2.0 %copy-done = f32[4,896,256]{2,1,0:T(8,128)S(1)} copy-done((f32[4,896,256]{2,1,0:T(8,128)S(1)}, f32[4,896,256]{2,1,0:T(8,128)}, u32[]{:S(2)}) %copy-start) | copy-done | bytes 3670040
  6.2 0.3 shard_map.29
  6.5 3.9 %collective-permute-done.first = f32[2,256,128]{2,1,0:T(8,128)S(1)} collective-permute-done((f32[2,256,128]{2,1,0:T(8,128)S(1)}, f32[2,256,128]{2,1,0:T(8,128)S(1)}, u32[]{:S(2)}, u32[]{:S(2)}) %collective-permute-start) | collective-permute-done | bytes 262176 | tf_op jit(solution)/shard_map/ppermute | solution.py:204
  10.3 1.0 %collective-permute-done.1.second = f32[2,256,128]{2,1,0:T(8,128)S(1)} collective-permute-done((f32[2,256,128]{2,1,0:T(8,128)S(1)}, f32[2,256,128]{2,1,0:T(8,128)S(1)}, u32[]{:S(2)}, u32[]{:S(2)}) %collective-permute-start.1) | collective-permute-done | bytes 262176 | tf_op jit(solution)/shard_map/ppermute | solution.py:204
  11.3 2.0 %collective-permute-start.15 = (f32[2,896,256]{2,1,0:T(8,128)S(1)}, f32[2,896,256]{2,1,0:T(8,128)S(1)}, u32[]{:S(2)}, u32[]{:S(2)}) collective-permute-start(f32[2,896,256]{2,1,0:T(8,128)S(1)} %get-tuple-element.32.refs_0_), channel_id=1, source_target_pairs={{0,8},{1,17},{2,10},{3,19},{4,12},{5,21},{6,14},{7,23},{8,0},{9,25... | collective-permute-start | bytes 5505032 | tf_op jit(solution)/shard_map/ppermute | solution.py:204
  13.3 2.7 %collective-permute-start.2 = (f32[2,2,256,128]{3,2,1,0:T(8,128)S(1)}, f32[2,2,256,128]{3,2,1,0:T(8,128)S(1)}, u32[]{:S(2)}, u32[]{:S(2)}) collective-permute-start(f32[2,2,256,128]{3,2,1,0:T(8,128)S(1)} %shard_map.30.held), channel_id=1, source_target_pairs={{0,4},{1,3},{2,6},{3,1},{4,0},{5,7},{6,2},{7,5},{8,12},{9,11},{10,... | collective-permute-start | bytes 1572872 | tf_op jit(solution)/shard_map/ppermute | solution.py:204
  16.0 13.2 %collective-permute-done.2.got = f32[2,2,256,128]{3,2,1,0:T(8,128)S(1)} collective-permute-done((f32[2,2,256,128]{3,2,1,0:T(8,128)S(1)}, f32[2,2,256,128]{3,2,1,0:T(8,128)S(1)}, u32[]{:S(2)}, u32[]{:S(2)}) %collective-permute-start.2) | collective-permute-done | bytes 524320 | tf_op jit(solution)/shard_map/ppermute | solution.py:204
  29.3 1.2 %collective-permute-done.3.small = f32[8,128]{1,0:T(8,128)S(1)} collective-permute-done((f32[8,128]{1,0:T(8,128)S(1)}, f32[8,128]{1,0:T(8,128)S(1)}, u32[]{:S(2)}, u32[]{:S(2)}) %collective-permute-start.3) | collective-permute-done | bytes 4128 | tf_op jit(solution)/shard_map/ppermute | solution.py:204
  30.5 0.7 collective-permute-start.5
  31.2 1.5 %collective-permute-start.10 = (f32[2,512,256]{2,1,0:T(8,128)S(1)}, f32[2,512,256]{2,1,0:T(8,128)S(1)}, u32[]{:S(2)}, u32[]{:S(2)}) collective-permute-start(f32[2,512,256]{2,1,0:T(8,128)S(1)} %get-tuple-element.30.refs_0_), channel_id=1, source_target_pairs={{0,16},{1,9},{2,18},{3,11},{4,20},{5,13},{6,22},{7,15},{8,24},{9,1... | collective-permute-start | bytes 3145736 | tf_op jit(solution)/shard_map/ppermute | solution.py:204
  32.6 0.6 collective-permute-start.11
  33.2 1.0 %collective-permute-done.4.second = f32[2,256,128]{2,1,0:T(8,128)S(1)} collective-permute-done((f32[2,256,128]{2,1,0:T(8,128)S(1)}, f32[2,256,128]{2,1,0:T(8,128)S(1)}, u32[]{:S(2)}, u32[]{:S(2)}) %collective-permute-start.4) | collective-permute-done | bytes 262176 | tf_op jit(solution)/shard_map/ppermute | solution.py:204
  34.2 0.1 collective-permute-start.12
  34.3 11.0 %collective-permute-done.5.far = f32[2,2,256,128]{3,2,1,0:T(8,128)S(1)} collective-permute-done((f32[2,2,256,128]{3,2,1,0:T(8,128)S(1)}, f32[2,2,256,128]{3,2,1,0:T(8,128)S(1)}, u32[]{:S(2)}, u32[]{:S(2)}) %collective-permute-start.5) | collective-permute-done | bytes 524320 | tf_op jit(solution)/shard_map/ppermute | solution.py:204
  45.3 1.7 %collective-permute-start.6 = (f32[2,2,256,128]{3,2,1,0:T(8,128)S(1)}, f32[2,2,256,128]{3,2,1,0:T(8,128)S(1)}, u32[]{:S(2)}, u32[]{:S(2)}) collective-permute-start(f32[2,2,256,128]{3,2,1,0:T(8,128)S(1)} %shard_map.33.held), channel_id=1, source_target_pairs={{0,4},{1,3},{2,6},{3,1},{4,0},{5,7},{6,2},{7,5},{8,12},{9,11},{10,... | collective-permute-start | bytes 1572872 | tf_op jit(solution)/shard_map/ppermute | solution.py:204
  47.0 1.8 %shard_map.38 = f32[2,256,896]{2,1,0:T(8,128)S(1)} custom-call(f32[2,2,256,128]{3,2,1,0:T(8,128)S(1)} %shard_map.32.near, f32[2,2,256,128]{3,2,1,0:T(8,128)S(1)} %collective-permute-done.5.far, f32[2,896,256]{2,1,0:T(8,128)S(1)} %get-tuple-element.32.refs_0_, f32[2,896,256]{2,1,0:T(8,128)S(1)} %collective-permute-done.15.refs_1_), custom_call_target="tpu_custom_call" | custom-call | flops 1409286144 | bytes 6553600 | tf_op jit(solution)/shard_map/pallas_call | solution.py:52
  48.9 1.5 %collective-permute-start.16 = (f32[2,256,896]{2,1,0:T(8,128)S(1)}, f32[2,256,896]{2,1,0:T(8,128)S(1)}, u32[]{:S(2)}, u32[]{:S(2)}) collective-permute-start(f32[2,256,896]{2,1,0:T(8,128)S(1)} %shard_map.38), channel_id=1, source_target_pairs={{0,16},{1,9},{2,18},{3,11},{4,20},{5,13},{6,22},{7,15},{8,24},{9,1... | collective-permute-start | bytes 5505032 | tf_op jit(solution)/shard_map/ppermute | solution.py:204
  50.4 4.0 %collective-permute-done.11.refs_3_ = f32[2,384,256]{2,1,0:T(8,128)S(1)} collective-permute-done((f32[2,384,256]{2,1,0:T(8,128)S(1)}, f32[2,384,256]{2,1,0:T(8,128)S(1)}, u32[]{:S(2)}, u32[]{:S(2)}) %collective-permute-start.11) | collective-permute-done | bytes 786464 | tf_op jit(solution)/shard_map/ppermute | solution.py:204
  54.4 1.8 %shard_map.36 = f32[2,256,896]{2,1,0:T(8,128)S(1)} custom-call(f32[2,2,256,128]{3,2,1,0:T(8,128)S(1)} %collective-permute-done.12.near, f32[2,2,256,128]{3,2,1,0:T(8,128)S(1)} %collective-permute-done.13.far, f32[2,512,256]{2,1,0:T(8,128)S(1)} %get-tuple-element.30.refs_0_, f32[2,512,256]{2,1,0:T(8,128)S(1)} %collective-permute-done.10.refs_1_, ...), custom_call_target="tpu_custom_call" | custom-call | flops 1409286144 | bytes 6553600 | tf_op jit(solution)/shard_map/pallas_call | solution.py:52
  56.2 0.6 collective-permute-start.14
  56.8 3.6 %collective-permute-done.6.got = f32[2,2,256,128]{3,2,1,0:T(8,128)S(1)} collective-permute-done((f32[2,2,256,128]{3,2,1,0:T(8,128)S(1)}, f32[2,2,256,128]{3,2,1,0:T(8,128)S(1)}, u32[]{:S(2)}, u32[]{:S(2)}) %collective-permute-start.6) | collective-permute-done | bytes 524320 | tf_op jit(solution)/shard_map/ppermute | solution.py:204
  60.6 1.9 %collective-permute-done.7.near = f32[2,2,256,128]{3,2,1,0:T(8,128)S(1)} collective-permute-done((f32[2,2,256,128]{3,2,1,0:T(8,128)S(1)}, f32[2,2,256,128]{3,2,1,0:T(8,128)S(1)}, u32[]{:S(2)}, u32[]{:S(2)}) %collective-permute-start.7) | collective-permute-done | bytes 524320 | tf_op jit(solution)/shard_map/ppermute | solution.py:204
  62.5 1.6 %collective-permute-start.8 = (f32[2,2,256,128]{3,2,1,0:T(8,128)S(1)}, f32[2,2,256,128]{3,2,1,0:T(8,128)S(1)}, u32[]{:S(2)}, u32[]{:S(2)}) collective-permute-start(f32[2,2,256,128]{3,2,1,0:T(8,128)S(1)} %shard_map.34.near), channel_id=1, source_target_pairs={{0,2},{1,5},{2,0},{3,7},{4,6},{5,1},{6,4},{7,3},{8,10},{9,13},{10,... | collective-permute-start | bytes 1572872 | tf_op jit(solution)/shard_map/ppermute | solution.py:204
  64.1 13.2 %collective-permute-done.8.far = f32[2,2,256,128]{3,2,1,0:T(8,128)S(1)} collective-permute-done((f32[2,2,256,128]{3,2,1,0:T(8,128)S(1)}, f32[2,2,256,128]{3,2,1,0:T(8,128)S(1)}, u32[]{:S(2)}, u32[]{:S(2)}) %collective-permute-start.8) | collective-permute-done | bytes 524320 | tf_op jit(solution)/shard_map/ppermute | solution.py:204
  77.3 1.8 %shard_map.37.kept = f32[2,256,896]{2,1,0:T(8,128)S(1)} custom-call(f32[2,2,256,128]{3,2,1,0:T(8,128)S(1)} %shard_map.34.near, f32[2,2,256,128]{3,2,1,0:T(8,128)S(1)} %collective-permute-done.8.far, f32[2,896,256]{2,1,0:T(8,128)S(1)} %get-tuple-element.32.refs_0_, f32[2,896,256]{2,1,0:T(8,128)S(1)} %collective-permute-done.15.refs_1_), custom_call_target="tpu_custom_call" | custom-call | flops 1409286144 | bytes 6553600 | tf_op jit(solution)/shard_map/pallas_call | solution.py:52
  79.2 1.8 %shard_map.35.kept = f32[2,256,896]{2,1,0:T(8,128)S(1)} custom-call(f32[2,2,256,128]{3,2,1,0:T(8,128)S(1)} %collective-permute-done.7.near, f32[2,2,256,128]{3,2,1,0:T(8,128)S(1)} %collective-permute-done.9.far, f32[2,512,256]{2,1,0:T(8,128)S(1)} %get-tuple-element.30.refs_0_, f32[2,512,256]{2,1,0:T(8,128)S(1)} %collective-permute-done.10.refs_1_, ...), custom_call_target="tpu_custom_call" | custom-call | flops 1409286144 | bytes 6553600 | tf_op jit(solution)/shard_map/pallas_call | solution.py:52
  81.1 8.2 %collective-permute-done.16.came = f32[2,256,896]{2,1,0:T(8,128)S(1)} collective-permute-done((f32[2,256,896]{2,1,0:T(8,128)S(1)}, f32[2,256,896]{2,1,0:T(8,128)S(1)}, u32[]{:S(2)}, u32[]{:S(2)}) %collective-permute-start.16) | collective-permute-done | bytes 1835040 | tf_op jit(solution)/shard_map/ppermute | solution.py:204
  89.3 1.3 %shard_map.39.refs_0_ = f32[4,256,896]{2,1,0:T(8,128)} custom-call(f32[2,256,896]{2,1,0:T(8,128)S(1)} %shard_map.37.kept, f32[2,256,896]{2,1,0:T(8,128)S(1)} %collective-permute-done.16.came), custom_call_target="tpu_custom_call" | custom-call | flops 917504 | bytes 7340032 | tf_op jit(solution)/shard_map/pallas_call | solution.py:52
  90.6 2.9 %collective-permute-done.14.came = f32[2,256,896]{2,1,0:T(8,128)S(1)} collective-permute-done((f32[2,256,896]{2,1,0:T(8,128)S(1)}, f32[2,256,896]{2,1,0:T(8,128)S(1)}, u32[]{:S(2)}, u32[]{:S(2)}) %collective-permute-start.14) | collective-permute-done | bytes 1835040 | tf_op jit(solution)/shard_map/ppermute | solution.py:204
  93.5 1.3 %shard_map.40 = f32[4,256,896]{2,1,0:T(8,128)} custom-call(f32[2,256,896]{2,1,0:T(8,128)S(1)} %shard_map.35.kept, f32[2,256,896]{2,1,0:T(8,128)S(1)} %collective-permute-done.14.came, f32[4,256,896]{2,1,0:T(8,128)} %shard_map.39.refs_0_), custom_call_target="tpu_custom_call", output_to_operand_aliasing={{}: (2, {})} | custom-call | flops 917504 | bytes 11010048 | tf_op jit(solution)/shard_map/pallas_call | solution.py:52
  (19 shorter events, 0.5 us)
Async XLA Ops:
  0.0 1.0 %copy-start.1 = (f32[4,256,128]{2,1,0:T(8,128)S(1)}, f32[4,256,128]{2,1,0:T(8,128)}, u32[]{:S(2)}) copy-start(f32[4,256,128]{2,1,0:T(8,128)} %whole.2) | copy-start | bytes 1572868
  1.1 9.2 %collective-permute-start = (f32[2,256,128]{2,1,0:T(8,128)S(1)}, f32[2,256,128]{2,1,0:T(8,128)S(1)}, u32[]{:S(2)}, u32[]{:S(2)}) collective-permute-start(f32[2,256,128]{2,1,0:T(8,128)S(1)} %get-tuple-element.19.first), channel_id=1, source_target_pairs={{0,16},{1,9},{2,18},{3,11},{4,20},{5,13},{6,22},{7,15},{8,24},{9,1... | collective-permute-start | bytes 786440 | tf_op jit(solution)/shard_map/ppermute | solution.py:204
  4.1 7.2 %collective-permute-start.1 = (f32[2,256,128]{2,1,0:T(8,128)S(1)}, f32[2,256,128]{2,1,0:T(8,128)S(1)}, u32[]{:S(2)}, u32[]{:S(2)}) collective-permute-start(f32[2,256,128]{2,1,0:T(8,128)S(1)} %get-tuple-element.27), channel_id=1, source_target_pairs={{0,9},{1,16},{2,11},{3,18},{4,13},{5,20},{6,15},{7,22},{8,1},{9,24... | collective-permute-start | bytes 786440 | tf_op jit(solution)/shard_map/ppermute | solution.py:204
  4.1 2.0 %copy-start = (f32[4,896,256]{2,1,0:T(8,128)S(1)}, f32[4,896,256]{2,1,0:T(8,128)}, u32[]{:S(2)}) copy-start(f32[4,896,256]{2,1,0:T(8,128)} %whole.3) | copy-start | bytes 11010052
  11.3 34.0 %collective-permute-start.15 = (f32[2,896,256]{2,1,0:T(8,128)S(1)}, f32[2,896,256]{2,1,0:T(8,128)S(1)}, u32[]{:S(2)}, u32[]{:S(2)}) collective-permute-start(f32[2,896,256]{2,1,0:T(8,128)S(1)} %get-tuple-element.32.refs_0_), channel_id=1, source_target_pairs={{0,8},{1,17},{2,10},{3,19},{4,12},{5,21},{6,14},{7,23},{8,0},{9,25... | collective-permute-start | bytes 5505032 | tf_op jit(solution)/shard_map/ppermute | solution.py:204
  13.3 15.8 %collective-permute-start.2 = (f32[2,2,256,128]{3,2,1,0:T(8,128)S(1)}, f32[2,2,256,128]{3,2,1,0:T(8,128)S(1)}, u32[]{:S(2)}, u32[]{:S(2)}) collective-permute-start(f32[2,2,256,128]{3,2,1,0:T(8,128)S(1)} %shard_map.30.held), channel_id=1, source_target_pairs={{0,4},{1,3},{2,6},{3,1},{4,0},{5,7},{6,2},{7,5},{8,12},{9,11},{10,... | collective-permute-start | bytes 1572872 | tf_op jit(solution)/shard_map/ppermute | solution.py:204
  29.2 1.2 %collective-permute-start.3 = (f32[8,128]{1,0:T(8,128)S(1)}, f32[8,128]{1,0:T(8,128)S(1)}, u32[]{:S(2)}, u32[]{:S(2)}) collective-permute-start(f32[8,128]{1,0:T(8,128)S(1)} %get-tuple-element.26), channel_id=1, source_target_pairs={{0,1},{1,0},{2,3},{3,2},{4,5},{5,4},{6,7},{7,6},{8,9},{9,8},{10,11... | collective-permute-start | bytes 12296 | tf_op jit(solution)/shard_map/ppermute | solution.py:204
  30.5 14.8 %collective-permute-start.5 = (f32[2,2,256,128]{3,2,1,0:T(8,128)S(1)}, f32[2,2,256,128]{3,2,1,0:T(8,128)S(1)}, u32[]{:S(2)}, u32[]{:S(2)}) collective-permute-start(f32[2,2,256,128]{3,2,1,0:T(8,128)S(1)} %shard_map.32.near), channel_id=1, source_target_pairs={{0,2},{1,5},{2,0},{3,7},{4,6},{5,1},{6,4},{7,3},{8,10},{9,13},{10,... | collective-permute-start | bytes 1572872 | tf_op jit(solution)/shard_map/ppermute | solution.py:204
  31.2 23.2 %collective-permute-start.10 = (f32[2,512,256]{2,1,0:T(8,128)S(1)}, f32[2,512,256]{2,1,0:T(8,128)S(1)}, u32[]{:S(2)}, u32[]{:S(2)}) collective-permute-start(f32[2,512,256]{2,1,0:T(8,128)S(1)} %get-tuple-element.30.refs_0_), channel_id=1, source_target_pairs={{0,16},{1,9},{2,18},{3,11},{4,20},{5,13},{6,22},{7,15},{8,24},{9,1... | collective-permute-start | bytes 3145736 | tf_op jit(solution)/shard_map/ppermute | solution.py:204
  32.6 1.5 %collective-permute-start.4 = (f32[2,256,128]{2,1,0:T(8,128)S(1)}, f32[2,256,128]{2,1,0:T(8,128)S(1)}, u32[]{:S(2)}, u32[]{:S(2)}) collective-permute-start(f32[2,256,128]{2,1,0:T(8,128)S(1)} %get-tuple-element.27), channel_id=1, source_target_pairs={{0,1},{1,0},{2,3},{3,2},{4,5},{5,4},{6,7},{7,6},{8,9},{9,8},{10,11... | collective-permute-start | bytes 786440 | tf_op jit(solution)/shard_map/ppermute | solution.py:204
  32.6 21.8 %collective-permute-start.11 = (f32[2,384,256]{2,1,0:T(8,128)S(1)}, f32[2,384,256]{2,1,0:T(8,128)S(1)}, u32[]{:S(2)}, u32[]{:S(2)}) collective-permute-start(f32[2,384,256]{2,1,0:T(8,128)S(1)} %get-tuple-element.31.refs_2_), channel_id=1, source_target_pairs={{0,16},{1,9},{2,18},{3,11},{4,20},{5,13},{6,22},{7,15},{8,24},{9,1... | collective-permute-start | bytes 2359304 | tf_op jit(solution)/shard_map/ppermute | solution.py:204
  34.2 14.7 %collective-permute-start.12 = (f32[2,2,256,128]{3,2,1,0:T(8,128)S(1)}, f32[2,2,256,128]{3,2,1,0:T(8,128)S(1)}, u32[]{:S(2)}, u32[]{:S(2)}) collective-permute-start(f32[2,2,256,128]{3,2,1,0:T(8,128)S(1)} %shard_map.32.near), channel_id=1, source_target_pairs={{0,1},{1,0},{2,3},{3,2},{4,5},{5,4},{6,7},{7,6},{8,9},{9,8},{10,11... | collective-permute-start | bytes 1572872 | tf_op jit(solution)/shard_map/ppermute | solution.py:204
  45.3 9.1 %collective-permute-start.13 = (f32[2,2,256,128]{3,2,1,0:T(8,128)S(1)}, f32[2,2,256,128]{3,2,1,0:T(8,128)S(1)}, u32[]{:S(2)}, u32[]{:S(2)}) collective-permute-start(f32[2,2,256,128]{3,2,1,0:T(8,128)S(1)} %collective-permute-done.5.far), channel_id=1, source_target_pairs={{0,1},{1,0},{2,3},{3,2},{4,5},{5,4},{6,7},{7,6},{8,9},{9,8},{10,11... | collective-permute-start | bytes 1572872 | tf_op jit(solution)/shard_map/ppermute | solution.py:204
  45.3 15.1 %collective-permute-start.6 = (f32[2,2,256,128]{3,2,1,0:T(8,128)S(1)}, f32[2,2,256,128]{3,2,1,0:T(8,128)S(1)}, u32[]{:S(2)}, u32[]{:S(2)}) collective-permute-start(f32[2,2,256,128]{3,2,1,0:T(8,128)S(1)} %shard_map.33.held), channel_id=1, source_target_pairs={{0,4},{1,3},{2,6},{3,1},{4,0},{5,7},{6,2},{7,5},{8,12},{9,11},{10,... | collective-permute-start | bytes 1572872 | tf_op jit(solution)/shard_map/ppermute | solution.py:204
  48.9 40.4 %collective-permute-start.16 = (f32[2,256,896]{2,1,0:T(8,128)S(1)}, f32[2,256,896]{2,1,0:T(8,128)S(1)}, u32[]{:S(2)}, u32[]{:S(2)}) collective-permute-start(f32[2,256,896]{2,1,0:T(8,128)S(1)} %shard_map.38), channel_id=1, source_target_pairs={{0,16},{1,9},{2,18},{3,11},{4,20},{5,13},{6,22},{7,15},{8,24},{9,1... | collective-permute-start | bytes 5505032 | tf_op jit(solution)/shard_map/ppermute | solution.py:204
  56.2 37.3 %collective-permute-start.14 = (f32[2,256,896]{2,1,0:T(8,128)S(1)}, f32[2,256,896]{2,1,0:T(8,128)S(1)}, u32[]{:S(2)}, u32[]{:S(2)}) collective-permute-start(f32[2,256,896]{2,1,0:T(8,128)S(1)} %shard_map.36), channel_id=1, source_target_pairs={{0,8},{1,17},{2,10},{3,19},{4,12},{5,21},{6,14},{7,23},{8,0},{9,25... | collective-permute-start | bytes 5505032 | tf_op jit(solution)/shard_map/ppermute | solution.py:204
  60.5 2.0 %collective-permute-start.7 = (f32[2,2,256,128]{3,2,1,0:T(8,128)S(1)}, f32[2,2,256,128]{3,2,1,0:T(8,128)S(1)}, u32[]{:S(2)}, u32[]{:S(2)}) collective-permute-start(f32[2,2,256,128]{3,2,1,0:T(8,128)S(1)} %shard_map.34.near), channel_id=1, source_target_pairs={{0,1},{1,0},{2,3},{3,2},{4,5},{5,4},{6,7},{7,6},{8,9},{9,8},{10,11... | collective-permute-start | bytes 1572872 | tf_op jit(solution)/shard_map/ppermute | solution.py:204
  62.5 14.8 %collective-permute-start.8 = (f32[2,2,256,128]{3,2,1,0:T(8,128)S(1)}, f32[2,2,256,128]{3,2,1,0:T(8,128)S(1)}, u32[]{:S(2)}, u32[]{:S(2)}) collective-permute-start(f32[2,2,256,128]{3,2,1,0:T(8,128)S(1)} %shard_map.34.near), channel_id=1, source_target_pairs={{0,2},{1,5},{2,0},{3,7},{4,6},{5,1},{6,4},{7,3},{8,10},{9,13},{10,... | collective-permute-start | bytes 1572872 | tf_op jit(solution)/shard_map/ppermute | solution.py:204
  77.3 1.9 %collective-permute-start.9 = (f32[2,2,256,128]{3,2,1,0:T(8,128)S(1)}, f32[2,2,256,128]{3,2,1,0:T(8,128)S(1)}, u32[]{:S(2)}, u32[]{:S(2)}) collective-permute-start(f32[2,2,256,128]{3,2,1,0:T(8,128)S(1)} %collective-permute-done.8.far), channel_id=1, source_target_pairs={{0,1},{1,0},{2,3},{3,2},{4,5},{5,4},{6,7},{7,6},{8,9},{9,8},{10,11... | collective-permute-start | bytes 1572872 | tf_op jit(solution)/shard_map/ppermute | solution.py:204

commit v4 on v3

--- a/solution.py
+++ b/solution.py
@@ -9,7 +9,6 @@
 
 MESH = {"occ": 4, "vir": 8}
 STEP = 256
-CUTS = (), (512,)
 
 
 def contract_block(left, piece):
@@ -220,9 +219,10 @@
 def hybrid_body(amplitudes, integrals):
     (mine,), (give,) = kinds(amplitudes, (), ())
     same, cross = permute(mine, SAME_CORE), permute(give, CROSS_CORE)
-    own = kinds(integrals, *CUTS)
+    n_ab = integrals.shape[1]
+    own = kinds(integrals, (n_ab * 25 // 28,), (n_ab * 9 // 14,))
     send = spread(merge(tie(same, *own[0], *own[1]), cross), True)
-    own[0] = [tie(a, same, cross) for a in own[0]]
+
     own[1] = [tie(a, send[0][0]) for a in own[1]]
     got = [[permute(a, perm) for a in pieces] for pieces, perm in zip(own, (FIRST_KIND, SECOND_KIND))]
     came = []

time: 95 us -> 94.2 us (level)
  waiting for transfers between devices: 65 us -> 59.8 us
  Pallas kernels: 10.6 us -> 12.8 us
  starting transfers between devices: 16.1 us -> 18.1 us
    ppermute x17 -> x18, waiting for transfers between devices: 65 us -> 59.8 us  [permute(): return lax.ppermute(a, BOTH, perm)]
    pallas_call x13, Pallas kernels: 10.6 us -> 12.8 us  [call(): pl.pallas_call(kernel, out_shape=out_shape, in_specs=in_specs, out_specs=...]
    ppermute x17 -> x18, starting transfers between devices: 16.1 us -> 18.1 us  [permute(): return lax.ppermute(a, BOTH, perm)]
  transfers between devices with their start and end apart: 17 -> 18, of which waited for: 13 -> 12; matrix products, arithmetic and copies ran while one was open for 0% -> 0% of each run, Pallas kernels for 10% -> 12%
where the time goes in v4:
time: 94.2 us; the launch traced here: 93.9 us
  waiting for transfers between devices  59.8 us (63%)
  starting transfers between devices  18.1 us (19%)
  Pallas kernels  12.8 us (14%)
  local copies, waits for them, and re-layouts  3.08 us (3%)
    ppermute x18, waiting for transfers between devices, permute(): return lax.ppermute(a, BOTH, perm)  59.8 us
    ppermute x18, starting transfers between devices, permute(): return lax.ppermute(a, BOTH, perm)  18.1 us
    pallas_call x13, Pallas kernels, call(): pl.pallas_call(kernel, out_shape=out_shape, in_specs=in_specs, out_specs=...  12.8 us
    unnamed x4, local copies, waits for them, and re-layouts  3.08 us
  transfers between devices with their start and end apart: 18, of which 12 were waited for; matrix products, arithmetic and copies ran while one was open for 0% of the time, Pallas kernels for 12%

profile of v4, /device:TPU:0, one launch (start us, length us, event | category | flops | bytes accessed | tf_op | source)
XLA Modules:
  0.0 93.9 jit_solution(7857770974679918621)
XLA Ops:
  0.0 1.0 %copy-done.1 = f32[4,256,128]{2,1,0:T(8,128)S(1)} copy-done((f32[4,256,128]{2,1,0:T(8,128)S(1)}, f32[4,256,128]{2,1,0:T(8,128)}, u32[]{:S(2)}) %copy-start.1) | copy-done | bytes 524312
  1.1 3.0 %collective-permute-start = (f32[2,256,128]{2,1,0:T(8,128)S(1)}, f32[2,256,128]{2,1,0:T(8,128)S(1)}, u32[]{:S(2)}, u32[]{:S(2)}) collective-permute-start(f32[2,256,128]{2,1,0:T(8,128)S(1)} %get-tuple-element.19.first), channel_id=1, source_target_pairs={{0,16},{1,9},{2,18},{3,11},{4,20},{5,13},{6,22},{7,15},{8,24},{9,1... | collective-permute-start | bytes 786440 | tf_op jit(solution)/shard_map/ppermute | solution.py:203
  4.1 2.0 %copy-done = f32[4,896,256]{2,1,0:T(8,128)S(1)} copy-done((f32[4,896,256]{2,1,0:T(8,128)S(1)}, f32[4,896,256]{2,1,0:T(8,128)}, u32[]{:S(2)}) %copy-start) | copy-done | bytes 3670040
  6.2 0.6 shard_map.29
  6.8 1.6 %collective-permute-start.15 = (f32[2,800,256]{2,1,0:T(8,128)S(1)}, f32[2,800,256]{2,1,0:T(8,128)S(1)}, u32[]{:S(2)}, u32[]{:S(2)}) collective-permute-start(f32[2,800,256]{2,1,0:T(8,128)S(1)} %get-tuple-element.21.refs_0_), channel_id=1, source_target_pairs={{0,8},{1,17},{2,10},{3,19},{4,12},{5,21},{6,14},{7,23},{8,0},{9,25... | collective-permute-start | bytes 4915208 | tf_op jit(solution)/shard_map/ppermute | solution.py:203
  8.3 2.4 %collective-permute-done.first = f32[2,256,128]{2,1,0:T(8,128)S(1)} collective-permute-done((f32[2,256,128]{2,1,0:T(8,128)S(1)}, f32[2,256,128]{2,1,0:T(8,128)S(1)}, u32[]{:S(2)}, u32[]{:S(2)}) %collective-permute-start) | collective-permute-done | bytes 262176 | tf_op jit(solution)/shard_map/ppermute | solution.py:203
  10.8 0.5 collective-permute-done.1.second
  11.3 3.2 %collective-permute-start.2 = (f32[2,2,256,128]{3,2,1,0:T(8,128)S(1)}, f32[2,2,256,128]{3,2,1,0:T(8,128)S(1)}, u32[]{:S(2)}, u32[]{:S(2)}) collective-permute-start(f32[2,2,256,128]{3,2,1,0:T(8,128)S(1)} %shard_map.30.held), channel_id=1, source_target_pairs={{0,4},{1,3},{2,6},{3,1},{4,0},{5,7},{6,2},{7,5},{8,12},{9,11},{10,... | collective-permute-start | bytes 1572872 | tf_op jit(solution)/shard_map/ppermute | solution.py:203
  14.5 12.8 %collective-permute-done.2.got = f32[2,2,256,128]{3,2,1,0:T(8,128)S(1)} collective-permute-done((f32[2,2,256,128]{3,2,1,0:T(8,128)S(1)}, f32[2,2,256,128]{3,2,1,0:T(8,128)S(1)}, u32[]{:S(2)}, u32[]{:S(2)}) %collective-permute-start.2) | collective-permute-done | bytes 524320 | tf_op jit(solution)/shard_map/ppermute | solution.py:203
  27.5 1.2 %collective-permute-done.3.small = f32[8,128]{1,0:T(8,128)S(1)} collective-permute-done((f32[8,128]{1,0:T(8,128)S(1)}, f32[8,128]{1,0:T(8,128)S(1)}, u32[]{:S(2)}, u32[]{:S(2)}) %collective-permute-start.3) | collective-permute-done | bytes 4128 | tf_op jit(solution)/shard_map/ppermute | solution.py:203
  28.6 1.8 %collective-permute-start.10 = (f32[2,576,256]{2,1,0:T(8,128)S(1)}, f32[2,576,256]{2,1,0:T(8,128)S(1)}, u32[]{:S(2)}, u32[]{:S(2)}) collective-permute-start(f32[2,576,256]{2,1,0:T(8,128)S(1)} %get-tuple-element.31.refs_0_), channel_id=1, source_target_pairs={{0,16},{1,9},{2,18},{3,11},{4,20},{5,13},{6,22},{7,15},{8,24},{9,1... | collective-permute-start | bytes 3538952 | tf_op jit(solution)/shard_map/ppermute | solution.py:203
  30.4 0.8 collective-permute-start.5
  31.2 1.5 %collective-permute-start.16 = (f32[2,96,256]{2,1,0:T(8,128)S(1)}, f32[2,96,256]{2,1,0:T(8,128)S(1)}, u32[]{:S(2)}, u32[]{:S(2)}) collective-permute-start(f32[2,96,256]{2,1,0:T(8,128)S(1)} %get-tuple-element.22.refs_2_), channel_id=1, source_target_pairs={{0,8},{1,17},{2,10},{3,19},{4,12},{5,21},{6,14},{7,23},{8,0},{9,25... | collective-permute-start | bytes 589832 | tf_op jit(solution)/shard_map/ppermute | solution.py:203
  32.7 6.3 %collective-permute-done.16.refs_3_ = f32[2,96,256]{2,1,0:T(8,128)S(1)} collective-permute-done((f32[2,96,256]{2,1,0:T(8,128)S(1)}, f32[2,96,256]{2,1,0:T(8,128)S(1)}, u32[]{:S(2)}, u32[]{:S(2)}) %collective-permute-start.16) | collective-permute-done | bytes 196640 | tf_op jit(solution)/shard_map/ppermute | solution.py:203
  39.0 0.5 collective-permute-start.11
  39.6 5.5 %collective-permute-done.5.far = f32[2,2,256,128]{3,2,1,0:T(8,128)S(1)} collective-permute-done((f32[2,2,256,128]{3,2,1,0:T(8,128)S(1)}, f32[2,2,256,128]{3,2,1,0:T(8,128)S(1)}, u32[]{:S(2)}, u32[]{:S(2)}) %collective-permute-start.5) | collective-permute-done | bytes 524320 | tf_op jit(solution)/shard_map/ppermute | solution.py:203
  45.1 1.8 %collective-permute-start.6 = (f32[2,2,256,128]{3,2,1,0:T(8,128)S(1)}, f32[2,2,256,128]{3,2,1,0:T(8,128)S(1)}, u32[]{:S(2)}, u32[]{:S(2)}) collective-permute-start(f32[2,2,256,128]{3,2,1,0:T(8,128)S(1)} %shard_map.33.held), channel_id=1, source_target_pairs={{0,4},{1,3},{2,6},{3,1},{4,0},{5,7},{6,2},{7,5},{8,12},{9,11},{10,... | collective-permute-start | bytes 1572872 | tf_op jit(solution)/shard_map/ppermute | solution.py:203
  46.9 2.3 %shard_map.38 = f32[2,256,896]{2,1,0:T(8,128)S(1)} custom-call(f32[2,2,256,128]{3,2,1,0:T(8,128)S(1)} %shard_map.32.near, f32[2,2,256,128]{3,2,1,0:T(8,128)S(1)} %collective-permute-done.5.far, f32[2,800,256]{2,1,0:T(8,128)S(1)} %get-tuple-element.21.refs_0_, f32[2,800,256]{2,1,0:T(8,128)S(1)} %collective-permute-done.15.refs_1_, ...), custom_call_target="tpu_custom_call" | custom-call | flops 1409286144 | bytes 6553600 | tf_op jit(solution)/shard_map/pallas_call | solution.py:51
  49.2 1.0 %collective-permute-start.17 = (f32[2,256,896]{2,1,0:T(8,128)S(1)}, f32[2,256,896]{2,1,0:T(8,128)S(1)}, u32[]{:S(2)}, u32[]{:S(2)}) collective-permute-start(f32[2,256,896]{2,1,0:T(8,128)S(1)} %shard_map.38), channel_id=1, source_target_pairs={{0,16},{1,9},{2,18},{3,11},{4,20},{5,13},{6,22},{7,15},{8,24},{9,1... | collective-permute-start | bytes 5505032 | tf_op jit(solution)/shard_map/ppermute | solution.py:203
  50.2 3.8 %collective-permute-done.11.refs_3_ = f32[2,320,256]{2,1,0:T(8,128)S(1)} collective-permute-done((f32[2,320,256]{2,1,0:T(8,128)S(1)}, f32[2,320,256]{2,1,0:T(8,128)S(1)}, u32[]{:S(2)}, u32[]{:S(2)}) %collective-permute-start.11) | collective-permute-done | bytes 655392 | tf_op jit(solution)/shard_map/ppermute | solution.py:203
  54.0 2.3 %shard_map.36 = f32[2,256,896]{2,1,0:T(8,128)S(1)} custom-call(f32[2,2,256,128]{3,2,1,0:T(8,128)S(1)} %collective-permute-done.12.near, f32[2,2,256,128]{3,2,1,0:T(8,128)S(1)} %collective-permute-done.13.far, f32[2,576,256]{2,1,0:T(8,128)S(1)} %get-tuple-element.31.refs_0_, f32[2,576,256]{2,1,0:T(8,128)S(1)} %collective-permute-done.10.refs_1_, ...), custom_call_target="tpu_custom_call" | custom-call | flops 1409286144 | bytes 6553600 | tf_op jit(solution)/shard_map/pallas_call | solution.py:51
  56.3 1.1 %collective-permute-start.14 = (f32[2,256,896]{2,1,0:T(8,128)S(1)}, f32[2,256,896]{2,1,0:T(8,128)S(1)}, u32[]{:S(2)}, u32[]{:S(2)}) collective-permute-start(f32[2,256,896]{2,1,0:T(8,128)S(1)} %shard_map.36), channel_id=1, source_target_pairs={{0,8},{1,17},{2,10},{3,19},{4,12},{5,21},{6,14},{7,23},{8,0},{9,25... | collective-permute-start | bytes 5505032 | tf_op jit(solution)/shard_map/ppermute | solution.py:203
  57.4 2.8 %collective-permute-done.6.got = f32[2,2,256,128]{3,2,1,0:T(8,128)S(1)} collective-permute-done((f32[2,2,256,128]{3,2,1,0:T(8,128)S(1)}, f32[2,2,256,128]{3,2,1,0:T(8,128)S(1)}, u32[]{:S(2)}, u32[]{:S(2)}) %collective-permute-start.6) | collective-permute-done | bytes 524320 | tf_op jit(solution)/shard_map/ppermute | solution.py:203
  60.3 1.9 %collective-permute-done.7.near = f32[2,2,256,128]{3,2,1,0:T(8,128)S(1)} collective-permute-done((f32[2,2,256,128]{3,2,1,0:T(8,128)S(1)}, f32[2,2,256,128]{3,2,1,0:T(8,128)S(1)}, u32[]{:S(2)}, u32[]{:S(2)}) %collective-permute-start.7) | collective-permute-done | bytes 524320 | tf_op jit(solution)/shard_map/ppermute | solution.py:203
  62.2 1.8 %collective-permute-start.8 = (f32[2,2,256,128]{3,2,1,0:T(8,128)S(1)}, f32[2,2,256,128]{3,2,1,0:T(8,128)S(1)}, u32[]{:S(2)}, u32[]{:S(2)}) collective-permute-start(f32[2,2,256,128]{3,2,1,0:T(8,128)S(1)} %shard_map.34.near), channel_id=1, source_target_pairs={{0,2},{1,5},{2,0},{3,7},{4,6},{5,1},{6,4},{7,3},{8,10},{9,13},{10,... | collective-permute-start | bytes 1572872 | tf_op jit(solution)/shard_map/ppermute | solution.py:203
  64.1 13.0 %collective-permute-done.8.far = f32[2,2,256,128]{3,2,1,0:T(8,128)S(1)} collective-permute-done((f32[2,2,256,128]{3,2,1,0:T(8,128)S(1)}, f32[2,2,256,128]{3,2,1,0:T(8,128)S(1)}, u32[]{:S(2)}, u32[]{:S(2)}) %collective-permute-start.8) | collective-permute-done | bytes 524320 | tf_op jit(solution)/shard_map/ppermute | solution.py:203
  77.0 2.3 %shard_map.37.kept = f32[2,256,896]{2,1,0:T(8,128)S(1)} custom-call(f32[2,2,256,128]{3,2,1,0:T(8,128)S(1)} %shard_map.34.near, f32[2,2,256,128]{3,2,1,0:T(8,128)S(1)} %collective-permute-done.8.far, f32[2,800,256]{2,1,0:T(8,128)S(1)} %get-tuple-element.21.refs_0_, f32[2,800,256]{2,1,0:T(8,128)S(1)} %collective-permute-done.15.refs_1_, ...), custom_call_target="tpu_custom_call" | custom-call | flops 1409286144 | bytes 6553600 | tf_op jit(solution)/shard_map/pallas_call | solution.py:51
  79.4 2.3 %shard_map.35.kept = f32[2,256,896]{2,1,0:T(8,128)S(1)} custom-call(f32[2,2,256,128]{3,2,1,0:T(8,128)S(1)} %collective-permute-done.7.near, f32[2,2,256,128]{3,2,1,0:T(8,128)S(1)} %collective-permute-done.9.far, f32[2,576,256]{2,1,0:T(8,128)S(1)} %get-tuple-element.31.refs_0_, f32[2,576,256]{2,1,0:T(8,128)S(1)} %collective-permute-done.10.refs_1_, ...), custom_call_target="tpu_custom_call" | custom-call | flops 1409286144 | bytes 6553600 | tf_op jit(solution)/shard_map/pallas_call | solution.py:51
  81.7 7.1 %collective-permute-done.17.came = f32[2,256,896]{2,1,0:T(8,128)S(1)} collective-permute-done((f32[2,256,896]{2,1,0:T(8,128)S(1)}, f32[2,256,896]{2,1,0:T(8,128)S(1)}, u32[]{:S(2)}, u32[]{:S(2)}) %collective-permute-start.17) | collective-permute-done | bytes 1835040 | tf_op jit(solution)/shard_map/ppermute | solution.py:203
  88.8 1.3 %shard_map.39.refs_0_ = f32[4,256,896]{2,1,0:T(8,128)} custom-call(f32[2,256,896]{2,1,0:T(8,128)S(1)} %shard_map.37.kept, f32[2,256,896]{2,1,0:T(8,128)S(1)} %collective-permute-done.17.came), custom_call_target="tpu_custom_call" | custom-call | flops 917504 | bytes 7340032 | tf_op jit(solution)/shard_map/pallas_call | solution.py:51
  90.2 2.4 %collective-permute-done.14.came = f32[2,256,896]{2,1,0:T(8,128)S(1)} collective-permute-done((f32[2,256,896]{2,1,0:T(8,128)S(1)}, f32[2,256,896]{2,1,0:T(8,128)S(1)}, u32[]{:S(2)}, u32[]{:S(2)}) %collective-permute-start.14) | collective-permute-done | bytes 1835040 | tf_op jit(solution)/shard_map/ppermute | solution.py:203
  92.6 1.3 %shard_map.40 = f32[4,256,896]{2,1,0:T(8,128)} custom-call(f32[2,256,896]{2,1,0:T(8,128)S(1)} %shard_map.35.kept, f32[2,256,896]{2,1,0:T(8,128)S(1)} %collective-permute-done.14.came, f32[4,256,896]{2,1,0:T(8,128)} %shard_map.39.refs_0_), custom_call_target="tpu_custom_call", output_to_operand_aliasing={{}: (2, {})} | custom-call | flops 917504 | bytes 11010048 | tf_op jit(solution)/shard_map/pallas_call | solution.py:51
  (21 shorter events, 0.5 us)
Async XLA Ops:
  0.0 1.0 %copy-start.1 = (f32[4,256,128]{2,1,0:T(8,128)S(1)}, f32[4,256,128]{2,1,0:T(8,128)}, u32[]{:S(2)}) copy-start(f32[4,256,128]{2,1,0:T(8,128)} %whole.2) | copy-start | bytes 1572868
  1.1 9.7 %collective-permute-start = (f32[2,256,128]{2,1,0:T(8,128)S(1)}, f32[2,256,128]{2,1,0:T(8,128)S(1)}, u32[]{:S(2)}, u32[]{:S(2)}) collective-permute-start(f32[2,256,128]{2,1,0:T(8,128)S(1)} %get-tuple-element.19.first), channel_id=1, source_target_pairs={{0,16},{1,9},{2,18},{3,11},{4,20},{5,13},{6,22},{7,15},{8,24},{9,1... | collective-permute-start | bytes 786440 | tf_op jit(solution)/shard_map/ppermute | solution.py:203
  4.1 7.2 %collective-permute-start.1 = (f32[2,256,128]{2,1,0:T(8,128)S(1)}, f32[2,256,128]{2,1,0:T(8,128)S(1)}, u32[]{:S(2)}, u32[]{:S(2)}) collective-permute-start(f32[2,256,128]{2,1,0:T(8,128)S(1)} %get-tuple-element.28), channel_id=1, source_target_pairs={{0,9},{1,16},{2,11},{3,18},{4,13},{5,20},{6,15},{7,22},{8,1},{9,24... | collective-permute-start | bytes 786440 | tf_op jit(solution)/shard_map/ppermute | solution.py:203
  4.1 2.0 %copy-start = (f32[4,896,256]{2,1,0:T(8,128)S(1)}, f32[4,896,256]{2,1,0:T(8,128)}, u32[]{:S(2)}) copy-start(f32[4,896,256]{2,1,0:T(8,128)} %whole.3) | copy-start | bytes 11010052
  6.8 38.4 %collective-permute-start.15 = (f32[2,800,256]{2,1,0:T(8,128)S(1)}, f32[2,800,256]{2,1,0:T(8,128)S(1)}, u32[]{:S(2)}, u32[]{:S(2)}) collective-permute-start(f32[2,800,256]{2,1,0:T(8,128)S(1)} %get-tuple-element.21.refs_0_), channel_id=1, source_target_pairs={{0,8},{1,17},{2,10},{3,19},{4,12},{5,21},{6,14},{7,23},{8,0},{9,25... | collective-permute-start | bytes 4915208 | tf_op jit(solution)/shard_map/ppermute | solution.py:203
  11.3 16.0 %collective-permute-start.2 = (f32[2,2,256,128]{3,2,1,0:T(8,128)S(1)}, f32[2,2,256,128]{3,2,1,0:T(8,128)S(1)}, u32[]{:S(2)}, u32[]{:S(2)}) collective-permute-start(f32[2,2,256,128]{3,2,1,0:T(8,128)S(1)} %shard_map.30.held), channel_id=1, source_target_pairs={{0,4},{1,3},{2,6},{3,1},{4,0},{5,7},{6,2},{7,5},{8,12},{9,11},{10,... | collective-permute-start | bytes 1572872 | tf_op jit(solution)/shard_map/ppermute | solution.py:203
  27.4 1.2 %collective-permute-start.3 = (f32[8,128]{1,0:T(8,128)S(1)}, f32[8,128]{1,0:T(8,128)S(1)}, u32[]{:S(2)}, u32[]{:S(2)}) collective-permute-start(f32[8,128]{1,0:T(8,128)S(1)} %get-tuple-element.27), channel_id=1, source_target_pairs={{0,1},{1,0},{2,3},{3,2},{4,5},{5,4},{6,7},{7,6},{8,9},{9,8},{10,11... | collective-permute-start | bytes 12296 | tf_op jit(solution)/shard_map/ppermute | solution.py:203
  28.6 25.3 %collective-permute-start.10 = (f32[2,576,256]{2,1,0:T(8,128)S(1)}, f32[2,576,256]{2,1,0:T(8,128)S(1)}, u32[]{:S(2)}, u32[]{:S(2)}) collective-permute-start(f32[2,576,256]{2,1,0:T(8,128)S(1)} %get-tuple-element.31.refs_0_), channel_id=1, source_target_pairs={{0,16},{1,9},{2,18},{3,11},{4,20},{5,13},{6,22},{7,15},{8,24},{9,1... | collective-permute-start | bytes 3538952 | tf_op jit(solution)/shard_map/ppermute | solution.py:203
  30.4 14.7 %collective-permute-start.5 = (f32[2,2,256,128]{3,2,1,0:T(8,128)S(1)}, f32[2,2,256,128]{3,2,1,0:T(8,128)S(1)}, u32[]{:S(2)}, u32[]{:S(2)}) collective-permute-start(f32[2,2,256,128]{3,2,1,0:T(8,128)S(1)} %shard_map.32.near), channel_id=1, source_target_pairs={{0,2},{1,5},{2,0},{3,7},{4,6},{5,1},{6,4},{7,3},{8,10},{9,13},{10,... | collective-permute-start | bytes 1572872 | tf_op jit(solution)/shard_map/ppermute | solution.py:203
  31.2 7.8 %collective-permute-start.16 = (f32[2,96,256]{2,1,0:T(8,128)S(1)}, f32[2,96,256]{2,1,0:T(8,128)S(1)}, u32[]{:S(2)}, u32[]{:S(2)}) collective-permute-start(f32[2,96,256]{2,1,0:T(8,128)S(1)} %get-tuple-element.22.refs_2_), channel_id=1, source_target_pairs={{0,8},{1,17},{2,10},{3,19},{4,12},{5,21},{6,14},{7,23},{8,0},{9,25... | collective-permute-start | bytes 589832 | tf_op jit(solution)/shard_map/ppermute | solution.py:203
  32.7 6.9 %collective-permute-start.4 = (f32[2,256,128]{2,1,0:T(8,128)S(1)}, f32[2,256,128]{2,1,0:T(8,128)S(1)}, u32[]{:S(2)}, u32[]{:S(2)}) collective-permute-start(f32[2,256,128]{2,1,0:T(8,128)S(1)} %get-tuple-element.28), channel_id=1, source_target_pairs={{0,1},{1,0},{2,3},{3,2},{4,5},{5,4},{6,7},{7,6},{8,9},{9,8},{10,11... | collective-permute-start | bytes 786440 | tf_op jit(solution)/shard_map/ppermute | solution.py:203
  39.0 14.9 %collective-permute-start.11 = (f32[2,320,256]{2,1,0:T(8,128)S(1)}, f32[2,320,256]{2,1,0:T(8,128)S(1)}, u32[]{:S(2)}, u32[]{:S(2)}) collective-permute-start(f32[2,320,256]{2,1,0:T(8,128)S(1)} %get-tuple-element.32.refs_2_), channel_id=1, source_target_pairs={{0,16},{1,9},{2,18},{3,11},{4,20},{5,13},{6,22},{7,15},{8,24},{9,1... | collective-permute-start | bytes 1966088 | tf_op jit(solution)/shard_map/ppermute | solution.py:203
  39.6 9.7 %collective-permute-start.12 = (f32[2,2,256,128]{3,2,1,0:T(8,128)S(1)}, f32[2,2,256,128]{3,2,1,0:T(8,128)S(1)}, u32[]{:S(2)}, u32[]{:S(2)}) collective-permute-start(f32[2,2,256,128]{3,2,1,0:T(8,128)S(1)} %shard_map.32.near), channel_id=1, source_target_pairs={{0,1},{1,0},{2,3},{3,2},{4,5},{5,4},{6,7},{7,6},{8,9},{9,8},{10,11... | collective-permute-start | bytes 1572872 | tf_op jit(solution)/shard_map/ppermute | solution.py:203
  45.1 8.9 %collective-permute-start.13 = (f32[2,2,256,128]{3,2,1,0:T(8,128)S(1)}, f32[2,2,256,128]{3,2,1,0:T(8,128)S(1)}, u32[]{:S(2)}, u32[]{:S(2)}) collective-permute-start(f32[2,2,256,128]{3,2,1,0:T(8,128)S(1)} %collective-permute-done.5.far), channel_id=1, source_target_pairs={{0,1},{1,0},{2,3},{3,2},{4,5},{5,4},{6,7},{7,6},{8,9},{9,8},{10,11... | collective-permute-start | bytes 1572872 | tf_op jit(solution)/shard_map/ppermute | solution.py:203
  45.1 15.0 %collective-permute-start.6 = (f32[2,2,256,128]{3,2,1,0:T(8,128)S(1)}, f32[2,2,256,128]{3,2,1,0:T(8,128)S(1)}, u32[]{:S(2)}, u32[]{:S(2)}) collective-permute-start(f32[2,2,256,128]{3,2,1,0:T(8,128)S(1)} %shard_map.33.held), channel_id=1, source_target_pairs={{0,4},{1,3},{2,6},{3,1},{4,0},{5,7},{6,2},{7,5},{8,12},{9,11},{10,... | collective-permute-start | bytes 1572872 | tf_op jit(solution)/shard_map/ppermute | solution.py:203
  49.2 39.6 %collective-permute-start.17 = (f32[2,256,896]{2,1,0:T(8,128)S(1)}, f32[2,256,896]{2,1,0:T(8,128)S(1)}, u32[]{:S(2)}, u32[]{:S(2)}) collective-permute-start(f32[2,256,896]{2,1,0:T(8,128)S(1)} %shard_map.38), channel_id=1, source_target_pairs={{0,16},{1,9},{2,18},{3,11},{4,20},{5,13},{6,22},{7,15},{8,24},{9,1... | collective-permute-start | bytes 5505032 | tf_op jit(solution)/shard_map/ppermute | solution.py:203
  56.3 36.2 %collective-permute-start.14 = (f32[2,256,896]{2,1,0:T(8,128)S(1)}, f32[2,256,896]{2,1,0:T(8,128)S(1)}, u32[]{:S(2)}, u32[]{:S(2)}) collective-permute-start(f32[2,256,896]{2,1,0:T(8,128)S(1)} %shard_map.36), channel_id=1, source_target_pairs={{0,8},{1,17},{2,10},{3,19},{4,12},{5,21},{6,14},{7,23},{8,0},{9,25... | collective-permute-start | bytes 5505032 | tf_op jit(solution)/shard_map/ppermute | solution.py:203
  60.3 2.0 %collective-permute-start.7 = (f32[2,2,256,128]{3,2,1,0:T(8,128)S(1)}, f32[2,2,256,128]{3,2,1,0:T(8,128)S(1)}, u32[]{:S(2)}, u32[]{:S(2)}) collective-permute-start(f32[2,2,256,128]{3,2,1,0:T(8,128)S(1)} %shard_map.34.near), channel_id=1, source_target_pairs={{0,1},{1,0},{2,3},{3,2},{4,5},{5,4},{6,7},{7,6},{8,9},{9,8},{10,11... | collective-permute-start | bytes 1572872 | tf_op jit(solution)/shard_map/ppermute | solution.py:203
  62.2 14.8 %collective-permute-start.8 = (f32[2,2,256,128]{3,2,1,0:T(8,128)S(1)}, f32[2,2,256,128]{3,2,1,0:T(8,128)S(1)}, u32[]{:S(2)}, u32[]{:S(2)}) collective-permute-start(f32[2,2,256,128]{3,2,1,0:T(8,128)S(1)} %shard_map.34.near), channel_id=1, source_target_pairs={{0,2},{1,5},{2,0},{3,7},{4,6},{5,1},{6,4},{7,3},{8,10},{9,13},{10,... | collective-permute-start | bytes 1572872 | tf_op jit(solution)/shard_map/ppermute | solution.py:203
  77.0 2.3 %collective-permute-start.9 = (f32[2,2,256,128]{3,2,1,0:T(8,128)S(1)}, f32[2,2,256,128]{3,2,1,0:T(8,128)S(1)}, u32[]{:S(2)}, u32[]{:S(2)}) collective-permute-start(f32[2,2,256,128]{3,2,1,0:T(8,128)S(1)} %collective-permute-done.8.far), channel_id=1, source_target_pairs={{0,1},{1,0},{2,3},{3,2},{4,5},{5,4},{6,7},{7,6},{8,9},{9,8},{10,11... | collective-permute-start | bytes 1572872 | tf_op jit(solution)/shard_map/ppermute | solution.py:203

commit v5 on v4

--- a/solution.py
+++ b/solution.py
@@ -205,15 +205,16 @@
 
 def spread(held, short):
     if short:
-        near, small = choose(held, permute(held, FIRST_Z), 1)
-        near = gate(near, permute(small, OVER_CORE))
+        ready, small = choose(held, permute(held, FIRST_Z), 1)
+        near = gate(ready, permute(small, OVER_CORE))
         near_other = permute(near, OVER_CORE)
         far = permute(near, SECOND_Z)
     else:
         (near,) = choose(held, permute(held, FIRST_Z))
+        ready = near
         near_other = permute(near, OVER_CORE)
         far = permute(tie(near, near_other), SECOND_Z)
-    return [[near, far], [near_other, permute(far, OVER_CORE)]]
+    return [[near, far], [near_other, permute(far, OVER_CORE)]], ready
 
 
 def hybrid_body(amplitudes, integrals):
@@ -221,15 +222,15 @@
     same, cross = permute(mine, SAME_CORE), permute(give, CROSS_CORE)
     n_ab = integrals.shape[1]
     own = kinds(integrals, (n_ab * 25 // 28,), (n_ab * 9 // 14,))
-    send = spread(merge(tie(same, *own[0], *own[1]), cross), True)
-
-    own[1] = [tie(a, send[0][0]) for a in own[1]]
+    send, ready = spread(merge(tie(same, *own[0], *own[1]), cross), True)
+
+    own[1] = [tie(a, ready) for a in own[1]]
     got = [[permute(a, perm) for a in pieces] for pieces, perm in zip(own, (FIRST_KIND, SECOND_KIND))]
     came = []
     for order, perm in enumerate((SECOND_KIND, FIRST_KIND)):
         came.append(permute(partial_sum(order, *send[order], own[order], got[order]), perm))
 
-    keep = spread(tie(merge(mine, permute(tie(give, send[0][0]), OVER_CORE)), send[0][1]), False)
+    keep, _ = spread(tie(merge(mine, permute(tie(give, send[0][0]), OVER_CORE)), send[0][1]), False)
     out = []
     for order in range(2):
         kept = partial_sum(order, *keep[order], own[order], got[order])

time: 94.2 us -> 93.4 us (level)
  waiting for transfers between devices: 59.8 us -> 58.5 us
    ppermute x18, waiting for transfers between devices: 59.8 us -> 58.5 us  [permute(): return lax.ppermute(a, BOTH, perm)]
  transfers between devices with their start and end apart: 18 -> 18, of which waited for: 12 -> 11; matrix products, arithmetic and copies ran while one was open for 0% -> 0% of each run, Pallas kernels for 12% -> 12%
where the time goes in v5:
time: 93.4 us; the launch traced here: 93 us
  waiting for transfers between devices  58.5 us (63%)
  starting transfers between devices  18.4 us (20%)
  Pallas kernels  12.8 us (14%)
  local copies, waits for them, and re-layouts  3.08 us (3%)
    ppermute x18, waiting for transfers between devices, permute(): return lax.ppermute(a, BOTH, perm)  58.5 us
    ppermute x18, starting transfers between devices, permute(): return lax.ppermute(a, BOTH, perm)  18.4 us
    pallas_call x13, Pallas kernels, call(): pl.pallas_call(kernel, out_shape=out_shape, in_specs=in_specs, out_specs=...  12.8 us
    unnamed x4, local copies, waits for them, and re-layouts  3.08 us
  transfers between devices with their start and end apart: 18, of which 11 were waited for; matrix products, arithmetic and copies ran while one was open for 0% of the time, Pallas kernels for 12%

profile of v5, /device:TPU:0, one launch (start us, length us, event | category | flops | bytes accessed | tf_op | source)
XLA Modules:
  0.0 93.0 jit_solution(10943361401014084949)
XLA Ops:
  0.0 1.0 %copy-done.1 = f32[4,256,128]{2,1,0:T(8,128)S(1)} copy-done((f32[4,256,128]{2,1,0:T(8,128)S(1)}, f32[4,256,128]{2,1,0:T(8,128)}, u32[]{:S(2)}) %copy-start.1) | copy-done | bytes 524312
  1.1 3.0 %collective-permute-start = (f32[2,256,128]{2,1,0:T(8,128)S(1)}, f32[2,256,128]{2,1,0:T(8,128)S(1)}, u32[]{:S(2)}, u32[]{:S(2)}) collective-permute-start(f32[2,256,128]{2,1,0:T(8,128)S(1)} %get-tuple-element.19.first), channel_id=1, source_target_pairs={{0,16},{1,9},{2,18},{3,11},{4,20},{5,13},{6,22},{7,15},{8,24},{9,1... | collective-permute-start | bytes 786440 | tf_op jit(solution)/shard_map/ppermute | solution.py:203
  4.1 2.0 %copy-done = f32[4,896,256]{2,1,0:T(8,128)S(1)} copy-done((f32[4,896,256]{2,1,0:T(8,128)S(1)}, f32[4,896,256]{2,1,0:T(8,128)}, u32[]{:S(2)}) %copy-start) | copy-done | bytes 3670040
  6.2 0.6 shard_map.29
  6.8 1.6 %collective-permute-start.15 = (f32[2,800,256]{2,1,0:T(8,128)S(1)}, f32[2,800,256]{2,1,0:T(8,128)S(1)}, u32[]{:S(2)}, u32[]{:S(2)}) collective-permute-start(f32[2,800,256]{2,1,0:T(8,128)S(1)} %get-tuple-element.21.refs_0_), channel_id=1, source_target_pairs={{0,8},{1,17},{2,10},{3,19},{4,12},{5,21},{6,14},{7,23},{8,0},{9,25... | collective-permute-start | bytes 4915208 | tf_op jit(solution)/shard_map/ppermute | solution.py:203
  8.3 2.4 %collective-permute-done.first = f32[2,256,128]{2,1,0:T(8,128)S(1)} collective-permute-done((f32[2,256,128]{2,1,0:T(8,128)S(1)}, f32[2,256,128]{2,1,0:T(8,128)S(1)}, u32[]{:S(2)}, u32[]{:S(2)}) %collective-permute-start) | collective-permute-done | bytes 262176 | tf_op jit(solution)/shard_map/ppermute | solution.py:203
  10.8 0.5 collective-permute-done.1.second
  11.3 3.2 %collective-permute-start.2 = (f32[2,2,256,128]{3,2,1,0:T(8,128)S(1)}, f32[2,2,256,128]{3,2,1,0:T(8,128)S(1)}, u32[]{:S(2)}, u32[]{:S(2)}) collective-permute-start(f32[2,2,256,128]{3,2,1,0:T(8,128)S(1)} %shard_map.30.held), channel_id=1, source_target_pairs={{0,4},{1,3},{2,6},{3,1},{4,0},{5,7},{6,2},{7,5},{8,12},{9,11},{10,... | collective-permute-start | bytes 1572872 | tf_op jit(solution)/shard_map/ppermute | solution.py:203
  14.5 12.8 %collective-permute-done.2.got = f32[2,2,256,128]{3,2,1,0:T(8,128)S(1)} collective-permute-done((f32[2,2,256,128]{3,2,1,0:T(8,128)S(1)}, f32[2,2,256,128]{3,2,1,0:T(8,128)S(1)}, u32[]{:S(2)}, u32[]{:S(2)}) %collective-permute-start.2) | collective-permute-done | bytes 524320 | tf_op jit(solution)/shard_map/ppermute | solution.py:203
  27.4 1.8 %collective-permute-start.10 = (f32[2,576,256]{2,1,0:T(8,128)S(1)}, f32[2,576,256]{2,1,0:T(8,128)S(1)}, u32[]{:S(2)}, u32[]{:S(2)}) collective-permute-start(f32[2,576,256]{2,1,0:T(8,128)S(1)} %get-tuple-element.31.refs_0_), channel_id=1, source_target_pairs={{0,16},{1,9},{2,18},{3,11},{4,20},{5,13},{6,22},{7,15},{8,24},{9,1... | collective-permute-start | bytes 3538952 | tf_op jit(solution)/shard_map/ppermute | solution.py:203
  29.3 1.2 %collective-permute-done.3.small = f32[8,128]{1,0:T(8,128)S(1)} collective-permute-done((f32[8,128]{1,0:T(8,128)S(1)}, f32[8,128]{1,0:T(8,128)S(1)}, u32[]{:S(2)}, u32[]{:S(2)}) %collective-permute-start.3) | collective-permute-done | bytes 4128 | tf_op jit(solution)/shard_map/ppermute | solution.py:203
  30.4 0.8 collective-permute-start.5
  31.2 1.5 %collective-permute-start.16 = (f32[2,96,256]{2,1,0:T(8,128)S(1)}, f32[2,96,256]{2,1,0:T(8,128)S(1)}, u32[]{:S(2)}, u32[]{:S(2)}) collective-permute-start(f32[2,96,256]{2,1,0:T(8,128)S(1)} %get-tuple-element.22.refs_2_), channel_id=1, source_target_pairs={{0,8},{1,17},{2,10},{3,19},{4,12},{5,21},{6,14},{7,23},{8,0},{9,25... | collective-permute-start | bytes 589832 | tf_op jit(solution)/shard_map/ppermute | solution.py:203
  32.7 6.3 %collective-permute-done.16.refs_3_ = f32[2,96,256]{2,1,0:T(8,128)S(1)} collective-permute-done((f32[2,96,256]{2,1,0:T(8,128)S(1)}, f32[2,96,256]{2,1,0:T(8,128)S(1)}, u32[]{:S(2)}, u32[]{:S(2)}) %collective-permute-start.16) | collective-permute-done | bytes 196640 | tf_op jit(solution)/shard_map/ppermute | solution.py:203
  39.0 0.5 collective-permute-start.11
  39.6 5.7 %collective-permute-done.5.far = f32[2,2,256,128]{3,2,1,0:T(8,128)S(1)} collective-permute-done((f32[2,2,256,128]{3,2,1,0:T(8,128)S(1)}, f32[2,2,256,128]{3,2,1,0:T(8,128)S(1)}, u32[]{:S(2)}, u32[]{:S(2)}) %collective-permute-start.5) | collective-permute-done | bytes 524320 | tf_op jit(solution)/shard_map/ppermute | solution.py:203
  45.3 1.8 %collective-permute-start.6 = (f32[2,2,256,128]{3,2,1,0:T(8,128)S(1)}, f32[2,2,256,128]{3,2,1,0:T(8,128)S(1)}, u32[]{:S(2)}, u32[]{:S(2)}) collective-permute-start(f32[2,2,256,128]{3,2,1,0:T(8,128)S(1)} %shard_map.33.held), channel_id=1, source_target_pairs={{0,4},{1,3},{2,6},{3,1},{4,0},{5,7},{6,2},{7,5},{8,12},{9,11},{10,... | collective-permute-start | bytes 1572872 | tf_op jit(solution)/shard_map/ppermute | solution.py:203
  47.0 2.3 %shard_map.38 = f32[2,256,896]{2,1,0:T(8,128)S(1)} custom-call(f32[2,2,256,128]{3,2,1,0:T(8,128)S(1)} %shard_map.32.near, f32[2,2,256,128]{3,2,1,0:T(8,128)S(1)} %collective-permute-done.5.far, f32[2,800,256]{2,1,0:T(8,128)S(1)} %get-tuple-element.21.refs_0_, f32[2,800,256]{2,1,0:T(8,128)S(1)} %collective-permute-done.15.refs_1_, ...), custom_call_target="tpu_custom_call" | custom-call | flops 1409286144 | bytes 6553600 | tf_op jit(solution)/shard_map/pallas_call | solution.py:51
  49.3 0.6 collective-permute-start.17
  49.9 2.9 %collective-permute-done.11.refs_3_ = f32[2,320,256]{2,1,0:T(8,128)S(1)} collective-permute-done((f32[2,320,256]{2,1,0:T(8,128)S(1)}, f32[2,320,256]{2,1,0:T(8,128)S(1)}, u32[]{:S(2)}, u32[]{:S(2)}) %collective-permute-start.11) | collective-permute-done | bytes 655392 | tf_op jit(solution)/shard_map/ppermute | solution.py:203
  52.8 2.3 %shard_map.36 = f32[2,256,896]{2,1,0:T(8,128)S(1)} custom-call(f32[2,2,256,128]{3,2,1,0:T(8,128)S(1)} %collective-permute-done.12.near, f32[2,2,256,128]{3,2,1,0:T(8,128)S(1)} %collective-permute-done.13.far, f32[2,576,256]{2,1,0:T(8,128)S(1)} %get-tuple-element.31.refs_0_, f32[2,576,256]{2,1,0:T(8,128)S(1)} %collective-permute-done.10.refs_1_, ...), custom_call_target="tpu_custom_call" | custom-call | flops 1409286144 | bytes 6553600 | tf_op jit(solution)/shard_map/pallas_call | solution.py:51
  55.2 1.9 %collective-permute-start.14 = (f32[2,256,896]{2,1,0:T(8,128)S(1)}, f32[2,256,896]{2,1,0:T(8,128)S(1)}, u32[]{:S(2)}, u32[]{:S(2)}) collective-permute-start(f32[2,256,896]{2,1,0:T(8,128)S(1)} %shard_map.36), channel_id=1, source_target_pairs={{0,8},{1,17},{2,10},{3,19},{4,12},{5,21},{6,14},{7,23},{8,0},{9,25... | collective-permute-start | bytes 5505032 | tf_op jit(solution)/shard_map/ppermute | solution.py:203
  57.0 3.3 %collective-permute-done.6.got = f32[2,2,256,128]{3,2,1,0:T(8,128)S(1)} collective-permute-done((f32[2,2,256,128]{3,2,1,0:T(8,128)S(1)}, f32[2,2,256,128]{3,2,1,0:T(8,128)S(1)}, u32[]{:S(2)}, u32[]{:S(2)}) %collective-permute-start.6) | collective-permute-done | bytes 524320 | tf_op jit(solution)/shard_map/ppermute | solution.py:203
  60.4 0.1 collective-permute-start.7
  60.5 1.9 %collective-permute-done.7.near = f32[2,2,256,128]{3,2,1,0:T(8,128)S(1)} collective-permute-done((f32[2,2,256,128]{3,2,1,0:T(8,128)S(1)}, f32[2,2,256,128]{3,2,1,0:T(8,128)S(1)}, u32[]{:S(2)}, u32[]{:S(2)}) %collective-permute-start.7) | collective-permute-done | bytes 524320 | tf_op jit(solution)/shard_map/ppermute | solution.py:203
  62.4 1.8 %collective-permute-start.8 = (f32[2,2,256,128]{3,2,1,0:T(8,128)S(1)}, f32[2,2,256,128]{3,2,1,0:T(8,128)S(1)}, u32[]{:S(2)}, u32[]{:S(2)}) collective-permute-start(f32[2,2,256,128]{3,2,1,0:T(8,128)S(1)} %shard_map.34.near), channel_id=1, source_target_pairs={{0,2},{1,5},{2,0},{3,7},{4,6},{5,1},{6,4},{7,3},{8,10},{9,13},{10,... | collective-permute-start | bytes 1572872 | tf_op jit(solution)/shard_map/ppermute | solution.py:203
  64.2 13.0 %collective-permute-done.8.far = f32[2,2,256,128]{3,2,1,0:T(8,128)S(1)} collective-permute-done((f32[2,2,256,128]{3,2,1,0:T(8,128)S(1)}, f32[2,2,256,128]{3,2,1,0:T(8,128)S(1)}, u32[]{:S(2)}, u32[]{:S(2)}) %collective-permute-start.8) | collective-permute-done | bytes 524320 | tf_op jit(solution)/shard_map/ppermute | solution.py:203
  77.2 2.3 %shard_map.37.kept = f32[2,256,896]{2,1,0:T(8,128)S(1)} custom-call(f32[2,2,256,128]{3,2,1,0:T(8,128)S(1)} %shard_map.34.near, f32[2,2,256,128]{3,2,1,0:T(8,128)S(1)} %collective-permute-done.8.far, f32[2,800,256]{2,1,0:T(8,128)S(1)} %get-tuple-element.21.refs_0_, f32[2,800,256]{2,1,0:T(8,128)S(1)} %collective-permute-done.15.refs_1_, ...), custom_call_target="tpu_custom_call" | custom-call | flops 1409286144 | bytes 6553600 | tf_op jit(solution)/shard_map/pallas_call | solution.py:51
  79.5 2.3 %shard_map.35.kept = f32[2,256,896]{2,1,0:T(8,128)S(1)} custom-call(f32[2,2,256,128]{3,2,1,0:T(8,128)S(1)} %collective-permute-done.7.near, f32[2,2,256,128]{3,2,1,0:T(8,128)S(1)} %collective-permute-done.9.far, f32[2,576,256]{2,1,0:T(8,128)S(1)} %get-tuple-element.31.refs_0_, f32[2,576,256]{2,1,0:T(8,128)S(1)} %collective-permute-done.10.refs_1_, ...), custom_call_target="tpu_custom_call" | custom-call | flops 1409286144 | bytes 6553600 | tf_op jit(solution)/shard_map/pallas_call | solution.py:51
  81.9 8.4 %collective-permute-done.17.came = f32[2,256,896]{2,1,0:T(8,128)S(1)} collective-permute-done((f32[2,256,896]{2,1,0:T(8,128)S(1)}, f32[2,256,896]{2,1,0:T(8,128)S(1)}, u32[]{:S(2)}, u32[]{:S(2)}) %collective-permute-start.17) | collective-permute-done | bytes 1835040 | tf_op jit(solution)/shard_map/ppermute | solution.py:203
  90.3 1.3 %shard_map.39.refs_0_ = f32[4,256,896]{2,1,0:T(8,128)} custom-call(f32[2,256,896]{2,1,0:T(8,128)S(1)} %shard_map.37.kept, f32[2,256,896]{2,1,0:T(8,128)S(1)} %collective-permute-done.17.came), custom_call_target="tpu_custom_call" | custom-call | flops 917504 | bytes 7340032 | tf_op jit(solution)/shard_map/pallas_call | solution.py:51
  91.7 1.3 %shard_map.40 = f32[4,256,896]{2,1,0:T(8,128)} custom-call(f32[2,256,896]{2,1,0:T(8,128)S(1)} %shard_map.35.kept, f32[2,256,896]{2,1,0:T(8,128)S(1)} %collective-permute-done.14.came, f32[4,256,896]{2,1,0:T(8,128)} %shard_map.39.refs_0_), custom_call_target="tpu_custom_call", output_to_operand_aliasing={{}: (2, {})} | custom-call | flops 917504 | bytes 11010048 | tf_op jit(solution)/shard_map/pallas_call | solution.py:51
  (21 shorter events, 0.3 us)
Async XLA Ops:
  0.0 1.0 %copy-start.1 = (f32[4,256,128]{2,1,0:T(8,128)S(1)}, f32[4,256,128]{2,1,0:T(8,128)}, u32[]{:S(2)}) copy-start(f32[4,256,128]{2,1,0:T(8,128)} %whole.2) | copy-start | bytes 1572868
  1.1 9.7 %collective-permute-start = (f32[2,256,128]{2,1,0:T(8,128)S(1)}, f32[2,256,128]{2,1,0:T(8,128)S(1)}, u32[]{:S(2)}, u32[]{:S(2)}) collective-permute-start(f32[2,256,128]{2,1,0:T(8,128)S(1)} %get-tuple-element.19.first), channel_id=1, source_target_pairs={{0,16},{1,9},{2,18},{3,11},{4,20},{5,13},{6,22},{7,15},{8,24},{9,1... | collective-permute-start | bytes 786440 | tf_op jit(solution)/shard_map/ppermute | solution.py:203
  4.1 7.2 %collective-permute-start.1 = (f32[2,256,128]{2,1,0:T(8,128)S(1)}, f32[2,256,128]{2,1,0:T(8,128)S(1)}, u32[]{:S(2)}, u32[]{:S(2)}) collective-permute-start(f32[2,256,128]{2,1,0:T(8,128)S(1)} %get-tuple-element.28), channel_id=1, source_target_pairs={{0,9},{1,16},{2,11},{3,18},{4,13},{5,20},{6,15},{7,22},{8,1},{9,24... | collective-permute-start | bytes 786440 | tf_op jit(solution)/shard_map/ppermute | solution.py:203
  4.1 2.0 %copy-start = (f32[4,896,256]{2,1,0:T(8,128)S(1)}, f32[4,896,256]{2,1,0:T(8,128)}, u32[]{:S(2)}) copy-start(f32[4,896,256]{2,1,0:T(8,128)} %whole.3) | copy-start | bytes 11010052
  6.8 38.5 %collective-permute-start.15 = (f32[2,800,256]{2,1,0:T(8,128)S(1)}, f32[2,800,256]{2,1,0:T(8,128)S(1)}, u32[]{:S(2)}, u32[]{:S(2)}) collective-permute-start(f32[2,800,256]{2,1,0:T(8,128)S(1)} %get-tuple-element.21.refs_0_), channel_id=1, source_target_pairs={{0,8},{1,17},{2,10},{3,19},{4,12},{5,21},{6,14},{7,23},{8,0},{9,25... | collective-permute-start | bytes 4915208 | tf_op jit(solution)/shard_map/ppermute | solution.py:203
  11.3 16.0 %collective-permute-start.2 = (f32[2,2,256,128]{3,2,1,0:T(8,128)S(1)}, f32[2,2,256,128]{3,2,1,0:T(8,128)S(1)}, u32[]{:S(2)}, u32[]{:S(2)}) collective-permute-start(f32[2,2,256,128]{3,2,1,0:T(8,128)S(1)} %shard_map.30.held), channel_id=1, source_target_pairs={{0,4},{1,3},{2,6},{3,1},{4,0},{5,7},{6,2},{7,5},{8,12},{9,11},{10,... | collective-permute-start | bytes 1572872 | tf_op jit(solution)/shard_map/ppermute | solution.py:203
  27.4 25.4 %collective-permute-start.10 = (f32[2,576,256]{2,1,0:T(8,128)S(1)}, f32[2,576,256]{2,1,0:T(8,128)S(1)}, u32[]{:S(2)}, u32[]{:S(2)}) collective-permute-start(f32[2,576,256]{2,1,0:T(8,128)S(1)} %get-tuple-element.31.refs_0_), channel_id=1, source_target_pairs={{0,16},{1,9},{2,18},{3,11},{4,20},{5,13},{6,22},{7,15},{8,24},{9,1... | collective-permute-start | bytes 3538952 | tf_op jit(solution)/shard_map/ppermute | solution.py:203
  29.3 1.2 %collective-permute-start.3 = (f32[8,128]{1,0:T(8,128)S(1)}, f32[8,128]{1,0:T(8,128)S(1)}, u32[]{:S(2)}, u32[]{:S(2)}) collective-permute-start(f32[8,128]{1,0:T(8,128)S(1)} %get-tuple-element.27), channel_id=1, source_target_pairs={{0,1},{1,0},{2,3},{3,2},{4,5},{5,4},{6,7},{7,6},{8,9},{9,8},{10,11... | collective-permute-start | bytes 12296 | tf_op jit(solution)/shard_map/ppermute | solution.py:203
  30.4 14.8 %collective-permute-start.5 = (f32[2,2,256,128]{3,2,1,0:T(8,128)S(1)}, f32[2,2,256,128]{3,2,1,0:T(8,128)S(1)}, u32[]{:S(2)}, u32[]{:S(2)}) collective-permute-start(f32[2,2,256,128]{3,2,1,0:T(8,128)S(1)} %shard_map.32.near), channel_id=1, source_target_pairs={{0,2},{1,5},{2,0},{3,7},{4,6},{5,1},{6,4},{7,3},{8,10},{9,13},{10,... | collective-permute-start | bytes 1572872 | tf_op jit(solution)/shard_map/ppermute | solution.py:203
  31.2 7.8 %collective-permute-start.16 = (f32[2,96,256]{2,1,0:T(8,128)S(1)}, f32[2,96,256]{2,1,0:T(8,128)S(1)}, u32[]{:S(2)}, u32[]{:S(2)}) collective-permute-start(f32[2,96,256]{2,1,0:T(8,128)S(1)} %get-tuple-element.22.refs_2_), channel_id=1, source_target_pairs={{0,8},{1,17},{2,10},{3,19},{4,12},{5,21},{6,14},{7,23},{8,0},{9,25... | collective-permute-start | bytes 589832 | tf_op jit(solution)/shard_map/ppermute | solution.py:203
  32.7 6.9 %collective-permute-start.4 = (f32[2,256,128]{2,1,0:T(8,128)S(1)}, f32[2,256,128]{2,1,0:T(8,128)S(1)}, u32[]{:S(2)}, u32[]{:S(2)}) collective-permute-start(f32[2,256,128]{2,1,0:T(8,128)S(1)} %get-tuple-element.28), channel_id=1, source_target_pairs={{0,1},{1,0},{2,3},{3,2},{4,5},{5,4},{6,7},{7,6},{8,9},{9,8},{10,11... | collective-permute-start | bytes 786440 | tf_op jit(solution)/shard_map/ppermute | solution.py:203
  39.0 13.8 %collective-permute-start.11 = (f32[2,320,256]{2,1,0:T(8,128)S(1)}, f32[2,320,256]{2,1,0:T(8,128)S(1)}, u32[]{:S(2)}, u32[]{:S(2)}) collective-permute-start(f32[2,320,256]{2,1,0:T(8,128)S(1)} %get-tuple-element.32.refs_2_), channel_id=1, source_target_pairs={{0,16},{1,9},{2,18},{3,11},{4,20},{5,13},{6,22},{7,15},{8,24},{9,1... | collective-permute-start | bytes 1966088 | tf_op jit(solution)/shard_map/ppermute | solution.py:203
  39.6 9.8 %collective-permute-start.12 = (f32[2,2,256,128]{3,2,1,0:T(8,128)S(1)}, f32[2,2,256,128]{3,2,1,0:T(8,128)S(1)}, u32[]{:S(2)}, u32[]{:S(2)}) collective-permute-start(f32[2,2,256,128]{3,2,1,0:T(8,128)S(1)} %shard_map.32.near), channel_id=1, source_target_pairs={{0,1},{1,0},{2,3},{3,2},{4,5},{5,4},{6,7},{7,6},{8,9},{9,8},{10,11... | collective-permute-start | bytes 1572872 | tf_op jit(solution)/shard_map/ppermute | solution.py:203
  45.2 7.6 %collective-permute-start.13 = (f32[2,2,256,128]{3,2,1,0:T(8,128)S(1)}, f32[2,2,256,128]{3,2,1,0:T(8,128)S(1)}, u32[]{:S(2)}, u32[]{:S(2)}) collective-permute-start(f32[2,2,256,128]{3,2,1,0:T(8,128)S(1)} %collective-permute-done.5.far), channel_id=1, source_target_pairs={{0,1},{1,0},{2,3},{3,2},{4,5},{5,4},{6,7},{7,6},{8,9},{9,8},{10,11... | collective-permute-start | bytes 1572872 | tf_op jit(solution)/shard_map/ppermute | solution.py:203
  45.3 15.1 %collective-permute-start.6 = (f32[2,2,256,128]{3,2,1,0:T(8,128)S(1)}, f32[2,2,256,128]{3,2,1,0:T(8,128)S(1)}, u32[]{:S(2)}, u32[]{:S(2)}) collective-permute-start(f32[2,2,256,128]{3,2,1,0:T(8,128)S(1)} %shard_map.33.held), channel_id=1, source_target_pairs={{0,4},{1,3},{2,6},{3,1},{4,0},{5,7},{6,2},{7,5},{8,12},{9,11},{10,... | collective-permute-start | bytes 1572872 | tf_op jit(solution)/shard_map/ppermute | solution.py:203
  49.3 41.0 %collective-permute-start.17 = (f32[2,256,896]{2,1,0:T(8,128)S(1)}, f32[2,256,896]{2,1,0:T(8,128)S(1)}, u32[]{:S(2)}, u32[]{:S(2)}) collective-permute-start(f32[2,256,896]{2,1,0:T(8,128)S(1)} %shard_map.38), channel_id=1, source_target_pairs={{0,16},{1,9},{2,18},{3,11},{4,20},{5,13},{6,22},{7,15},{8,24},{9,1... | collective-permute-start | bytes 5505032 | tf_op jit(solution)/shard_map/ppermute | solution.py:203
  55.2 36.5 %collective-permute-start.14 = (f32[2,256,896]{2,1,0:T(8,128)S(1)}, f32[2,256,896]{2,1,0:T(8,128)S(1)}, u32[]{:S(2)}, u32[]{:S(2)}) collective-permute-start(f32[2,256,896]{2,1,0:T(8,128)S(1)} %shard_map.36), channel_id=1, source_target_pairs={{0,8},{1,17},{2,10},{3,19},{4,12},{5,21},{6,14},{7,23},{8,0},{9,25... | collective-permute-start | bytes 5505032 | tf_op jit(solution)/shard_map/ppermute | solution.py:203
  60.4 2.0 %collective-permute-start.7 = (f32[2,2,256,128]{3,2,1,0:T(8,128)S(1)}, f32[2,2,256,128]{3,2,1,0:T(8,128)S(1)}, u32[]{:S(2)}, u32[]{:S(2)}) collective-permute-start(f32[2,2,256,128]{3,2,1,0:T(8,128)S(1)} %shard_map.34.near), channel_id=1, source_target_pairs={{0,1},{1,0},{2,3},{3,2},{4,5},{5,4},{6,7},{7,6},{8,9},{9,8},{10,11... | collective-permute-start | bytes 1572872 | tf_op jit(solution)/shard_map/ppermute | solution.py:203
  62.4 14.8 %collective-permute-start.8 = (f32[2,2,256,128]{3,2,1,0:T(8,128)S(1)}, f32[2,2,256,128]{3,2,1,0:T(8,128)S(1)}, u32[]{:S(2)}, u32[]{:S(2)}) collective-permute-start(f32[2,2,256,128]{3,2,1,0:T(8,128)S(1)} %shard_map.34.near), channel_id=1, source_target_pairs={{0,2},{1,5},{2,0},{3,7},{4,6},{5,1},{6,4},{7,3},{8,10},{9,13},{10,... | collective-permute-start | bytes 1572872 | tf_op jit(solution)/shard_map/ppermute | solution.py:203
  77.2 2.3 %collective-permute-start.9 = (f32[2,2,256,128]{3,2,1,0:T(8,128)S(1)}, f32[2,2,256,128]{3,2,1,0:T(8,128)S(1)}, u32[]{:S(2)}, u32[]{:S(2)}) collective-permute-start(f32[2,2,256,128]{3,2,1,0:T(8,128)S(1)} %collective-permute-done.8.far), channel_id=1, source_target_pairs={{0,1},{1,0},{2,3},{3,2},{4,5},{5,4},{6,7},{7,6},{8,9},{9,8},{10,11... | collective-permute-start | bytes 1572872 | tf_op jit(solution)/shard_map/ppermute | solution.py:203

commit v6 on v5

--- a/solution.py
+++ b/solution.py
@@ -221,7 +221,7 @@
     (mine,), (give,) = kinds(amplitudes, (), ())
     same, cross = permute(mine, SAME_CORE), permute(give, CROSS_CORE)
     n_ab = integrals.shape[1]
-    own = kinds(integrals, (n_ab * 25 // 28,), (n_ab * 9 // 14,))
+    own = kinds(integrals, (n_ab * 51 // 56,), (n_ab * 19 // 28,))
     send, ready = spread(merge(tie(same, *own[0], *own[1]), cross), True)
 
     own[1] = [tie(a, ready) for a in own[1]]

time: 93.4 us -> 93.4 us (level)
  no operation moved by 1% of the time
where the time goes in v6:
time: 93.4 us; the launch traced here: 93 us
  waiting for transfers between devices  58.2 us (62%)
  starting transfers between devices  18.8 us (20%)
  Pallas kernels  12.8 us (14%)
  local copies, waits for them, and re-layouts  3.08 us (3%)
    ppermute x18, waiting for transfers between devices, permute(): return lax.ppermute(a, BOTH, perm)  58.2 us
    ppermute x18, starting transfers between devices, permute(): return lax.ppermute(a, BOTH, perm)  18.8 us
    pallas_call x13, Pallas kernels, call(): pl.pallas_call(kernel, out_shape=out_shape, in_specs=in_specs, out_specs=...  12.8 us
    unnamed x4, local copies, waits for them, and re-layouts  3.08 us
  transfers between devices with their start and end apart: 18, of which 11 were waited for; matrix products, arithmetic and copies ran while one was open for 0% of the time, Pallas kernels for 12%

profile of v6, /device:TPU:0, one launch (start us, length us, event | category | flops | bytes accessed | tf_op | source)
XLA Modules:
  0.0 93.0 jit_solution(7022032522747155458)
XLA Ops:
  0.0 1.0 %copy-done.1 = f32[4,256,128]{2,1,0:T(8,128)S(1)} copy-done((f32[4,256,128]{2,1,0:T(8,128)S(1)}, f32[4,256,128]{2,1,0:T(8,128)}, u32[]{:S(2)}) %copy-start.1) | copy-done | bytes 524312
  1.1 3.0 %collective-permute-start = (f32[2,256,128]{2,1,0:T(8,128)S(1)}, f32[2,256,128]{2,1,0:T(8,128)S(1)}, u32[]{:S(2)}, u32[]{:S(2)}) collective-permute-start(f32[2,256,128]{2,1,0:T(8,128)S(1)} %get-tuple-element.19.first), channel_id=1, source_target_pairs={{0,16},{1,9},{2,18},{3,11},{4,20},{5,13},{6,22},{7,15},{8,24},{9,1... | collective-permute-start | bytes 786440 | tf_op jit(solution)/shard_map/ppermute | solution.py:203
  4.1 2.0 %copy-done = f32[4,896,256]{2,1,0:T(8,128)S(1)} copy-done((f32[4,896,256]{2,1,0:T(8,128)S(1)}, f32[4,896,256]{2,1,0:T(8,128)}, u32[]{:S(2)}) %copy-start) | copy-done | bytes 3670040
  6.2 0.6 shard_map.29
  6.8 1.6 %collective-permute-start.15 = (f32[2,816,256]{2,1,0:T(8,128)S(1)}, f32[2,816,256]{2,1,0:T(8,128)S(1)}, u32[]{:S(2)}, u32[]{:S(2)}) collective-permute-start(f32[2,816,256]{2,1,0:T(8,128)S(1)} %get-tuple-element.21.refs_0_), channel_id=1, source_target_pairs={{0,8},{1,17},{2,10},{3,19},{4,12},{5,21},{6,14},{7,23},{8,0},{9,25... | collective-permute-start | bytes 5013512 | tf_op jit(solution)/shard_map/ppermute | solution.py:203
  8.3 2.4 %collective-permute-done.first = f32[2,256,128]{2,1,0:T(8,128)S(1)} collective-permute-done((f32[2,256,128]{2,1,0:T(8,128)S(1)}, f32[2,256,128]{2,1,0:T(8,128)S(1)}, u32[]{:S(2)}, u32[]{:S(2)}) %collective-permute-start) | collective-permute-done | bytes 262176 | tf_op jit(solution)/shard_map/ppermute | solution.py:203
  10.8 0.5 collective-permute-done.1.second
  11.3 3.2 %collective-permute-start.2 = (f32[2,2,256,128]{3,2,1,0:T(8,128)S(1)}, f32[2,2,256,128]{3,2,1,0:T(8,128)S(1)}, u32[]{:S(2)}, u32[]{:S(2)}) collective-permute-start(f32[2,2,256,128]{3,2,1,0:T(8,128)S(1)} %shard_map.30.held), channel_id=1, source_target_pairs={{0,4},{1,3},{2,6},{3,1},{4,0},{5,7},{6,2},{7,5},{8,12},{9,11},{10,... | collective-permute-start | bytes 1572872 | tf_op jit(solution)/shard_map/ppermute | solution.py:203
  14.5 12.8 %collective-permute-done.2.got = f32[2,2,256,128]{3,2,1,0:T(8,128)S(1)} collective-permute-done((f32[2,2,256,128]{3,2,1,0:T(8,128)S(1)}, f32[2,2,256,128]{3,2,1,0:T(8,128)S(1)}, u32[]{:S(2)}, u32[]{:S(2)}) %collective-permute-start.2) | collective-permute-done | bytes 524320 | tf_op jit(solution)/shard_map/ppermute | solution.py:203
  27.4 1.8 %collective-permute-start.10 = (f32[2,608,256]{2,1,0:T(8,128)S(1)}, f32[2,608,256]{2,1,0:T(8,128)S(1)}, u32[]{:S(2)}, u32[]{:S(2)}) collective-permute-start(f32[2,608,256]{2,1,0:T(8,128)S(1)} %get-tuple-element.31.refs_0_), channel_id=1, source_target_pairs={{0,16},{1,9},{2,18},{3,11},{4,20},{5,13},{6,22},{7,15},{8,24},{9,1... | collective-permute-start | bytes 3735560 | tf_op jit(solution)/shard_map/ppermute | solution.py:203
  29.3 1.2 %collective-permute-done.3.small = f32[8,128]{1,0:T(8,128)S(1)} collective-permute-done((f32[8,128]{1,0:T(8,128)S(1)}, f32[8,128]{1,0:T(8,128)S(1)}, u32[]{:S(2)}, u32[]{:S(2)}) %collective-permute-start.3) | collective-permute-done | bytes 4128 | tf_op jit(solution)/shard_map/ppermute | solution.py:203
  30.4 0.8 collective-permute-start.5
  31.2 1.5 %collective-permute-start.16 = (f32[2,80,256]{2,1,0:T(8,128)S(1)}, f32[2,80,256]{2,1,0:T(8,128)S(1)}, u32[]{:S(2)}, u32[]{:S(2)}) collective-permute-start(f32[2,80,256]{2,1,0:T(8,128)S(1)} %get-tuple-element.22.refs_2_), channel_id=1, source_target_pairs={{0,8},{1,17},{2,10},{3,19},{4,12},{5,21},{6,14},{7,23},{8,0},{9,25... | collective-permute-start | bytes 491528 | tf_op jit(solution)/shard_map/ppermute | solution.py:203
  32.7 5.6 %collective-permute-done.16.refs_3_ = f32[2,80,256]{2,1,0:T(8,128)S(1)} collective-permute-done((f32[2,80,256]{2,1,0:T(8,128)S(1)}, f32[2,80,256]{2,1,0:T(8,128)S(1)}, u32[]{:S(2)}, u32[]{:S(2)}) %collective-permute-start.16) | collective-permute-done | bytes 163872 | tf_op jit(solution)/shard_map/ppermute | solution.py:203
  38.3 0.5 collective-permute-start.11
  38.9 0.4 collective-permute-start.12
  39.2 6.0 %collective-permute-done.5.far = f32[2,2,256,128]{3,2,1,0:T(8,128)S(1)} collective-permute-done((f32[2,2,256,128]{3,2,1,0:T(8,128)S(1)}, f32[2,2,256,128]{3,2,1,0:T(8,128)S(1)}, u32[]{:S(2)}, u32[]{:S(2)}) %collective-permute-start.5) | collective-permute-done | bytes 524320 | tf_op jit(solution)/shard_map/ppermute | solution.py:203
  45.3 1.8 %collective-permute-start.6 = (f32[2,2,256,128]{3,2,1,0:T(8,128)S(1)}, f32[2,2,256,128]{3,2,1,0:T(8,128)S(1)}, u32[]{:S(2)}, u32[]{:S(2)}) collective-permute-start(f32[2,2,256,128]{3,2,1,0:T(8,128)S(1)} %shard_map.33.held), channel_id=1, source_target_pairs={{0,4},{1,3},{2,6},{3,1},{4,0},{5,7},{6,2},{7,5},{8,12},{9,11},{10,... | collective-permute-start | bytes 1572872 | tf_op jit(solution)/shard_map/ppermute | solution.py:203
  47.0 2.3 %shard_map.38 = f32[2,256,896]{2,1,0:T(8,128)S(1)} custom-call(f32[2,2,256,128]{3,2,1,0:T(8,128)S(1)} %shard_map.32.near, f32[2,2,256,128]{3,2,1,0:T(8,128)S(1)} %collective-permute-done.5.far, f32[2,816,256]{2,1,0:T(8,128)S(1)} %get-tuple-element.21.refs_0_, f32[2,816,256]{2,1,0:T(8,128)S(1)} %collective-permute-done.15.refs_1_, ...), custom_call_target="tpu_custom_call" | custom-call | flops 1409286144 | bytes 6553600 | tf_op jit(solution)/shard_map/pallas_call | solution.py:51
  49.3 0.6 collective-permute-start.17
  49.9 2.5 %collective-permute-done.11.refs_3_ = f32[2,288,256]{2,1,0:T(8,128)S(1)} collective-permute-done((f32[2,288,256]{2,1,0:T(8,128)S(1)}, f32[2,288,256]{2,1,0:T(8,128)S(1)}, u32[]{:S(2)}, u32[]{:S(2)}) %collective-permute-start.11) | collective-permute-done | bytes 589856 | tf_op jit(solution)/shard_map/ppermute | solution.py:203
  52.5 2.3 %shard_map.36 = f32[2,256,896]{2,1,0:T(8,128)S(1)} custom-call(f32[2,2,256,128]{3,2,1,0:T(8,128)S(1)} %collective-permute-done.12.near, f32[2,2,256,128]{3,2,1,0:T(8,128)S(1)} %collective-permute-done.13.far, f32[2,608,256]{2,1,0:T(8,128)S(1)} %get-tuple-element.31.refs_0_, f32[2,608,256]{2,1,0:T(8,128)S(1)} %collective-permute-done.10.refs_1_, ...), custom_call_target="tpu_custom_call" | custom-call | flops 1409286144 | bytes 6553600 | tf_op jit(solution)/shard_map/pallas_call | solution.py:51
  54.8 1.9 %collective-permute-start.14 = (f32[2,256,896]{2,1,0:T(8,128)S(1)}, f32[2,256,896]{2,1,0:T(8,128)S(1)}, u32[]{:S(2)}, u32[]{:S(2)}) collective-permute-start(f32[2,256,896]{2,1,0:T(8,128)S(1)} %shard_map.36), channel_id=1, source_target_pairs={{0,8},{1,17},{2,10},{3,19},{4,12},{5,21},{6,14},{7,23},{8,0},{9,25... | collective-permute-start | bytes 5505032 | tf_op jit(solution)/shard_map/ppermute | solution.py:203
  56.7 3.7 %collective-permute-done.6.got = f32[2,2,256,128]{3,2,1,0:T(8,128)S(1)} collective-permute-done((f32[2,2,256,128]{3,2,1,0:T(8,128)S(1)}, f32[2,2,256,128]{3,2,1,0:T(8,128)S(1)}, u32[]{:S(2)}, u32[]{:S(2)}) %collective-permute-start.6) | collective-permute-done | bytes 524320 | tf_op jit(solution)/shard_map/ppermute | solution.py:203
  60.5 1.9 %collective-permute-done.7.near = f32[2,2,256,128]{3,2,1,0:T(8,128)S(1)} collective-permute-done((f32[2,2,256,128]{3,2,1,0:T(8,128)S(1)}, f32[2,2,256,128]{3,2,1,0:T(8,128)S(1)}, u32[]{:S(2)}, u32[]{:S(2)}) %collective-permute-start.7) | collective-permute-done | bytes 524320 | tf_op jit(solution)/shard_map/ppermute | solution.py:203
  62.4 1.8 %collective-permute-start.8 = (f32[2,2,256,128]{3,2,1,0:T(8,128)S(1)}, f32[2,2,256,128]{3,2,1,0:T(8,128)S(1)}, u32[]{:S(2)}, u32[]{:S(2)}) collective-permute-start(f32[2,2,256,128]{3,2,1,0:T(8,128)S(1)} %shard_map.34.near), channel_id=1, source_target_pairs={{0,2},{1,5},{2,0},{3,7},{4,6},{5,1},{6,4},{7,3},{8,10},{9,13},{10,... | collective-permute-start | bytes 1572872 | tf_op jit(solution)/shard_map/ppermute | solution.py:203
  64.2 13.0 %collective-permute-done.8.far = f32[2,2,256,128]{3,2,1,0:T(8,128)S(1)} collective-permute-done((f32[2,2,256,128]{3,2,1,0:T(8,128)S(1)}, f32[2,2,256,128]{3,2,1,0:T(8,128)S(1)}, u32[]{:S(2)}, u32[]{:S(2)}) %collective-permute-start.8) | collective-permute-done | bytes 524320 | tf_op jit(solution)/shard_map/ppermute | solution.py:203
  77.2 2.3 %shard_map.37.kept = f32[2,256,896]{2,1,0:T(8,128)S(1)} custom-call(f32[2,2,256,128]{3,2,1,0:T(8,128)S(1)} %shard_map.34.near, f32[2,2,256,128]{3,2,1,0:T(8,128)S(1)} %collective-permute-done.8.far, f32[2,816,256]{2,1,0:T(8,128)S(1)} %get-tuple-element.21.refs_0_, f32[2,816,256]{2,1,0:T(8,128)S(1)} %collective-permute-done.15.refs_1_, ...), custom_call_target="tpu_custom_call" | custom-call | flops 1409286144 | bytes 6553600 | tf_op jit(solution)/shard_map/pallas_call | solution.py:51
  79.5 2.3 %shard_map.35.kept = f32[2,256,896]{2,1,0:T(8,128)S(1)} custom-call(f32[2,2,256,128]{3,2,1,0:T(8,128)S(1)} %collective-permute-done.7.near, f32[2,2,256,128]{3,2,1,0:T(8,128)S(1)} %collective-permute-done.9.far, f32[2,608,256]{2,1,0:T(8,128)S(1)} %get-tuple-element.31.refs_0_, f32[2,608,256]{2,1,0:T(8,128)S(1)} %collective-permute-done.10.refs_1_, ...), custom_call_target="tpu_custom_call" | custom-call | flops 1409286144 | bytes 6553600 | tf_op jit(solution)/shard_map/pallas_call | solution.py:51
  81.9 8.4 %collective-permute-done.17.came = f32[2,256,896]{2,1,0:T(8,128)S(1)} collective-permute-done((f32[2,256,896]{2,1,0:T(8,128)S(1)}, f32[2,256,896]{2,1,0:T(8,128)S(1)}, u32[]{:S(2)}, u32[]{:S(2)}) %collective-permute-start.17) | collective-permute-done | bytes 1835040 | tf_op jit(solution)/shard_map/ppermute | solution.py:203
  90.3 1.3 %shard_map.39.refs_0_ = f32[4,256,896]{2,1,0:T(8,128)} custom-call(f32[2,256,896]{2,1,0:T(8,128)S(1)} %shard_map.37.kept, f32[2,256,896]{2,1,0:T(8,128)S(1)} %collective-permute-done.17.came), custom_call_target="tpu_custom_call" | custom-call | flops 917504 | bytes 7340032 | tf_op jit(solution)/shard_map/pallas_call | solution.py:51
  91.7 1.3 %shard_map.40 = f32[4,256,896]{2,1,0:T(8,128)} custom-call(f32[2,256,896]{2,1,0:T(8,128)S(1)} %shard_map.35.kept, f32[2,256,896]{2,1,0:T(8,128)S(1)} %collective-permute-done.14.came, f32[4,256,896]{2,1,0:T(8,128)} %shard_map.39.refs_0_), custom_call_target="tpu_custom_call", output_to_operand_aliasing={{}: (2, {})} | custom-call | flops 917504 | bytes 11010048 | tf_op jit(solution)/shard_map/pallas_call | solution.py:51
  (21 shorter events, 0.4 us)
Async XLA Ops:
  0.0 1.0 %copy-start.1 = (f32[4,256,128]{2,1,0:T(8,128)S(1)}, f32[4,256,128]{2,1,0:T(8,128)}, u32[]{:S(2)}) copy-start(f32[4,256,128]{2,1,0:T(8,128)} %whole.2) | copy-start | bytes 1572868
  1.1 9.7 %collective-permute-start = (f32[2,256,128]{2,1,0:T(8,128)S(1)}, f32[2,256,128]{2,1,0:T(8,128)S(1)}, u32[]{:S(2)}, u32[]{:S(2)}) collective-permute-start(f32[2,256,128]{2,1,0:T(8,128)S(1)} %get-tuple-element.19.first), channel_id=1, source_target_pairs={{0,16},{1,9},{2,18},{3,11},{4,20},{5,13},{6,22},{7,15},{8,24},{9,1... | collective-permute-start | bytes 786440 | tf_op jit(solution)/shard_map/ppermute | solution.py:203
  4.1 7.2 %collective-permute-start.1 = (f32[2,256,128]{2,1,0:T(8,128)S(1)}, f32[2,256,128]{2,1,0:T(8,128)S(1)}, u32[]{:S(2)}, u32[]{:S(2)}) collective-permute-start(f32[2,256,128]{2,1,0:T(8,128)S(1)} %get-tuple-element.28), channel_id=1, source_target_pairs={{0,9},{1,16},{2,11},{3,18},{4,13},{5,20},{6,15},{7,22},{8,1},{9,24... | collective-permute-start | bytes 786440 | tf_op jit(solution)/shard_map/ppermute | solution.py:203
  4.1 2.0 %copy-start = (f32[4,896,256]{2,1,0:T(8,128)S(1)}, f32[4,896,256]{2,1,0:T(8,128)}, u32[]{:S(2)}) copy-start(f32[4,896,256]{2,1,0:T(8,128)} %whole.3) | copy-start | bytes 11010052
  6.8 38.5 %collective-permute-start.15 = (f32[2,816,256]{2,1,0:T(8,128)S(1)}, f32[2,816,256]{2,1,0:T(8,128)S(1)}, u32[]{:S(2)}, u32[]{:S(2)}) collective-permute-start(f32[2,816,256]{2,1,0:T(8,128)S(1)} %get-tuple-element.21.refs_0_), channel_id=1, source_target_pairs={{0,8},{1,17},{2,10},{3,19},{4,12},{5,21},{6,14},{7,23},{8,0},{9,25... | collective-permute-start | bytes 5013512 | tf_op jit(solution)/shard_map/ppermute | solution.py:203
  11.3 16.0 %collective-permute-start.2 = (f32[2,2,256,128]{3,2,1,0:T(8,128)S(1)}, f32[2,2,256,128]{3,2,1,0:T(8,128)S(1)}, u32[]{:S(2)}, u32[]{:S(2)}) collective-permute-start(f32[2,2,256,128]{3,2,1,0:T(8,128)S(1)} %shard_map.30.held), channel_id=1, source_target_pairs={{0,4},{1,3},{2,6},{3,1},{4,0},{5,7},{6,2},{7,5},{8,12},{9,11},{10,... | collective-permute-start | bytes 1572872 | tf_op jit(solution)/shard_map/ppermute | solution.py:203
  27.4 25.1 %collective-permute-start.10 = (f32[2,608,256]{2,1,0:T(8,128)S(1)}, f32[2,608,256]{2,1,0:T(8,128)S(1)}, u32[]{:S(2)}, u32[]{:S(2)}) collective-permute-start(f32[2,608,256]{2,1,0:T(8,128)S(1)} %get-tuple-element.31.refs_0_), channel_id=1, source_target_pairs={{0,16},{1,9},{2,18},{3,11},{4,20},{5,13},{6,22},{7,15},{8,24},{9,1... | collective-permute-start | bytes 3735560 | tf_op jit(solution)/shard_map/ppermute | solution.py:203
  29.3 1.2 %collective-permute-start.3 = (f32[8,128]{1,0:T(8,128)S(1)}, f32[8,128]{1,0:T(8,128)S(1)}, u32[]{:S(2)}, u32[]{:S(2)}) collective-permute-start(f32[8,128]{1,0:T(8,128)S(1)} %get-tuple-element.27), channel_id=1, source_target_pairs={{0,1},{1,0},{2,3},{3,2},{4,5},{5,4},{6,7},{7,6},{8,9},{9,8},{10,11... | collective-permute-start | bytes 12296 | tf_op jit(solution)/shard_map/ppermute | solution.py:203
  30.4 14.8 %collective-permute-start.5 = (f32[2,2,256,128]{3,2,1,0:T(8,128)S(1)}, f32[2,2,256,128]{3,2,1,0:T(8,128)S(1)}, u32[]{:S(2)}, u32[]{:S(2)}) collective-permute-start(f32[2,2,256,128]{3,2,1,0:T(8,128)S(1)} %shard_map.32.near), channel_id=1, source_target_pairs={{0,2},{1,5},{2,0},{3,7},{4,6},{5,1},{6,4},{7,3},{8,10},{9,13},{10,... | collective-permute-start | bytes 1572872 | tf_op jit(solution)/shard_map/ppermute | solution.py:203
  31.2 7.6 %collective-permute-start.4 = (f32[2,256,128]{2,1,0:T(8,128)S(1)}, f32[2,256,128]{2,1,0:T(8,128)S(1)}, u32[]{:S(2)}, u32[]{:S(2)}) collective-permute-start(f32[2,256,128]{2,1,0:T(8,128)S(1)} %get-tuple-element.28), channel_id=1, source_target_pairs={{0,1},{1,0},{2,3},{3,2},{4,5},{5,4},{6,7},{7,6},{8,9},{9,8},{10,11... | collective-permute-start | bytes 786440 | tf_op jit(solution)/shard_map/ppermute | solution.py:203
  31.2 7.1 %collective-permute-start.16 = (f32[2,80,256]{2,1,0:T(8,128)S(1)}, f32[2,80,256]{2,1,0:T(8,128)S(1)}, u32[]{:S(2)}, u32[]{:S(2)}) collective-permute-start(f32[2,80,256]{2,1,0:T(8,128)S(1)} %get-tuple-element.22.refs_2_), channel_id=1, source_target_pairs={{0,8},{1,17},{2,10},{3,19},{4,12},{5,21},{6,14},{7,23},{8,0},{9,25... | collective-permute-start | bytes 491528 | tf_op jit(solution)/shard_map/ppermute | solution.py:203
  38.3 14.1 %collective-permute-start.11 = (f32[2,288,256]{2,1,0:T(8,128)S(1)}, f32[2,288,256]{2,1,0:T(8,128)S(1)}, u32[]{:S(2)}, u32[]{:S(2)}) collective-permute-start(f32[2,288,256]{2,1,0:T(8,128)S(1)} %get-tuple-element.32.refs_2_), channel_id=1, source_target_pairs={{0,16},{1,9},{2,18},{3,11},{4,20},{5,13},{6,22},{7,15},{8,24},{9,1... | collective-permute-start | bytes 1769480 | tf_op jit(solution)/shard_map/ppermute | solution.py:203
  38.9 10.5 %collective-permute-start.12 = (f32[2,2,256,128]{3,2,1,0:T(8,128)S(1)}, f32[2,2,256,128]{3,2,1,0:T(8,128)S(1)}, u32[]{:S(2)}, u32[]{:S(2)}) collective-permute-start(f32[2,2,256,128]{3,2,1,0:T(8,128)S(1)} %shard_map.32.near), channel_id=1, source_target_pairs={{0,1},{1,0},{2,3},{3,2},{4,5},{5,4},{6,7},{7,6},{8,9},{9,8},{10,11... | collective-permute-start | bytes 1572872 | tf_op jit(solution)/shard_map/ppermute | solution.py:203
  45.2 7.2 %collective-permute-start.13 = (f32[2,2,256,128]{3,2,1,0:T(8,128)S(1)}, f32[2,2,256,128]{3,2,1,0:T(8,128)S(1)}, u32[]{:S(2)}, u32[]{:S(2)}) collective-permute-start(f32[2,2,256,128]{3,2,1,0:T(8,128)S(1)} %collective-permute-done.5.far), channel_id=1, source_target_pairs={{0,1},{1,0},{2,3},{3,2},{4,5},{5,4},{6,7},{7,6},{8,9},{9,8},{10,11... | collective-permute-start | bytes 1572872 | tf_op jit(solution)/shard_map/ppermute | solution.py:203
  45.3 15.1 %collective-permute-start.6 = (f32[2,2,256,128]{3,2,1,0:T(8,128)S(1)}, f32[2,2,256,128]{3,2,1,0:T(8,128)S(1)}, u32[]{:S(2)}, u32[]{:S(2)}) collective-permute-start(f32[2,2,256,128]{3,2,1,0:T(8,128)S(1)} %shard_map.33.held), channel_id=1, source_target_pairs={{0,4},{1,3},{2,6},{3,1},{4,0},{5,7},{6,2},{7,5},{8,12},{9,11},{10,... | collective-permute-start | bytes 1572872 | tf_op jit(solution)/shard_map/ppermute | solution.py:203
  49.3 41.0 %collective-permute-start.17 = (f32[2,256,896]{2,1,0:T(8,128)S(1)}, f32[2,256,896]{2,1,0:T(8,128)S(1)}, u32[]{:S(2)}, u32[]{:S(2)}) collective-permute-start(f32[2,256,896]{2,1,0:T(8,128)S(1)} %shard_map.38), channel_id=1, source_target_pairs={{0,16},{1,9},{2,18},{3,11},{4,20},{5,13},{6,22},{7,15},{8,24},{9,1... | collective-permute-start | bytes 5505032 | tf_op jit(solution)/shard_map/ppermute | solution.py:203
  54.8 36.9 %collective-permute-start.14 = (f32[2,256,896]{2,1,0:T(8,128)S(1)}, f32[2,256,896]{2,1,0:T(8,128)S(1)}, u32[]{:S(2)}, u32[]{:S(2)}) collective-permute-start(f32[2,256,896]{2,1,0:T(8,128)S(1)} %shard_map.36), channel_id=1, source_target_pairs={{0,8},{1,17},{2,10},{3,19},{4,12},{5,21},{6,14},{7,23},{8,0},{9,25... | collective-permute-start | bytes 5505032 | tf_op jit(solution)/shard_map/ppermute | solution.py:203
  60.4 2.0 %collective-permute-start.7 = (f32[2,2,256,128]{3,2,1,0:T(8,128)S(1)}, f32[2,2,256,128]{3,2,1,0:T(8,128)S(1)}, u32[]{:S(2)}, u32[]{:S(2)}) collective-permute-start(f32[2,2,256,128]{3,2,1,0:T(8,128)S(1)} %shard_map.34.near), channel_id=1, source_target_pairs={{0,1},{1,0},{2,3},{3,2},{4,5},{5,4},{6,7},{7,6},{8,9},{9,8},{10,11... | collective-permute-start | bytes 1572872 | tf_op jit(solution)/shard_map/ppermute | solution.py:203
  62.4 14.8 %collective-permute-start.8 = (f32[2,2,256,128]{3,2,1,0:T(8,128)S(1)}, f32[2,2,256,128]{3,2,1,0:T(8,128)S(1)}, u32[]{:S(2)}, u32[]{:S(2)}) collective-permute-start(f32[2,2,256,128]{3,2,1,0:T(8,128)S(1)} %shard_map.34.near), channel_id=1, source_target_pairs={{0,2},{1,5},{2,0},{3,7},{4,6},{5,1},{6,4},{7,3},{8,10},{9,13},{10,... | collective-permute-start | bytes 1572872 | tf_op jit(solution)/shard_map/ppermute | solution.py:203
  77.2 2.3 %collective-permute-start.9 = (f32[2,2,256,128]{3,2,1,0:T(8,128)S(1)}, f32[2,2,256,128]{3,2,1,0:T(8,128)S(1)}, u32[]{:S(2)}, u32[]{:S(2)}) collective-permute-start(f32[2,2,256,128]{3,2,1,0:T(8,128)S(1)} %collective-permute-done.8.far), channel_id=1, source_target_pairs={{0,1},{1,0},{2,3},{3,2},{4,5},{5,4},{6,7},{7,6},{8,9},{9,8},{10,11... | collective-permute-start | bytes 1572872 | tf_op jit(solution)/shard_map/ppermute | solution.py:203

commit v7 on v6

--- a/solution.py
+++ b/solution.py
@@ -148,14 +148,15 @@
     for i in range(2):
         first, second = (jnp.concatenate([a[0, i], a[1, i]], axis=1) for a in (near, far))
         t = split(jnp.concatenate([jnp.where(in_order, first, second), jnp.where(in_order, second, first)], axis=1))
-        at = 0
-        for own, got in zip(chunks[::2], chunks[1::2]):
-            n_ab = own.shape[1]
-            for low in range(0, n_ab, STEP):
-                high = min(low + STEP, n_ab)
-                v = split(jnp.concatenate([own[i, low:high, :], got[i, low:high, :]], axis=1))
-                out[i, :, at : at + high - low] = dot3(t, v)
-                at += high - low
+        for low in range(0, out.shape[2], STEP):
+            high = min(low + STEP, out.shape[2])
+            rows, base = [], 0
+            for own, got in zip(chunks[::2], chunks[1::2]):
+                start, stop = max(low - base, 0), min(high - base, own.shape[1])
+                if start < stop:
+                    rows.append(jnp.concatenate([own[i, start:stop, :], got[i, start:stop, :]], axis=1))
+                base += own.shape[1]
+            out[i, :, low:high] = dot3(t, split(jnp.concatenate(rows, axis=0)))
 
 
 def partial_sum(order, near, far, own, got):

time: 93.4 us -> 93 us (level)
  Pallas kernels: 12.8 us -> 10.9 us
  waiting for transfers between devices: 58.2 us -> 59.7 us
    pallas_call x13, Pallas kernels: 12.8 us -> 10.9 us  [call(): pl.pallas_call(kernel, out_shape=out_shape, in_specs=in_specs, out_specs=...]
    ppermute x18, waiting for transfers between devices: 58.2 us -> 59.7 us  [permute(): return lax.ppermute(a, BOTH, perm)]
  transfers between devices with their start and end apart: 18 -> 18, of which waited for: 11 -> 12; matrix products, arithmetic and copies ran while one was open for 0% -> 0% of each run, Pallas kernels for 12% -> 10%
where the time goes in v7:
time: 93 us; the launch traced here: 92.6 us
  waiting for transfers between devices  59.7 us (64%)
  starting transfers between devices  18.8 us (20%)
  Pallas kernels  10.9 us (12%)
  local copies, waits for them, and re-layouts  3.08 us (3%)
    ppermute x18, waiting for transfers between devices, permute(): return lax.ppermute(a, BOTH, perm)  59.7 us
    ppermute x18, starting transfers between devices, permute(): return lax.ppermute(a, BOTH, perm)  18.8 us
    pallas_call x13, Pallas kernels, call(): pl.pallas_call(kernel, out_shape=out_shape, in_specs=in_specs, out_specs=...  10.9 us
    unnamed x4, local copies, waits for them, and re-layouts  3.08 us
  transfers between devices with their start and end apart: 18, of which 12 were waited for; matrix products, arithmetic and copies ran while one was open for 0% of the time, Pallas kernels for 10%

profile of v7, /device:TPU:0, one launch (start us, length us, event | category | flops | bytes accessed | tf_op | source)
XLA Modules:
  0.0 92.6 jit_solution(4722318283924093065)
XLA Ops:
  0.0 1.0 %copy-done.1 = f32[4,256,128]{2,1,0:T(8,128)S(1)} copy-done((f32[4,256,128]{2,1,0:T(8,128)S(1)}, f32[4,256,128]{2,1,0:T(8,128)}, u32[]{:S(2)}) %copy-start.1) | copy-done | bytes 524312
  1.1 3.0 %collective-permute-start = (f32[2,256,128]{2,1,0:T(8,128)S(1)}, f32[2,256,128]{2,1,0:T(8,128)S(1)}, u32[]{:S(2)}, u32[]{:S(2)}) collective-permute-start(f32[2,256,128]{2,1,0:T(8,128)S(1)} %get-tuple-element.19.first), channel_id=1, source_target_pairs={{0,16},{1,9},{2,18},{3,11},{4,20},{5,13},{6,22},{7,15},{8,24},{9,1... | collective-permute-start | bytes 786440 | tf_op jit(solution)/shard_map/ppermute | solution.py:204
  4.1 2.0 %copy-done = f32[4,896,256]{2,1,0:T(8,128)S(1)} copy-done((f32[4,896,256]{2,1,0:T(8,128)S(1)}, f32[4,896,256]{2,1,0:T(8,128)}, u32[]{:S(2)}) %copy-start) | copy-done | bytes 3670040
  6.2 0.6 shard_map.29
  6.8 1.6 %collective-permute-start.15 = (f32[2,816,256]{2,1,0:T(8,128)S(1)}, f32[2,816,256]{2,1,0:T(8,128)S(1)}, u32[]{:S(2)}, u32[]{:S(2)}) collective-permute-start(f32[2,816,256]{2,1,0:T(8,128)S(1)} %get-tuple-element.21.refs_0_), channel_id=1, source_target_pairs={{0,8},{1,17},{2,10},{3,19},{4,12},{5,21},{6,14},{7,23},{8,0},{9,25... | collective-permute-start | bytes 5013512 | tf_op jit(solution)/shard_map/ppermute | solution.py:204
  8.3 2.4 %collective-permute-done.first = f32[2,256,128]{2,1,0:T(8,128)S(1)} collective-permute-done((f32[2,256,128]{2,1,0:T(8,128)S(1)}, f32[2,256,128]{2,1,0:T(8,128)S(1)}, u32[]{:S(2)}, u32[]{:S(2)}) %collective-permute-start) | collective-permute-done | bytes 262176 | tf_op jit(solution)/shard_map/ppermute | solution.py:204
  10.8 0.5 collective-permute-done.1.second
  11.3 3.2 %collective-permute-start.2 = (f32[2,2,256,128]{3,2,1,0:T(8,128)S(1)}, f32[2,2,256,128]{3,2,1,0:T(8,128)S(1)}, u32[]{:S(2)}, u32[]{:S(2)}) collective-permute-start(f32[2,2,256,128]{3,2,1,0:T(8,128)S(1)} %shard_map.30.held), channel_id=1, source_target_pairs={{0,4},{1,3},{2,6},{3,1},{4,0},{5,7},{6,2},{7,5},{8,12},{9,11},{10,... | collective-permute-start | bytes 1572872 | tf_op jit(solution)/shard_map/ppermute | solution.py:204
  14.5 12.8 %collective-permute-done.2.got = f32[2,2,256,128]{3,2,1,0:T(8,128)S(1)} collective-permute-done((f32[2,2,256,128]{3,2,1,0:T(8,128)S(1)}, f32[2,2,256,128]{3,2,1,0:T(8,128)S(1)}, u32[]{:S(2)}, u32[]{:S(2)}) %collective-permute-start.2) | collective-permute-done | bytes 524320 | tf_op jit(solution)/shard_map/ppermute | solution.py:204
  27.4 1.8 %collective-permute-start.10 = (f32[2,608,256]{2,1,0:T(8,128)S(1)}, f32[2,608,256]{2,1,0:T(8,128)S(1)}, u32[]{:S(2)}, u32[]{:S(2)}) collective-permute-start(f32[2,608,256]{2,1,0:T(8,128)S(1)} %get-tuple-element.31.refs_0_), channel_id=1, source_target_pairs={{0,16},{1,9},{2,18},{3,11},{4,20},{5,13},{6,22},{7,15},{8,24},{9,1... | collective-permute-start | bytes 3735560 | tf_op jit(solution)/shard_map/ppermute | solution.py:204
  29.3 1.2 %collective-permute-done.3.small = f32[8,128]{1,0:T(8,128)S(1)} collective-permute-done((f32[8,128]{1,0:T(8,128)S(1)}, f32[8,128]{1,0:T(8,128)S(1)}, u32[]{:S(2)}, u32[]{:S(2)}) %collective-permute-start.3) | collective-permute-done | bytes 4128 | tf_op jit(solution)/shard_map/ppermute | solution.py:204
  30.4 0.8 collective-permute-start.5
  31.2 1.5 %collective-permute-start.16 = (f32[2,80,256]{2,1,0:T(8,128)S(1)}, f32[2,80,256]{2,1,0:T(8,128)S(1)}, u32[]{:S(2)}, u32[]{:S(2)}) collective-permute-start(f32[2,80,256]{2,1,0:T(8,128)S(1)} %get-tuple-element.22.refs_2_), channel_id=1, source_target_pairs={{0,8},{1,17},{2,10},{3,19},{4,12},{5,21},{6,14},{7,23},{8,0},{9,25... | collective-permute-start | bytes 491528 | tf_op jit(solution)/shard_map/ppermute | solution.py:204
  32.7 5.6 %collective-permute-done.16.refs_3_ = f32[2,80,256]{2,1,0:T(8,128)S(1)} collective-permute-done((f32[2,80,256]{2,1,0:T(8,128)S(1)}, f32[2,80,256]{2,1,0:T(8,128)S(1)}, u32[]{:S(2)}, u32[]{:S(2)}) %collective-permute-start.16) | collective-permute-done | bytes 163872 | tf_op jit(solution)/shard_map/ppermute | solution.py:204
  38.3 0.5 collective-permute-start.11
  38.9 0.4 collective-permute-start.12
  39.2 6.0 %collective-permute-done.5.far = f32[2,2,256,128]{3,2,1,0:T(8,128)S(1)} collective-permute-done((f32[2,2,256,128]{3,2,1,0:T(8,128)S(1)}, f32[2,2,256,128]{3,2,1,0:T(8,128)S(1)}, u32[]{:S(2)}, u32[]{:S(2)}) %collective-permute-start.5) | collective-permute-done | bytes 524320 | tf_op jit(solution)/shard_map/ppermute | solution.py:204
  45.3 1.8 %collective-permute-start.6 = (f32[2,2,256,128]{3,2,1,0:T(8,128)S(1)}, f32[2,2,256,128]{3,2,1,0:T(8,128)S(1)}, u32[]{:S(2)}, u32[]{:S(2)}) collective-permute-start(f32[2,2,256,128]{3,2,1,0:T(8,128)S(1)} %shard_map.33.held), channel_id=1, source_target_pairs={{0,4},{1,3},{2,6},{3,1},{4,0},{5,7},{6,2},{7,5},{8,12},{9,11},{10,... | collective-permute-start | bytes 1572872 | tf_op jit(solution)/shard_map/ppermute | solution.py:204
  47.0 1.8 %shard_map.38 = f32[2,256,896]{2,1,0:T(8,128)S(1)} custom-call(f32[2,2,256,128]{3,2,1,0:T(8,128)S(1)} %shard_map.32.near, f32[2,2,256,128]{3,2,1,0:T(8,128)S(1)} %collective-permute-done.5.far, f32[2,816,256]{2,1,0:T(8,128)S(1)} %get-tuple-element.21.refs_0_, f32[2,816,256]{2,1,0:T(8,128)S(1)} %collective-permute-done.15.refs_1_, ...), custom_call_target="tpu_custom_call" | custom-call | flops 1409286144 | bytes 6553600 | tf_op jit(solution)/shard_map/pallas_call | solution.py:51
  48.9 0.6 collective-permute-start.17
  49.5 3.0 %collective-permute-done.11.refs_3_ = f32[2,288,256]{2,1,0:T(8,128)S(1)} collective-permute-done((f32[2,288,256]{2,1,0:T(8,128)S(1)}, f32[2,288,256]{2,1,0:T(8,128)S(1)}, u32[]{:S(2)}, u32[]{:S(2)}) %collective-permute-start.11) | collective-permute-done | bytes 589856 | tf_op jit(solution)/shard_map/ppermute | solution.py:204
  52.5 1.8 %shard_map.36 = f32[2,256,896]{2,1,0:T(8,128)S(1)} custom-call(f32[2,2,256,128]{3,2,1,0:T(8,128)S(1)} %collective-permute-done.12.near, f32[2,2,256,128]{3,2,1,0:T(8,128)S(1)} %collective-permute-done.13.far, f32[2,608,256]{2,1,0:T(8,128)S(1)} %get-tuple-element.31.refs_0_, f32[2,608,256]{2,1,0:T(8,128)S(1)} %collective-permute-done.10.refs_1_, ...), custom_call_target="tpu_custom_call" | custom-call | flops 1409286144 | bytes 6553600 | tf_op jit(solution)/shard_map/pallas_call | solution.py:51
  54.3 1.9 %collective-permute-start.14 = (f32[2,256,896]{2,1,0:T(8,128)S(1)}, f32[2,256,896]{2,1,0:T(8,128)S(1)}, u32[]{:S(2)}, u32[]{:S(2)}) collective-permute-start(f32[2,256,896]{2,1,0:T(8,128)S(1)} %shard_map.36), channel_id=1, source_target_pairs={{0,8},{1,17},{2,10},{3,19},{4,12},{5,21},{6,14},{7,23},{8,0},{9,25... | collective-permute-start | bytes 5505032 | tf_op jit(solution)/shard_map/ppermute | solution.py:204
  56.2 4.2 %collective-permute-done.6.got = f32[2,2,256,128]{3,2,1,0:T(8,128)S(1)} collective-permute-done((f32[2,2,256,128]{3,2,1,0:T(8,128)S(1)}, f32[2,2,256,128]{3,2,1,0:T(8,128)S(1)}, u32[]{:S(2)}, u32[]{:S(2)}) %collective-permute-start.6) | collective-permute-done | bytes 524320 | tf_op jit(solution)/shard_map/ppermute | solution.py:204
  60.5 1.9 %collective-permute-done.7.near = f32[2,2,256,128]{3,2,1,0:T(8,128)S(1)} collective-permute-done((f32[2,2,256,128]{3,2,1,0:T(8,128)S(1)}, f32[2,2,256,128]{3,2,1,0:T(8,128)S(1)}, u32[]{:S(2)}, u32[]{:S(2)}) %collective-permute-start.7) | collective-permute-done | bytes 524320 | tf_op jit(solution)/shard_map/ppermute | solution.py:204
  62.4 1.8 %collective-permute-start.8 = (f32[2,2,256,128]{3,2,1,0:T(8,128)S(1)}, f32[2,2,256,128]{3,2,1,0:T(8,128)S(1)}, u32[]{:S(2)}, u32[]{:S(2)}) collective-permute-start(f32[2,2,256,128]{3,2,1,0:T(8,128)S(1)} %shard_map.34.near), channel_id=1, source_target_pairs={{0,2},{1,5},{2,0},{3,7},{4,6},{5,1},{6,4},{7,3},{8,10},{9,13},{10,... | collective-permute-start | bytes 1572872 | tf_op jit(solution)/shard_map/ppermute | solution.py:204
  64.2 13.0 %collective-permute-done.8.far = f32[2,2,256,128]{3,2,1,0:T(8,128)S(1)} collective-permute-done((f32[2,2,256,128]{3,2,1,0:T(8,128)S(1)}, f32[2,2,256,128]{3,2,1,0:T(8,128)S(1)}, u32[]{:S(2)}, u32[]{:S(2)}) %collective-permute-start.8) | collective-permute-done | bytes 524320 | tf_op jit(solution)/shard_map/ppermute | solution.py:204
  77.2 1.8 %shard_map.37.kept = f32[2,256,896]{2,1,0:T(8,128)S(1)} custom-call(f32[2,2,256,128]{3,2,1,0:T(8,128)S(1)} %shard_map.34.near, f32[2,2,256,128]{3,2,1,0:T(8,128)S(1)} %collective-permute-done.8.far, f32[2,816,256]{2,1,0:T(8,128)S(1)} %get-tuple-element.21.refs_0_, f32[2,816,256]{2,1,0:T(8,128)S(1)} %collective-permute-done.15.refs_1_, ...), custom_call_target="tpu_custom_call" | custom-call | flops 1409286144 | bytes 6553600 | tf_op jit(solution)/shard_map/pallas_call | solution.py:51
  79.1 1.8 %shard_map.35.kept = f32[2,256,896]{2,1,0:T(8,128)S(1)} custom-call(f32[2,2,256,128]{3,2,1,0:T(8,128)S(1)} %collective-permute-done.7.near, f32[2,2,256,128]{3,2,1,0:T(8,128)S(1)} %collective-permute-done.9.far, f32[2,608,256]{2,1,0:T(8,128)S(1)} %get-tuple-element.31.refs_0_, f32[2,608,256]{2,1,0:T(8,128)S(1)} %collective-permute-done.10.refs_1_, ...), custom_call_target="tpu_custom_call" | custom-call | flops 1409286144 | bytes 6553600 | tf_op jit(solution)/shard_map/pallas_call | solution.py:51
  81.0 8.9 %collective-permute-done.17.came = f32[2,256,896]{2,1,0:T(8,128)S(1)} collective-permute-done((f32[2,256,896]{2,1,0:T(8,128)S(1)}, f32[2,256,896]{2,1,0:T(8,128)S(1)}, u32[]{:S(2)}, u32[]{:S(2)}) %collective-permute-start.17) | collective-permute-done | bytes 1835040 | tf_op jit(solution)/shard_map/ppermute | solution.py:204
  89.9 1.3 %shard_map.39.refs_0_ = f32[4,256,896]{2,1,0:T(8,128)} custom-call(f32[2,256,896]{2,1,0:T(8,128)S(1)} %shard_map.37.kept, f32[2,256,896]{2,1,0:T(8,128)S(1)} %collective-permute-done.17.came), custom_call_target="tpu_custom_call" | custom-call | flops 917504 | bytes 7340032 | tf_op jit(solution)/shard_map/pallas_call | solution.py:51
  91.2 1.3 %shard_map.40 = f32[4,256,896]{2,1,0:T(8,128)} custom-call(f32[2,256,896]{2,1,0:T(8,128)S(1)} %shard_map.35.kept, f32[2,256,896]{2,1,0:T(8,128)S(1)} %collective-permute-done.14.came, f32[4,256,896]{2,1,0:T(8,128)} %shard_map.39.refs_0_), custom_call_target="tpu_custom_call", output_to_operand_aliasing={{}: (2, {})} | custom-call | flops 917504 | bytes 11010048 | tf_op jit(solution)/shard_map/pallas_call | solution.py:51
  (21 shorter events, 0.5 us)
Async XLA Ops:
  0.0 1.0 %copy-start.1 = (f32[4,256,128]{2,1,0:T(8,128)S(1)}, f32[4,256,128]{2,1,0:T(8,128)}, u32[]{:S(2)}) copy-start(f32[4,256,128]{2,1,0:T(8,128)} %whole.2) | copy-start | bytes 1572868
  1.1 9.7 %collective-permute-start = (f32[2,256,128]{2,1,0:T(8,128)S(1)}, f32[2,256,128]{2,1,0:T(8,128)S(1)}, u32[]{:S(2)}, u32[]{:S(2)}) collective-permute-start(f32[2,256,128]{2,1,0:T(8,128)S(1)} %get-tuple-element.19.first), channel_id=1, source_target_pairs={{0,16},{1,9},{2,18},{3,11},{4,20},{5,13},{6,22},{7,15},{8,24},{9,1... | collective-permute-start | bytes 786440 | tf_op jit(solution)/shard_map/ppermute | solution.py:204
  4.1 7.2 %collective-permute-start.1 = (f32[2,256,128]{2,1,0:T(8,128)S(1)}, f32[2,256,128]{2,1,0:T(8,128)S(1)}, u32[]{:S(2)}, u32[]{:S(2)}) collective-permute-start(f32[2,256,128]{2,1,0:T(8,128)S(1)} %get-tuple-element.28), channel_id=1, source_target_pairs={{0,9},{1,16},{2,11},{3,18},{4,13},{5,20},{6,15},{7,22},{8,1},{9,24... | collective-permute-start | bytes 786440 | tf_op jit(solution)/shard_map/ppermute | solution.py:204
  4.1 2.0 %copy-start = (f32[4,896,256]{2,1,0:T(8,128)S(1)}, f32[4,896,256]{2,1,0:T(8,128)}, u32[]{:S(2)}) copy-start(f32[4,896,256]{2,1,0:T(8,128)} %whole.3) | copy-start | bytes 11010052
  6.8 38.5 %collective-permute-start.15 = (f32[2,816,256]{2,1,0:T(8,128)S(1)}, f32[2,816,256]{2,1,0:T(8,128)S(1)}, u32[]{:S(2)}, u32[]{:S(2)}) collective-permute-start(f32[2,816,256]{2,1,0:T(8,128)S(1)} %get-tuple-element.21.refs_0_), channel_id=1, source_target_pairs={{0,8},{1,17},{2,10},{3,19},{4,12},{5,21},{6,14},{7,23},{8,0},{9,25... | collective-permute-start | bytes 5013512 | tf_op jit(solution)/shard_map/ppermute | solution.py:204
  11.3 16.0 %collective-permute-start.2 = (f32[2,2,256,128]{3,2,1,0:T(8,128)S(1)}, f32[2,2,256,128]{3,2,1,0:T(8,128)S(1)}, u32[]{:S(2)}, u32[]{:S(2)}) collective-permute-start(f32[2,2,256,128]{3,2,1,0:T(8,128)S(1)} %shard_map.30.held), channel_id=1, source_target_pairs={{0,4},{1,3},{2,6},{3,1},{4,0},{5,7},{6,2},{7,5},{8,12},{9,11},{10,... | collective-permute-start | bytes 1572872 | tf_op jit(solution)/shard_map/ppermute | solution.py:204
  27.4 25.1 %collective-permute-start.10 = (f32[2,608,256]{2,1,0:T(8,128)S(1)}, f32[2,608,256]{2,1,0:T(8,128)S(1)}, u32[]{:S(2)}, u32[]{:S(2)}) collective-permute-start(f32[2,608,256]{2,1,0:T(8,128)S(1)} %get-tuple-element.31.refs_0_), channel_id=1, source_target_pairs={{0,16},{1,9},{2,18},{3,11},{4,20},{5,13},{6,22},{7,15},{8,24},{9,1... | collective-permute-start | bytes 3735560 | tf_op jit(solution)/shard_map/ppermute | solution.py:204
  29.3 1.2 %collective-permute-start.3 = (f32[8,128]{1,0:T(8,128)S(1)}, f32[8,128]{1,0:T(8,128)S(1)}, u32[]{:S(2)}, u32[]{:S(2)}) collective-permute-start(f32[8,128]{1,0:T(8,128)S(1)} %get-tuple-element.27), channel_id=1, source_target_pairs={{0,1},{1,0},{2,3},{3,2},{4,5},{5,4},{6,7},{7,6},{8,9},{9,8},{10,11... | collective-permute-start | bytes 12296 | tf_op jit(solution)/shard_map/ppermute | solution.py:204
  30.4 14.8 %collective-permute-start.5 = (f32[2,2,256,128]{3,2,1,0:T(8,128)S(1)}, f32[2,2,256,128]{3,2,1,0:T(8,128)S(1)}, u32[]{:S(2)}, u32[]{:S(2)}) collective-permute-start(f32[2,2,256,128]{3,2,1,0:T(8,128)S(1)} %shard_map.32.near), channel_id=1, source_target_pairs={{0,2},{1,5},{2,0},{3,7},{4,6},{5,1},{6,4},{7,3},{8,10},{9,13},{10,... | collective-permute-start | bytes 1572872 | tf_op jit(solution)/shard_map/ppermute | solution.py:204
  31.2 7.6 %collective-permute-start.4 = (f32[2,256,128]{2,1,0:T(8,128)S(1)}, f32[2,256,128]{2,1,0:T(8,128)S(1)}, u32[]{:S(2)}, u32[]{:S(2)}) collective-permute-start(f32[2,256,128]{2,1,0:T(8,128)S(1)} %get-tuple-element.28), channel_id=1, source_target_pairs={{0,1},{1,0},{2,3},{3,2},{4,5},{5,4},{6,7},{7,6},{8,9},{9,8},{10,11... | collective-permute-start | bytes 786440 | tf_op jit(solution)/shard_map/ppermute | solution.py:204
  31.2 7.1 %collective-permute-start.16 = (f32[2,80,256]{2,1,0:T(8,128)S(1)}, f32[2,80,256]{2,1,0:T(8,128)S(1)}, u32[]{:S(2)}, u32[]{:S(2)}) collective-permute-start(f32[2,80,256]{2,1,0:T(8,128)S(1)} %get-tuple-element.22.refs_2_), channel_id=1, source_target_pairs={{0,8},{1,17},{2,10},{3,19},{4,12},{5,21},{6,14},{7,23},{8,0},{9,25... | collective-permute-start | bytes 491528 | tf_op jit(solution)/shard_map/ppermute | solution.py:204
  38.3 14.1 %collective-permute-start.11 = (f32[2,288,256]{2,1,0:T(8,128)S(1)}, f32[2,288,256]{2,1,0:T(8,128)S(1)}, u32[]{:S(2)}, u32[]{:S(2)}) collective-permute-start(f32[2,288,256]{2,1,0:T(8,128)S(1)} %get-tuple-element.32.refs_2_), channel_id=1, source_target_pairs={{0,16},{1,9},{2,18},{3,11},{4,20},{5,13},{6,22},{7,15},{8,24},{9,1... | collective-permute-start | bytes 1769480 | tf_op jit(solution)/shard_map/ppermute | solution.py:204
  38.9 10.0 %collective-permute-start.12 = (f32[2,2,256,128]{3,2,1,0:T(8,128)S(1)}, f32[2,2,256,128]{3,2,1,0:T(8,128)S(1)}, u32[]{:S(2)}, u32[]{:S(2)}) collective-permute-start(f32[2,2,256,128]{3,2,1,0:T(8,128)S(1)} %shard_map.32.near), channel_id=1, source_target_pairs={{0,1},{1,0},{2,3},{3,2},{4,5},{5,4},{6,7},{7,6},{8,9},{9,8},{10,11... | collective-permute-start | bytes 1572872 | tf_op jit(solution)/shard_map/ppermute | solution.py:204
  45.2 7.2 %collective-permute-start.13 = (f32[2,2,256,128]{3,2,1,0:T(8,128)S(1)}, f32[2,2,256,128]{3,2,1,0:T(8,128)S(1)}, u32[]{:S(2)}, u32[]{:S(2)}) collective-permute-start(f32[2,2,256,128]{3,2,1,0:T(8,128)S(1)} %collective-permute-done.5.far), channel_id=1, source_target_pairs={{0,1},{1,0},{2,3},{3,2},{4,5},{5,4},{6,7},{7,6},{8,9},{9,8},{10,11... | collective-permute-start | bytes 1572872 | tf_op jit(solution)/shard_map/ppermute | solution.py:204
  45.3 15.1 %collective-permute-start.6 = (f32[2,2,256,128]{3,2,1,0:T(8,128)S(1)}, f32[2,2,256,128]{3,2,1,0:T(8,128)S(1)}, u32[]{:S(2)}, u32[]{:S(2)}) collective-permute-start(f32[2,2,256,128]{3,2,1,0:T(8,128)S(1)} %shard_map.33.held), channel_id=1, source_target_pairs={{0,4},{1,3},{2,6},{3,1},{4,0},{5,7},{6,2},{7,5},{8,12},{9,11},{10,... | collective-permute-start | bytes 1572872 | tf_op jit(solution)/shard_map/ppermute | solution.py:204
  48.9 41.0 %collective-permute-start.17 = (f32[2,256,896]{2,1,0:T(8,128)S(1)}, f32[2,256,896]{2,1,0:T(8,128)S(1)}, u32[]{:S(2)}, u32[]{:S(2)}) collective-permute-start(f32[2,256,896]{2,1,0:T(8,128)S(1)} %shard_map.38), channel_id=1, source_target_pairs={{0,16},{1,9},{2,18},{3,11},{4,20},{5,13},{6,22},{7,15},{8,24},{9,1... | collective-permute-start | bytes 5505032 | tf_op jit(solution)/shard_map/ppermute | solution.py:204
  54.3 36.9 %collective-permute-start.14 = (f32[2,256,896]{2,1,0:T(8,128)S(1)}, f32[2,256,896]{2,1,0:T(8,128)S(1)}, u32[]{:S(2)}, u32[]{:S(2)}) collective-permute-start(f32[2,256,896]{2,1,0:T(8,128)S(1)} %shard_map.36), channel_id=1, source_target_pairs={{0,8},{1,17},{2,10},{3,19},{4,12},{5,21},{6,14},{7,23},{8,0},{9,25... | collective-permute-start | bytes 5505032 | tf_op jit(solution)/shard_map/ppermute | solution.py:204
  60.4 2.0 %collective-permute-start.7 = (f32[2,2,256,128]{3,2,1,0:T(8,128)S(1)}, f32[2,2,256,128]{3,2,1,0:T(8,128)S(1)}, u32[]{:S(2)}, u32[]{:S(2)}) collective-permute-start(f32[2,2,256,128]{3,2,1,0:T(8,128)S(1)} %shard_map.34.near), channel_id=1, source_target_pairs={{0,1},{1,0},{2,3},{3,2},{4,5},{5,4},{6,7},{7,6},{8,9},{9,8},{10,11... | collective-permute-start | bytes 1572872 | tf_op jit(solution)/shard_map/ppermute | solution.py:204
  62.4 14.8 %collective-permute-start.8 = (f32[2,2,256,128]{3,2,1,0:T(8,128)S(1)}, f32[2,2,256,128]{3,2,1,0:T(8,128)S(1)}, u32[]{:S(2)}, u32[]{:S(2)}) collective-permute-start(f32[2,2,256,128]{3,2,1,0:T(8,128)S(1)} %shard_map.34.near), channel_id=1, source_target_pairs={{0,2},{1,5},{2,0},{3,7},{4,6},{5,1},{6,4},{7,3},{8,10},{9,13},{10,... | collective-permute-start | bytes 1572872 | tf_op jit(solution)/shard_map/ppermute | solution.py:204
  77.2 1.9 %collective-permute-start.9 = (f32[2,2,256,128]{3,2,1,0:T(8,128)S(1)}, f32[2,2,256,128]{3,2,1,0:T(8,128)S(1)}, u32[]{:S(2)}, u32[]{:S(2)}) collective-permute-start(f32[2,2,256,128]{3,2,1,0:T(8,128)S(1)} %collective-permute-done.8.far), channel_id=1, source_target_pairs={{0,1},{1,0},{2,3},{3,2},{4,5},{5,4},{6,7},{7,6},{8,9},{9,8},{10,11... | collective-permute-start | bytes 1572872 | tf_op jit(solution)/shard_map/ppermute | solution.py:204
